TPU v7x, 32 devices: a whole 2x2x4 slice. The times are simulated.
32 devices in a mesh: sess: 2 (over x), ctx: 16 (over z, y, core).
Axes of the slice: x: 2, y: 2, z: 4, core: 2. Of those that a mesh axis runs over, the one named last changes fastest.
Arguments:
- query_rows: bfloat16 [2, 1024, 4096], P('sess', 'ctx'), may hold values from -6 to 6
- key_rows: bfloat16 [2, 1024, 4096], P('sess', 'ctx'), may hold values from -6 to 6
- value_rows: bfloat16 [2, 1024, 4096], P('sess', 'ctx'), may hold values from -6 to 6
- seg_starts: int32 [2, 4], P('sess'), may hold values from 0 to 1023, as said below
- norm_gain: float32 [4096], replicated, may hold values from 0.1 to 1.9
Outputs:
- attended: bfloat16 [2, 1024, 4096], P('sess', 'ctx')
Inputs may be any that keep to these rules, and one draw needn't show every extreme that they name: `seg_starts`: within each session the starts rise strictly, the first is 0 and the last is 1023.
All inputs are finite; a program needn't handle non-finite values.
Results may differ from a plain program's by a relative error of at most 0.0049.
Values sent between devices are 32-bit elements; how exact they have to be, the bound alone decides.
No kernel may reach another device: no remote copies, remote signals or barrier semaphores. Data moves between devices by JAX's collectives and lax.ppermute only.
A program may use at most 192 MiB of HBM per device.

v0:
```python
import jax
import jax.numpy as jnp
from jax import lax
from jax.sharding import PartitionSpec as P

HEADS = 32
HD = 128


def prefix(value, axis, join, neutral):
    count, mine = (lax.axis_size(axis), lax.axis_index(axis))
    pieces = jax.tree.map(lambda part: lax.all_gather(part, axis), value)
    total = jax.tree.map(
        lambda part, zero: jnp.full_like(part, 0) + jnp.asarray(zero, part.dtype), value, neutral
    )

    def step(position, total):
        longer = join(total, jax.tree.map(lambda part: part[position], pieces))
        return jax.tree.map(lambda new, old: jnp.where(position < mine, new, old), longer, total)

    return lax.fori_loop(0, count - 1, step, total)


def combine_states(earlier, later):
    flag_early, state_early = earlier
    flag_late, state_late = later
    return (jnp.maximum(flag_early, flag_late), state_late + (1.0 - flag_late[0]) * state_early)


def shards(query_rows, key_rows, value_rows, seg_starts, norm_gain):
    rows = query_rows.shape[1]
    width = query_rows.shape[2]
    block_start = lax.axis_index("ctx") * rows
    positions = block_start + jnp.arange(rows, dtype=jnp.int32)
    start_list = seg_starts[0]
    seg_ids = jnp.sum((start_list[None, :] <= positions[:, None]).astype(jnp.int32), axis=1)
    prior_count = jnp.sum((start_list < block_start).astype(jnp.int32))
    query_heads = query_rows[0].reshape(rows, HEADS, HD)
    key_heads = key_rows[0].reshape(rows, HEADS, HD)
    value_heads = value_rows[0].reshape(rows, HEADS, HD)
    last_seg = seg_ids[-1]
    keep_mask = (seg_ids == last_seg).astype(jnp.bfloat16)
    kept_keys = key_heads * keep_mask[:, None, None]
    reset_flag = (last_seg != prior_count).astype(jnp.float32).reshape(1)
    summary = jnp.einsum("uhe,uhf->hef", kept_keys, value_heads, preferred_element_type=jnp.float32)
    identity = (jnp.zeros((1,), jnp.float32), jnp.zeros_like(summary))
    flags_in, state_in = prefix((reset_flag, summary), "ctx", combine_states, identity)
    causal = jnp.arange(rows)[:, None] >= jnp.arange(rows)[None, :]
    allowed = causal & (seg_ids[:, None] == seg_ids[None, :])
    scores = jnp.einsum("the,uhe->htu", query_heads, key_heads, preferred_element_type=jnp.float32)
    weights = jnp.where(allowed[None], scores, 0.0).astype(jnp.bfloat16)
    intra = jnp.einsum("htu,uhe->the", weights, value_heads, preferred_element_type=jnp.float32)
    carried = state_in.astype(jnp.bfloat16)
    inter = jnp.einsum("the,hef->thf", query_heads, carried, preferred_element_type=jnp.float32)
    use_mask = (seg_ids == prior_count).astype(jnp.float32)
    mixed = (intra + use_mask[:, None, None] * inter).reshape(rows, width)
    scale_inv = lax.rsqrt(jnp.mean(mixed * mixed, axis=-1, keepdims=True) + 1e-05)
    attended = (mixed * scale_inv * norm_gain).astype(jnp.bfloat16)
    return attended.reshape(1, rows, width)


def solution(mesh):
    placed = (
        P("sess", "ctx", None),
        P("sess", "ctx", None),
        P("sess", "ctx", None),
        P("sess", None),
        P(),
    )
    return jax.shard_map(
        shards, mesh=mesh, in_specs=placed, out_specs=P("sess", "ctx", None), check_vma=False
    )
```

profile of v0, /device:TPU:0, one launch (start us, length us, event | category | flops | bytes accessed | tf_op | source)
XLA Modules:
  0.0 266.8 jit_solution(16019642517396885538)
XLA Ops:
  6.5 1.3 fusion.19
  10.4 1.1 copy.31
  11.5 1.3 compare_convert_fusion.1
  12.8 1.9 fusion.5
  17.5 35.8 %all-reduce = f32[16]{0:T(128)S(1)} all-reduce(f32[16]{0:T(128)S(1)} %dynamic-update-slice), channel_id=1, replica_groups=mesh['sess'=2,'ctx'=16] {'ctx'}, use_global_device_ids=true, to_apply=%add | all-reduce | flops 16 | bytes 128
  54.5 2.7 %convolution_bitcast_fusion = f32[64,32,128]{2,0,1:T(8,128)} fusion(pred[64,64]{1,0:T(8,128)(4,1)S(1)} %fusion.18, bf16[64,32,128]{2,1,0:T(8,128)(2,1)} %bitcast.37, bf16[64,32,128]{2,1,0:T(8,128)(2,1)S(1)} %bitcast.35, bf16[64,32,128]{2,1,0:T(8,128)(2,1)S(1)} %bitcast.32), kind=kOutput, calls=%fused_computation.7 | convolution fusion | flops 67371008 | bytes 2625536 | tf_op jit(solution)/shard_map/htu,uhe->the/dot_general | solution.py:52
  57.2 128.8 %all-gather.3.cloned.1.call-done = f32[512,128,128]{2,1,0:T(8,128)} async-done(((f32[32,128,128]{2,1,0:T(8,128)}), f32[512,128,128]{2,1,0:T(8,128)}) %all-gather.3.cloned.1.call-update) | async-done | bytes 33554448 | tf_op jit(solution)/shard_map/all_gather | solution.py:12
  186.0 70.4 %while.14 = (s32[]{:T(128)}, f32[32,128,128]{2,1,0:T(8,128)S(1)}, s32[]{:T(128)}, f32[16,32,128,128]{3,2,1,0:T(8,128)}, f32[16,1]{0,1:T(1,128)S(1)}, /*index=5*/s32[]{:T(128)}, s32[]{:T(128)}) while((s32[]{:T(128)}, f32[32,128,128]{2,1,0:T(8,128)S(1)}, s32[]{:T(128)}, f32[16,32,128,128]{3,2,1,0:T(8,128)}, f32[16,1]{0,1:T(1,128)S(1)}, ...), condition=%wide.region_3.4_spmd.clone, body=%wide.region_2.3_spmd.clone.sunk | while | flops 2097157 | bytes 6291573 | solution.py:21
  186.6 4.1 %fusion.25 = f32[32,128,128]{2,1,0:T(8,128)S(1)} fusion(f32[32,128,128]{2,1,0:T(8,128)S(1)} %get-tuple-element.171, f32[16,32,128,128]{3,2,1,0:T(8,128)} %get-tuple-element.180, s32[]{:T(128)} %get-tuple-element.170, f32[]{:T(128)} %bitcast.30, pred[]{:T(512)S(6)} %compare.3, pred[]{:T(512)S(6)} %lt.34), kind=kLoop, calls=%fused_computation.1.clone.1 | loop fusion | flops 2097152 | bytes 6291466 | tf_op jit(solution)/shard_map/while/body/eval_jaxpr/jit(_where)/select_n | solution.py:19
  191.3 4.1 %fusion.25 = f32[32,128,128]{2,1,0:T(8,128)S(1)} fusion(f32[32,128,128]{2,1,0:T(8,128)S(1)} %get-tuple-element.171, f32[16,32,128,128]{3,2,1,0:T(8,128)} %get-tuple-element.180, s32[]{:T(128)} %get-tuple-element.170, f32[]{:T(128)} %bitcast.30, pred[]{:T(512)S(6)} %compare.3, pred[]{:T(512)S(6)} %lt.34), kind=kLoop, calls=%fused_computation.1.clone.1 | loop fusion | flops 2097152 | bytes 6291466 | tf_op jit(solution)/shard_map/while/body/eval_jaxpr/jit(_where)/select_n | solution.py:19
  195.9 4.1 %fusion.25 = f32[32,128,128]{2,1,0:T(8,128)S(1)} fusion(f32[32,128,128]{2,1,0:T(8,128)S(1)} %get-tuple-element.171, f32[16,32,128,128]{3,2,1,0:T(8,128)} %get-tuple-element.180, s32[]{:T(128)} %get-tuple-element.170, f32[]{:T(128)} %bitcast.30, pred[]{:T(512)S(6)} %compare.3, pred[]{:T(512)S(6)} %lt.34), kind=kLoop, calls=%fused_computation.1.clone.1 | loop fusion | flops 2097152 | bytes 6291466 | tf_op jit(solution)/shard_map/while/body/eval_jaxpr/jit(_where)/select_n | solution.py:19
  200.6 4.1 %fusion.25 = f32[32,128,128]{2,1,0:T(8,128)S(1)} fusion(f32[32,128,128]{2,1,0:T(8,128)S(1)} %get-tuple-element.171, f32[16,32,128,128]{3,2,1,0:T(8,128)} %get-tuple-element.180, s32[]{:T(128)} %get-tuple-element.170, f32[]{:T(128)} %bitcast.30, pred[]{:T(512)S(6)} %compare.3, pred[]{:T(512)S(6)} %lt.34), kind=kLoop, calls=%fused_computation.1.clone.1 | loop fusion | flops 2097152 | bytes 6291466 | tf_op jit(solution)/shard_map/while/body/eval_jaxpr/jit(_where)/select_n | solution.py:19
  205.3 4.1 %fusion.25 = f32[32,128,128]{2,1,0:T(8,128)S(1)} fusion(f32[32,128,128]{2,1,0:T(8,128)S(1)} %get-tuple-element.171, f32[16,32,128,128]{3,2,1,0:T(8,128)} %get-tuple-element.180, s32[]{:T(128)} %get-tuple-element.170, f32[]{:T(128)} %bitcast.30, pred[]{:T(512)S(6)} %compare.3, pred[]{:T(512)S(6)} %lt.34), kind=kLoop, calls=%fused_computation.1.clone.1 | loop fusion | flops 2097152 | bytes 6291466 | tf_op jit(solution)/shard_map/while/body/eval_jaxpr/jit(_where)/select_n | solution.py:19
  210.0 4.1 %fusion.25 = f32[32,128,128]{2,1,0:T(8,128)S(1)} fusion(f32[32,128,128]{2,1,0:T(8,128)S(1)} %get-tuple-element.171, f32[16,32,128,128]{3,2,1,0:T(8,128)} %get-tuple-element.180, s32[]{:T(128)} %get-tuple-element.170, f32[]{:T(128)} %bitcast.30, pred[]{:T(512)S(6)} %compare.3, pred[]{:T(512)S(6)} %lt.34), kind=kLoop, calls=%fused_computation.1.clone.1 | loop fusion | flops 2097152 | bytes 6291466 | tf_op jit(solution)/shard_map/while/body/eval_jaxpr/jit(_where)/select_n | solution.py:19
  214.7 4.1 %fusion.25 = f32[32,128,128]{2,1,0:T(8,128)S(1)} fusion(f32[32,128,128]{2,1,0:T(8,128)S(1)} %get-tuple-element.171, f32[16,32,128,128]{3,2,1,0:T(8,128)} %get-tuple-element.180, s32[]{:T(128)} %get-tuple-element.170, f32[]{:T(128)} %bitcast.30, pred[]{:T(512)S(6)} %compare.3, pred[]{:T(512)S(6)} %lt.34), kind=kLoop, calls=%fused_computation.1.clone.1 | loop fusion | flops 2097152 | bytes 6291466 | tf_op jit(solution)/shard_map/while/body/eval_jaxpr/jit(_where)/select_n | solution.py:19
  219.4 4.1 %fusion.25 = f32[32,128,128]{2,1,0:T(8,128)S(1)} fusion(f32[32,128,128]{2,1,0:T(8,128)S(1)} %get-tuple-element.171, f32[16,32,128,128]{3,2,1,0:T(8,128)} %get-tuple-element.180, s32[]{:T(128)} %get-tuple-element.170, f32[]{:T(128)} %bitcast.30, pred[]{:T(512)S(6)} %compare.3, pred[]{:T(512)S(6)} %lt.34), kind=kLoop, calls=%fused_computation.1.clone.1 | loop fusion | flops 2097152 | bytes 6291466 | tf_op jit(solution)/shard_map/while/body/eval_jaxpr/jit(_where)/select_n | solution.py:19
  224.1 4.1 %fusion.25 = f32[32,128,128]{2,1,0:T(8,128)S(1)} fusion(f32[32,128,128]{2,1,0:T(8,128)S(1)} %get-tuple-element.171, f32[16,32,128,128]{3,2,1,0:T(8,128)} %get-tuple-element.180, s32[]{:T(128)} %get-tuple-element.170, f32[]{:T(128)} %bitcast.30, pred[]{:T(512)S(6)} %compare.3, pred[]{:T(512)S(6)} %lt.34), kind=kLoop, calls=%fused_computation.1.clone.1 | loop fusion | flops 2097152 | bytes 6291466 | tf_op jit(solution)/shard_map/while/body/eval_jaxpr/jit(_where)/select_n | solution.py:19
  228.8 4.1 %fusion.25 = f32[32,128,128]{2,1,0:T(8,128)S(1)} fusion(f32[32,128,128]{2,1,0:T(8,128)S(1)} %get-tuple-element.171, f32[16,32,128,128]{3,2,1,0:T(8,128)} %get-tuple-element.180, s32[]{:T(128)} %get-tuple-element.170, f32[]{:T(128)} %bitcast.30, pred[]{:T(512)S(6)} %compare.3, pred[]{:T(512)S(6)} %lt.34), kind=kLoop, calls=%fused_computation.1.clone.1 | loop fusion | flops 2097152 | bytes 6291466 | tf_op jit(solution)/shard_map/while/body/eval_jaxpr/jit(_where)/select_n | solution.py:19
  233.5 4.1 %fusion.25 = f32[32,128,128]{2,1,0:T(8,128)S(1)} fusion(f32[32,128,128]{2,1,0:T(8,128)S(1)} %get-tuple-element.171, f32[16,32,128,128]{3,2,1,0:T(8,128)} %get-tuple-element.180, s32[]{:T(128)} %get-tuple-element.170, f32[]{:T(128)} %bitcast.30, pred[]{:T(512)S(6)} %compare.3, pred[]{:T(512)S(6)} %lt.34), kind=kLoop, calls=%fused_computation.1.clone.1 | loop fusion | flops 2097152 | bytes 6291466 | tf_op jit(solution)/shard_map/while/body/eval_jaxpr/jit(_where)/select_n | solution.py:19
  238.2 4.1 %fusion.25 = f32[32,128,128]{2,1,0:T(8,128)S(1)} fusion(f32[32,128,128]{2,1,0:T(8,128)S(1)} %get-tuple-element.171, f32[16,32,128,128]{3,2,1,0:T(8,128)} %get-tuple-element.180, s32[]{:T(128)} %get-tuple-element.170, f32[]{:T(128)} %bitcast.30, pred[]{:T(512)S(6)} %compare.3, pred[]{:T(512)S(6)} %lt.34), kind=kLoop, calls=%fused_computation.1.clone.1 | loop fusion | flops 2097152 | bytes 6291466 | tf_op jit(solution)/shard_map/while/body/eval_jaxpr/jit(_where)/select_n | solution.py:19
  242.9 4.1 %fusion.25 = f32[32,128,128]{2,1,0:T(8,128)S(1)} fusion(f32[32,128,128]{2,1,0:T(8,128)S(1)} %get-tuple-element.171, f32[16,32,128,128]{3,2,1,0:T(8,128)} %get-tuple-element.180, s32[]{:T(128)} %get-tuple-element.170, f32[]{:T(128)} %bitcast.30, pred[]{:T(512)S(6)} %compare.3, pred[]{:T(512)S(6)} %lt.34), kind=kLoop, calls=%fused_computation.1.clone.1 | loop fusion | flops 2097152 | bytes 6291466 | tf_op jit(solution)/shard_map/while/body/eval_jaxpr/jit(_where)/select_n | solution.py:19
  247.6 4.1 %fusion.25 = f32[32,128,128]{2,1,0:T(8,128)S(1)} fusion(f32[32,128,128]{2,1,0:T(8,128)S(1)} %get-tuple-element.171, f32[16,32,128,128]{3,2,1,0:T(8,128)} %get-tuple-element.180, s32[]{:T(128)} %get-tuple-element.170, f32[]{:T(128)} %bitcast.30, pred[]{:T(512)S(6)} %compare.3, pred[]{:T(512)S(6)} %lt.34), kind=kLoop, calls=%fused_computation.1.clone.1 | loop fusion | flops 2097152 | bytes 6291466 | tf_op jit(solution)/shard_map/while/body/eval_jaxpr/jit(_where)/select_n | solution.py:19
  252.3 4.1 %fusion.25 = f32[32,128,128]{2,1,0:T(8,128)S(1)} fusion(f32[32,128,128]{2,1,0:T(8,128)S(1)} %get-tuple-element.171, f32[16,32,128,128]{3,2,1,0:T(8,128)} %get-tuple-element.180, s32[]{:T(128)} %get-tuple-element.170, f32[]{:T(128)} %bitcast.30, pred[]{:T(512)S(6)} %compare.3, pred[]{:T(512)S(6)} %lt.34), kind=kLoop, calls=%fused_computation.1.clone.1 | loop fusion | flops 2097152 | bytes 6291466 | tf_op jit(solution)/shard_map/while/body/eval_jaxpr/jit(_where)/select_n | solution.py:19
  256.4 1.8 multiply_reduce_fusion
  (37 shorter events, 15.8 us)
Async XLA Ops:
  6.5 179.4 %all-gather.3.cloned.1.call-start = ((), (), s32[]{:S(2)}) async-start(), calls=%async_computation | async-start | bytes 35651584 | tf_op jit(solution)/shard_map/all_gather | solution.py:12
  11.5 1.3 copy-start
  12.8 3.2 %copy-start.2 = (u32[32]{0:T(128)S(1)}, u32[32]{0:T(128)}, u32[]{:S(2)}) copy-start(u32[32]{0:T(128)} %constant.51) | copy-start | bytes 388
  258.2 0.8 copy-start.1
Sparse Core Ops, SparseCore 0:
  14.9 171.0 all-gather.2
where the time goes:
time: 268 us; the launch traced here: 267 us
  waiting for transfers between devices  129 us (48%)
  other arithmetic  74.5 us (28%)
  blocking collectives  35.8 us (13%)
  between operations  14.8 us (6%)
  matrix products  6.44 us (2%)
  local copies, waits for them, and re-layouts  6.37 us (2%)
    all_gather x1, waiting for transfers between devices, prefix(): pieces = jax.tree.map(lambda part: lax.all_gather(part, axis), value)  129 us
    select_n x15, other arithmetic, step(): jnp.where(position < mine, new, old)  61.4 us
    unnamed x1, blocking collectives  35.8 us
    sub x15, other arithmetic, combine_states(): 1.0 - flag_late[0]  8.78 us
  transfers between devices with their start and end apart: 1, of which 1 were waited for; matrix products, arithmetic and copies ran while one was open for 2% of the time, Pallas kernels for 0%

commit v1 on v0

v1 whole, which is shorter than its diff:
```python
import functools

import jax
import jax.numpy as jnp
from jax import lax
from jax.experimental import pallas as pl
from jax.experimental.pallas import tpu as pltpu
from jax.sharding import PartitionSpec as P

HD = 128
CHIPS = 4
F32 = jnp.float32
BF16 = jnp.bfloat16
VM = pl.BlockSpec(memory_space=pltpu.VMEM)
SM = pl.BlockSpec(memory_space=pltpu.SMEM)
PARAMS = pltpu.CompilerParams(vmem_limit_bytes=32 * 1024 * 1024)


def place():
    block = lax.axis_index("ctx")
    return block % 2, (block // 2) % CHIPS, block // (2 * CHIPS), block


def segment_at(starts, position):
    count = jnp.int32(0)
    for i in range(starts.shape[1]):
        count = count + (starts[0, i] <= position).astype(jnp.int32)
    return count


def same(starts, rows, late, early):
    one = segment_at(starts, (late + 1) * rows - 1)
    two = segment_at(starts, (early + 1) * rows - 1)
    return (one == two).astype(F32)


def column(head):
    return pl.ds(pl.multiple_of(head * HD, HD), HD)


def segment_rows(starts, positions):
    count = jnp.zeros(positions.shape, jnp.int32)
    for i in range(starts.shape[1]):
        count = count + (starts[0, i] <= positions).astype(jnp.int32)
    return count


def head_of(core, chip, step, quarter):
    which = lax.bitwise_xor(chip, step // quarter)
    return core * CHIPS * quarter + which * quarter + step % quarter


def summary_kernel(starts, key_ref, value_ref, send_ref, keep_ref):
    core, chip, _, block = place()
    rows, width = key_ref.shape
    half = width // HD // 2
    begin = block * rows
    last = segment_at(starts, begin + rows - 1)
    positions = begin + lax.broadcasted_iota(jnp.int32, (rows, HD), 0)
    kept = segment_rows(starts, positions) == last
    for out, which in ((send_ref, 1 - core), (keep_ref, core)):
        for step in range(half):
            at = column(head_of(which, chip, step, half // CHIPS))
            key = jnp.where(kept, key_ref[:, at].astype(F32), 0.0).astype(BF16)
            out[step * HD:(step + 1) * HD, :] = lax.dot_general(
                key, value_ref[:, at], (((0,), (0,)), ((), ())), preferred_element_type=F32)


def chip_kernel(starts, rows, keep_ref, got_ref, *pieces):
    core, _, _, block = place()
    joined = same(starts, rows, block // 2 * 2 + 1, block // 2 * 2)
    mine = jnp.where(core == 0, joined, 1.0)
    other = jnp.where(core == 0, 1.0, joined)
    size = pieces[0].shape[0]
    for k, piece in enumerate(pieces):
        at = slice(k * size, (k + 1) * size)
        piece[...] = mine * keep_ref[at, :] + other * got_ref[at, :]


def total_kernel(starts, rows, *refs):
    pieces, out = refs[:-1], refs[-1]
    _, chip, group, _ = place()
    first = group * 2 * CHIPS
    total = None
    for k, piece in enumerate(pieces):
        block = first + 2 * lax.bitwise_xor(chip, k) + 1
        term = same(starts, rows, first + 2 * CHIPS - 1, block) * piece[...]
        total = term if total is None else total + term
    out[...] = total


def carry_kernel(starts, rows, shifts, *refs):
    pieces, groups, outs = refs[:CHIPS], refs[CHIPS:CHIPS + shifts], refs[CHIPS + shifts:]
    _, chip, group, _ = place()
    first = group * 2 * CHIPS
    before = None
    for s, total in enumerate(groups):
        block = first - 1 - s * 2 * CHIPS
        term = jnp.where(block >= 0, same(starts, rows, first - 1, block), 0.0) * total[...]
        before = term if before is None else before + term
    for k, out in enumerate(outs):
        target = lax.bitwise_xor(chip, k)
        end = first + 2 * target - 1
        state = same(starts, rows, end, first - 1) * before
        for j, piece in enumerate(pieces):
            source = lax.bitwise_xor(chip, j)
            use = jnp.where(source < target, same(starts, rows, end, first + 2 * source + 1), 0.0)
            state = state + use * piece[...]
        out[...] = state


def pair_kernel(starts, rows, keep_ref, *refs):
    pieces, out = refs[:-1], refs[-1]
    core, _, _, block = place()
    joined = same(starts, rows, block, block - 1)
    scale = jnp.where(core == 0, joined, 1.0)
    add = jnp.where(core == 0, 1.0, 0.0)
    size = pieces[0].shape[0]
    for k, piece in enumerate(pieces):
        at = slice(k * size, (k + 1) * size)
        out[at, :] = scale * piece[...] + add * keep_ref[at, :]


def intra_kernel(starts, query_ref, key_ref, value_ref, out_ref):
    _, _, _, block = place()
    rows, width = query_ref.shape
    begin = block * rows
    late = begin + lax.broadcasted_iota(jnp.int32, (rows, rows), 0)
    early = begin + lax.broadcasted_iota(jnp.int32, (rows, rows), 1)
    allowed = (late >= early) & (segment_rows(starts, late) == segment_rows(starts, early))
    for head in range(width // HD):
        at = slice(head * HD, (head + 1) * HD)
        scores = lax.dot_general(
            query_ref[:, at], key_ref[:, at], (((1,), (1,)), ((), ())), preferred_element_type=F32)
        weights = jnp.where(allowed, scores, 0.0).astype(BF16)
        out_ref[:, at] = jnp.dot(weights, value_ref[:, at], preferred_element_type=F32)


def final_kernel(starts, query_ref, intra_ref, gain_ref, got_ref, sibling_ref, *refs):
    pieces, out_ref, mixed = refs[:CHIPS], refs[CHIPS], refs[CHIPS + 1]
    core, chip, _, block = place()
    rows, width = query_ref.shape
    half = width // HD // 2
    quarter = half // CHIPS
    begin = block * rows
    prior = segment_at(starts, begin - 1)
    positions = begin + lax.broadcasted_iota(jnp.int32, (rows, HD), 0)
    use = (segment_rows(starts, positions) == prior).astype(F32)
    joined = same(starts, rows, block - 1, block - 2)
    scale = jnp.where(core == 0, 1.0, joined)
    add = jnp.where(core == 0, 0.0, 1.0)
    squares = jnp.zeros((rows, HD), F32)
    for own in (True, False):
        which = core if own else 1 - core
        for step in range(half):
            at = column(head_of(which, chip, step, quarter))
            if own:
                part = (step % quarter) * HD
                state = scale * pieces[step // quarter][part:part + HD, :]
                state = state + add * got_ref[step * HD:(step + 1) * HD, :]
            else:
                state = sibling_ref[step * HD:(step + 1) * HD, :]
            inter = jnp.dot(query_ref[:, at], state.astype(BF16), preferred_element_type=F32)
            both = intra_ref[:, at] + use * inter
            mixed[:, at] = both
            squares = squares + both * both
    mean = jnp.sum(squares, axis=-1, keepdims=True) * (1.0 / width)
    norm = jnp.broadcast_to(lax.rsqrt(mean + 1e-05), (rows, HD))
    for head in range(width // HD):
        at = slice(head * HD, (head + 1) * HD)
        out_ref[:, at] = (mixed[:, at] * norm * gain_ref[:, at]).astype(BF16)


def arrays(shape, count, dtype=F32):
    return [jax.ShapeDtypeStruct(shape, dtype)] * count


def shards(count, query_rows, key_rows, value_rows, seg_starts, norm_gain):
    query, key, value = query_rows[0], key_rows[0], value_rows[0]
    rows, width = query.shape
    tall = width // 2
    groups = count // (2 * CHIPS)

    def call(kernel, outs, *args, scratch=()):
        return pl.pallas_call(
            kernel, out_shape=outs, in_specs=[SM] + [VM] * len(args),
            out_specs=jax.tree.map(lambda _: VM, outs), scratch_shapes=scratch, compiler_params=PARAMS,
        )(seg_starts, *args)

    def swap(array, bits):
        return lax.ppermute(array, "ctx", [(i, i ^ bits) for i in range(count)])

    send, keep = call(summary_kernel, arrays((tall, HD), 2), key, value)
    got = swap(send, 1)
    intra = call(intra_kernel, arrays((rows, width), 1)[0], query, key, value)
    lane = (tall // CHIPS, HD)
    own = call(lambda s, *r: chip_kernel(s, rows, *r), arrays(lane, CHIPS), keep, got)
    pieces = [own[0]] + [swap(own[k], 2 * k) for k in range(1, CHIPS)]
    total = call(lambda s, *r: total_kernel(s, rows, *r), arrays(lane, 1)[0], *pieces)
    before = [
        lax.ppermute(total, "ctx", [(i, i + shift * 2 * CHIPS) for i in range(count - shift * 2 * CHIPS)])
        for shift in range(1, groups)
    ]
    outs = call(lambda s, *r: carry_kernel(s, rows, groups - 1, *r), arrays(lane, CHIPS), *pieces, *before)
    states = [outs[0]] + [swap(outs[k], 2 * k) for k in range(1, CHIPS)]
    sibling = swap(call(lambda s, *r: pair_kernel(s, rows, *r), arrays((tall, HD), 1)[0], keep, *states), 1)
    attended = call(
        final_kernel, jax.ShapeDtypeStruct((rows, width), BF16), query, intra, norm_gain[None, :], got, sibling,
        *states, scratch=[pltpu.VMEM((rows, width), F32)])
    return attended[None]


def solution(mesh):
    placed = (
        P("sess", "ctx", None),
        P("sess", "ctx", None),
        P("sess", "ctx", None),
        P("sess", None),
        P(),
    )
    return jax.shard_map(
        functools.partial(shards, mesh.shape["ctx"]), mesh=mesh, in_specs=placed,
        out_specs=P("sess", "ctx", None), check_vma=False
    )
```

time: 268 us -> 63.7 us (0.24)
  waiting for transfers between devices: 129 us -> 30.7 us
  other arithmetic: 74.5 us -> 0 us
  blocking collectives: 35.8 us -> 0 us
  starting transfers between devices: 0.01 us -> 18.4 us
  between operations: 14.8 us -> 0.07 us
  Pallas kernels: 0 us -> 11 us
  matrix products: 6.44 us -> 0 us
  local copies, waits for them, and re-layouts: 6.37 us -> 3.35 us
    all_gather x1 -> x0, waiting for transfers between devices: 129 us -> none  [prefix(): pieces = jax.tree.map(lambda part: lax.all_gather(part, axis), value)]
    select_n x15 -> x0, other arithmetic: 61.4 us -> none  [step(): jnp.where(position < mine, new, old)]
    unnamed x1 -> x0, blocking collectives: 35.8 us -> none
    ppermute x0 -> x9, waiting for transfers between devices: none -> 30.7 us  [the longest x8 25.9 us: swap(): return lax.ppermute(array, 'ctx', [(i, i ^ bits) for i in range(count)])]
    ppermute x0 -> x9, starting transfers between devices: none -> 18.4 us  [the longest x8 13.8 us: swap(): return lax.ppermute(array, 'ctx', [(i, i ^ bits) for i in range(count)])]
    pallas_call x0 -> x7, Pallas kernels: none -> 11 us  [call(): pl.pallas_call(kernel, out_shape=outs, in_specs=[SM] + [VM] * len(args),...]
    sub x15 -> x0, other arithmetic: 8.78 us -> none  [combine_states(): 1.0 - flag_late[0]]
    dot_general x3 -> x0, matrix products: 6.44 us -> none  [the longest x1 2.7 us: shards(): jnp.einsum('htu,uhe->the', weights, value_heads, preferred_element_type=j...]
  transfers between devices with their start and end apart: 1 -> 9, of which waited for: 1 -> 7; matrix products, arithmetic and copies ran while one was open for 2% -> 0% of each run, Pallas kernels for 0% -> 8%
where the time goes in v1:
time: 63.7 us; the launch traced here: 63.5 us
  waiting for transfers between devices  30.7 us (48%)
  starting transfers between devices  18.4 us (29%)
  Pallas kernels  11 us (17%)
  local copies, waits for them, and re-layouts  3.35 us (5%)
    ppermute x8, waiting for transfers between devices, swap(): return lax.ppermute(array, 'ctx', [(i, i ^ bits) for i in range(count)])  25.9 us
    ppermute x8, starting transfers between devices, swap(): return lax.ppermute(array, 'ctx', [(i, i ^ bits) for i in range(count)])  13.8 us
    pallas_call x7, Pallas kernels, call(): pl.pallas_call(kernel, out_shape=outs, in_specs=[SM] + [VM] * len(args),...  11 us
    ppermute x1, waiting for transfers between devices, shards(): lax.ppermute(total, 'ctx', [(i, i + shift * 2 * CHIPS) for i in range(cou...  4.72 us
    ppermute x1, starting transfers between devices, shards(): lax.ppermute(total, 'ctx', [(i, i + shift * 2 * CHIPS) for i in range(cou...  4.65 us
    unnamed x14, local copies, waits for them, and re-layouts  3.35 us
  transfers between devices with their start and end apart: 9, of which 7 were waited for; matrix products, arithmetic and copies ran while one was open for 0% of the time, Pallas kernels for 8%

profile of v1, /device:TPU:0, one launch (start us, length us, event | category | flops | bytes accessed | tf_op | source)
XLA Modules:
  0.0 63.5 jit_solution(217473357086976425)
XLA Ops:
  0.0 0.7 %copy-done.5 = s32[1,4]{1,0:T(1,128)S(1)} copy-done((s32[1,4]{1,0:T(1,128)S(1)}, s32[1,4]{1,0:T(1,128)}, u32[]{:S(2)}) %copy-start.5) | copy-done | bytes 40
  0.7 1.0 %copy-done = bf16[1,64,4096]{2,1,0:T(8,128)(2,1)S(1)} copy-done((bf16[1,64,4096]{2,1,0:T(8,128)(2,1)S(1)}, bf16[1,64,4096]{2,1,0:T(8,128)(2,1)}, u32[]{:S(2)}) %copy-start) | copy-done | bytes 524312
  1.7 1.0 %copy-done.2 = bf16[1,64,4096]{2,1,0:T(8,128)(2,1)S(1)} copy-done((bf16[1,64,4096]{2,1,0:T(8,128)(2,1)S(1)}, bf16[1,64,4096]{2,1,0:T(8,128)(2,1)}, u32[]{:S(2)}) %copy-start.2) | copy-done | bytes 524312
  2.7 1.0 %shard_map.56 = (f32[2048,128]{1,0:T(8,128)S(1)}, f32[2048,128]{1,0:T(8,128)S(1)}) custom-call(s32[1,4]{1,0:T(1,128)S(1)} %copy-done.5, bf16[64,4096]{1,0:T(8,128)(2,1)S(1)} %bitcast.5, bf16[64,4096]{1,0:T(8,128)(2,1)S(1)} %bitcast.7), custom_call_target="tpu_custom_call" | custom-call | tf_op jit(solution)/shard_map/pallas_call | solution.py:185
  3.8 0.5 collective-permute-start
  4.3 2.3 %collective-permute-done.r_1_.got_ref = f32[2048,128]{1,0:T(8,128)S(1)} collective-permute-done((f32[2048,128]{1,0:T(8,128)S(1)}, f32[2048,128]{1,0:T(8,128)S(1)}, u32[]{:S(2)}, u32[]{:S(2)}) %collective-permute-start) | collective-permute-done | bytes 1048608 | tf_op jit(solution)/shard_map/ppermute | solution.py:191
  6.6 0.7 %shard_map.57 = (f32[512,128]{1,0:T(8,128)S(1)}, f32[512,128]{1,0:T(8,128)S(1)}, f32[512,128]{1,0:T(8,128)S(1)}, f32[512,128]{1,0:T(8,128)S(1)}) custom-call(s32[1,4]{1,0:T(1,128)S(1)} %copy-done.5, f32[2048,128]{1,0:T(8,128)S(1)} %get-tuple-element.16.r_0_, f32[2048,128]{1,0:T(8,128)S(1)} %collective-permute-done.r_1_.got_ref), custom_call_target="tpu_custom_call" | custom-call | tf_op jit(solution)/shard_map/pallas_call | solution.py:185
  7.3 3.0 %collective-permute-start.1 = (f32[512,128]{1,0:T(8,128)S(1)}, f32[512,128]{1,0:T(8,128)S(1)}, u32[]{:S(2)}, u32[]{:S(2)}) collective-permute-start(f32[512,128]{1,0:T(8,128)S(1)} %get-tuple-element.18), channel_id=1, source_target_pairs={{0,2},{1,3},{2,0},{3,1},{4,6},{5,7},{6,4},{7,5},{8,10},{9,11},{10,... | collective-permute-start | bytes 786440 | tf_op jit(solution)/shard_map/ppermute | solution.py:191
  10.2 1.6 %collective-permute-start.2 = (f32[512,128]{1,0:T(8,128)S(1)}, f32[512,128]{1,0:T(8,128)S(1)}, u32[]{:S(2)}, u32[]{:S(2)}) collective-permute-start(f32[512,128]{1,0:T(8,128)S(1)} %get-tuple-element.19), channel_id=1, source_target_pairs={{0,4},{1,5},{2,6},{3,7},{4,0},{5,1},{6,2},{7,3},{8,12},{9,13},{10,... | collective-permute-start | bytes 786440 | tf_op jit(solution)/shard_map/ppermute | solution.py:191
  11.8 5.0 %collective-permute-done.1.r_1_ = f32[512,128]{1,0:T(8,128)S(1)} collective-permute-done((f32[512,128]{1,0:T(8,128)S(1)}, f32[512,128]{1,0:T(8,128)S(1)}, u32[]{:S(2)}, u32[]{:S(2)}) %collective-permute-start.1) | collective-permute-done | bytes 262176 | tf_op jit(solution)/shard_map/ppermute | solution.py:191
  16.8 2.6 %collective-permute-done.2.r_2_ = f32[512,128]{1,0:T(8,128)S(1)} collective-permute-done((f32[512,128]{1,0:T(8,128)S(1)}, f32[512,128]{1,0:T(8,128)S(1)}, u32[]{:S(2)}, u32[]{:S(2)}) %collective-permute-start.2) | collective-permute-done | bytes 262176 | tf_op jit(solution)/shard_map/ppermute | solution.py:191
  19.4 4.3 %collective-permute-done.3.r_3_ = f32[512,128]{1,0:T(8,128)S(1)} collective-permute-done((f32[512,128]{1,0:T(8,128)S(1)}, f32[512,128]{1,0:T(8,128)S(1)}, u32[]{:S(2)}, u32[]{:S(2)}) %collective-permute-start.3) | collective-permute-done | bytes 262176 | tf_op jit(solution)/shard_map/ppermute | solution.py:191
  23.7 0.6 %shard_map.58 = f32[512,128]{1,0:T(8,128)S(1)} custom-call(s32[1,4]{1,0:T(1,128)S(1)} %copy-done.5, f32[512,128]{1,0:T(8,128)S(1)} %get-tuple-element.17.r_0_, f32[512,128]{1,0:T(8,128)S(1)} %collective-permute-done.1.r_1_, f32[512,128]{1,0:T(8,128)S(1)} %collective-permute-done.2.r_2_, f32[512,128]{1,0:T(8,128)S(1)} %collective-permute-done.3.r_3_), custom_call_target="tpu_custom_call" | custom-call | tf_op jit(solution)/shard_map/pallas_call | solution.py:185
  24.4 4.7 %collective-permute-start.4 = (f32[512,128]{1,0:T(8,128)S(1)}, f32[512,128]{1,0:T(8,128)S(1)}, u32[]{:S(2)}, u32[]{:S(2)}) collective-permute-start(f32[512,128]{1,0:T(8,128)S(1)} %shard_map.58), channel_id=1, source_target_pairs={{0,8},{1,9},{2,10},{3,11},{4,12},{5,13},{6,14},{7,15},{16,24},{17,... | collective-permute-start | bytes 786440 | tf_op jit(solution)/shard_map/ppermute | solution.py:201
  29.0 4.7 %collective-permute-done.4.r_4_ = f32[512,128]{1,0:T(8,128)S(1)} collective-permute-done((f32[512,128]{1,0:T(8,128)S(1)}, f32[512,128]{1,0:T(8,128)S(1)}, u32[]{:S(2)}, u32[]{:S(2)}) %collective-permute-start.4) | collective-permute-done | bytes 262176 | tf_op jit(solution)/shard_map/ppermute | solution.py:201
  33.7 0.9 %shard_map.59 = (f32[512,128]{1,0:T(8,128)S(1)}, f32[512,128]{1,0:T(8,128)S(1)}, f32[512,128]{1,0:T(8,128)S(1)}, f32[512,128]{1,0:T(8,128)S(1)}) custom-call(s32[1,4]{1,0:T(1,128)S(1)} %copy-done.5, f32[512,128]{1,0:T(8,128)S(1)} %get-tuple-element.17.r_0_, f32[512,128]{1,0:T(8,128)S(1)} %collective-permute-done.1.r_1_, ...), custom_call_target="tpu_custom_call" | custom-call | tf_op jit(solution)/shard_map/pallas_call | solution.py:185
  34.7 1.6 %collective-permute-start.5 = (f32[512,128]{1,0:T(8,128)S(1)}, f32[512,128]{1,0:T(8,128)S(1)}, u32[]{:S(2)}, u32[]{:S(2)}) collective-permute-start(f32[512,128]{1,0:T(8,128)S(1)} %get-tuple-element.22), channel_id=1, source_target_pairs={{0,2},{1,3},{2,0},{3,1},{4,6},{5,7},{6,4},{7,5},{8,10},{9,11},{10,... | collective-permute-start | bytes 786440 | tf_op jit(solution)/shard_map/ppermute | solution.py:191
  36.3 7.0 %collective-permute-start.6 = (f32[512,128]{1,0:T(8,128)S(1)}, f32[512,128]{1,0:T(8,128)S(1)}, u32[]{:S(2)}, u32[]{:S(2)}) collective-permute-start(f32[512,128]{1,0:T(8,128)S(1)} %get-tuple-element.23), channel_id=1, source_target_pairs={{0,4},{1,5},{2,6},{3,7},{4,0},{5,1},{6,2},{7,3},{8,12},{9,13},{10,... | collective-permute-start | bytes 786440 | tf_op jit(solution)/shard_map/ppermute | solution.py:191
  43.3 7.1 %collective-permute-done.6.r_3_.refs_2_ = f32[512,128]{1,0:T(8,128)S(1)} collective-permute-done((f32[512,128]{1,0:T(8,128)S(1)}, f32[512,128]{1,0:T(8,128)S(1)}, u32[]{:S(2)}, u32[]{:S(2)}) %collective-permute-start.6) | collective-permute-done | bytes 262176 | tf_op jit(solution)/shard_map/ppermute | solution.py:191
  50.4 4.6 %collective-permute-done.7.r_4_.refs_3_ = f32[512,128]{1,0:T(8,128)S(1)} collective-permute-done((f32[512,128]{1,0:T(8,128)S(1)}, f32[512,128]{1,0:T(8,128)S(1)}, u32[]{:S(2)}, u32[]{:S(2)}) %collective-permute-start.7) | collective-permute-done | bytes 262176 | tf_op jit(solution)/shard_map/ppermute | solution.py:191
  55.1 0.7 %shard_map.60 = f32[2048,128]{1,0:T(8,128)S(1)} custom-call(s32[1,4]{1,0:T(1,128)S(1)} %copy-done.5, f32[2048,128]{1,0:T(8,128)S(1)} %get-tuple-element.16.r_0_, f32[512,128]{1,0:T(8,128)S(1)} %get-tuple-element.21.r_1_.refs_0_, f32[512,128]{1,0:T(8,128)S(1)} %collective-permute-done.5.r_2_.refs_1_, f32[512,128]{1,0:T(8,128)S(1)} %collective-permute-done.6.r_3_.refs_2_, ...), custom_call_target="tpu_custom_call" | custom-call | tf_op jit(solution)/shard_map/pallas_call | solution.py:185
  55.8 0.3 copy-done.1
  56.4 4.9 %shard_map.55.intra_ref = f32[64,4096]{1,0:T(8,128)S(1)} custom-call(s32[1,4]{1,0:T(1,128)S(1)} %copy-done.5, bf16[64,4096]{1,0:T(8,128)(2,1)S(1)} %bitcast.9, bf16[64,4096]{1,0:T(8,128)(2,1)S(1)} %bitcast.6, bf16[64,4096]{1,0:T(8,128)(2,1)S(1)} %bitcast.8), custom_call_target="tpu_custom_call" | custom-call | tf_op jit(solution)/shard_map/pallas_call | solution.py:185
  61.4 2.1 %shard_map.61 = bf16[64,4096]{1,0:T(8,128)(2,1)} custom-call(s32[1,4]{1,0:T(1,128)S(1)} %copy-done.5, bf16[64,4096]{1,0:T(8,128)(2,1)S(1)} %bitcast.10, f32[64,4096]{1,0:T(8,128)S(1)} %shard_map.55.intra_ref, f32[1,4096]{1,0:T(1,128)S(1)} %bitcast.11, f32[2048,128]{1,0:T(8,128)S(1)} %collective-permute-done.r_1_.got_ref, ...), custom_call_target="tpu_custom_call" | custom-call | tf_op jit(solution)/shard_map/pallas_call | solution.py:185
  (15 shorter events, 0.4 us)
Async XLA Ops:
  0.0 0.7 %copy-start.5 = (s32[1,4]{1,0:T(1,128)S(1)}, s32[1,4]{1,0:T(1,128)}, u32[]{:S(2)}) copy-start(s32[1,4]{1,0:T(1,128)} %starts.5) | copy-start | bytes 52
  0.7 1.0 %copy-start = (bf16[1,64,4096]{2,1,0:T(8,128)(2,1)S(1)}, bf16[1,64,4096]{2,1,0:T(8,128)(2,1)}, u32[]{:S(2)}) copy-start(bf16[1,64,4096]{2,1,0:T(8,128)(2,1)} %param.6) | copy-start | bytes 1572868
  1.7 1.0 %copy-start.2 = (bf16[1,64,4096]{2,1,0:T(8,128)(2,1)S(1)}, bf16[1,64,4096]{2,1,0:T(8,128)(2,1)}, u32[]{:S(2)}) copy-start(bf16[1,64,4096]{2,1,0:T(8,128)(2,1)} %param.7) | copy-start | bytes 1572868
  3.8 2.8 %collective-permute-start = (f32[2048,128]{1,0:T(8,128)S(1)}, f32[2048,128]{1,0:T(8,128)S(1)}, u32[]{:S(2)}, u32[]{:S(2)}) collective-permute-start(f32[2048,128]{1,0:T(8,128)S(1)} %get-tuple-element.15), channel_id=1, source_target_pairs={{0,1},{1,0},{2,3},{3,2},{4,5},{5,4},{6,7},{7,6},{8,9},{9,8},{10,11... | collective-permute-start | bytes 3145736 | tf_op jit(solution)/shard_map/ppermute | solution.py:191
  7.3 9.6 %collective-permute-start.1 = (f32[512,128]{1,0:T(8,128)S(1)}, f32[512,128]{1,0:T(8,128)S(1)}, u32[]{:S(2)}, u32[]{:S(2)}) collective-permute-start(f32[512,128]{1,0:T(8,128)S(1)} %get-tuple-element.18), channel_id=1, source_target_pairs={{0,2},{1,3},{2,0},{3,1},{4,6},{5,7},{6,4},{7,5},{8,10},{9,11},{10,... | collective-permute-start | bytes 786440 | tf_op jit(solution)/shard_map/ppermute | solution.py:191
  10.2 9.2 %collective-permute-start.2 = (f32[512,128]{1,0:T(8,128)S(1)}, f32[512,128]{1,0:T(8,128)S(1)}, u32[]{:S(2)}, u32[]{:S(2)}) collective-permute-start(f32[512,128]{1,0:T(8,128)S(1)} %get-tuple-element.19), channel_id=1, source_target_pairs={{0,4},{1,5},{2,6},{3,7},{4,0},{5,1},{6,2},{7,3},{8,12},{9,13},{10,... | collective-permute-start | bytes 786440 | tf_op jit(solution)/shard_map/ppermute | solution.py:191
  11.8 11.9 %collective-permute-start.3 = (f32[512,128]{1,0:T(8,128)S(1)}, f32[512,128]{1,0:T(8,128)S(1)}, u32[]{:S(2)}, u32[]{:S(2)}) collective-permute-start(f32[512,128]{1,0:T(8,128)S(1)} %get-tuple-element.20), channel_id=1, source_target_pairs={{0,6},{1,7},{2,4},{3,5},{4,2},{5,3},{6,0},{7,1},{8,14},{9,15},{10,... | collective-permute-start | bytes 786440 | tf_op jit(solution)/shard_map/ppermute | solution.py:191
  24.4 9.4 %collective-permute-start.4 = (f32[512,128]{1,0:T(8,128)S(1)}, f32[512,128]{1,0:T(8,128)S(1)}, u32[]{:S(2)}, u32[]{:S(2)}) collective-permute-start(f32[512,128]{1,0:T(8,128)S(1)} %shard_map.58), channel_id=1, source_target_pairs={{0,8},{1,9},{2,10},{3,11},{4,12},{5,13},{6,14},{7,15},{16,24},{17,... | collective-permute-start | bytes 786440 | tf_op jit(solution)/shard_map/ppermute | solution.py:201
  34.7 8.6 %collective-permute-start.5 = (f32[512,128]{1,0:T(8,128)S(1)}, f32[512,128]{1,0:T(8,128)S(1)}, u32[]{:S(2)}, u32[]{:S(2)}) collective-permute-start(f32[512,128]{1,0:T(8,128)S(1)} %get-tuple-element.22), channel_id=1, source_target_pairs={{0,2},{1,3},{2,0},{3,1},{4,6},{5,7},{6,4},{7,5},{8,10},{9,11},{10,... | collective-permute-start | bytes 786440 | tf_op jit(solution)/shard_map/ppermute | solution.py:191
  36.3 14.2 %collective-permute-start.6 = (f32[512,128]{1,0:T(8,128)S(1)}, f32[512,128]{1,0:T(8,128)S(1)}, u32[]{:S(2)}, u32[]{:S(2)}) collective-permute-start(f32[512,128]{1,0:T(8,128)S(1)} %get-tuple-element.23), channel_id=1, source_target_pairs={{0,4},{1,5},{2,6},{3,7},{4,0},{5,1},{6,2},{7,3},{8,12},{9,13},{10,... | collective-permute-start | bytes 786440 | tf_op jit(solution)/shard_map/ppermute | solution.py:191
  43.3 11.8 %collective-permute-start.7 = (f32[512,128]{1,0:T(8,128)S(1)}, f32[512,128]{1,0:T(8,128)S(1)}, u32[]{:S(2)}, u32[]{:S(2)}) collective-permute-start(f32[512,128]{1,0:T(8,128)S(1)} %get-tuple-element.24), channel_id=1, source_target_pairs={{0,6},{1,7},{2,4},{3,5},{4,2},{5,3},{6,0},{7,1},{8,14},{9,15},{10,... | collective-permute-start | bytes 786440 | tf_op jit(solution)/shard_map/ppermute | solution.py:191
  55.1 1.0 %copy-start.1 = (bf16[1,64,4096]{2,1,0:T(8,128)(2,1)S(1)}, bf16[1,64,4096]{2,1,0:T(8,128)(2,1)}, u32[]{:S(2)}) copy-start(bf16[1,64,4096]{2,1,0:T(8,128)(2,1)} %param.6) | copy-start | bytes 1572868
  55.1 1.2 %copy-start.3 = (bf16[1,64,4096]{2,1,0:T(8,128)(2,1)S(1)}, bf16[1,64,4096]{2,1,0:T(8,128)(2,1)}, u32[]{:S(2)}) copy-start(bf16[1,64,4096]{2,1,0:T(8,128)(2,1)} %param.7) | copy-start | bytes 1572868
  55.1 1.4 %copy-start.4 = (bf16[1,64,4096]{2,1,0:T(8,128)(2,1)S(1)}, bf16[1,64,4096]{2,1,0:T(8,128)(2,1)}, u32[]{:S(2)}) copy-start(bf16[1,64,4096]{2,1,0:T(8,128)(2,1)} %param.5) | copy-start | bytes 1572868
  55.7 5.6 %collective-permute-start.8 = (f32[2048,128]{1,0:T(8,128)S(1)}, f32[2048,128]{1,0:T(8,128)S(1)}, u32[]{:S(2)}, u32[]{:S(2)}) collective-permute-start(f32[2048,128]{1,0:T(8,128)S(1)} %shard_map.60), channel_id=1, source_target_pairs={{0,1},{1,0},{2,3},{3,2},{4,5},{5,4},{6,7},{7,6},{8,9},{9,8},{10,11... | collective-permute-start | bytes 3145736 | tf_op jit(solution)/shard_map/ppermute | solution.py:191
  56.4 4.9 %copy-start.6 = (f32[4096]{0:T(1024)S(1)}, f32[4096]{0:T(1024)}, u32[]{:S(2)}) copy-start(f32[4096]{0:T(1024)} %param.9) | copy-start | bytes 49156

commit v2 on v1

--- a/solution.py
+++ b/solution.py
@@ -8,10 +8,12 @@
 from jax.sharding import PartitionSpec as P
 
 HD = 128
+PARTS = 2
 CHIPS = 4
 F32 = jnp.float32
 BF16 = jnp.bfloat16
 VM = pl.BlockSpec(memory_space=pltpu.VMEM)
+HB = pl.BlockSpec(memory_space=pltpu.HBM)
 SM = pl.BlockSpec(memory_space=pltpu.SMEM)
 PARAMS = pltpu.CompilerParams(vmem_limit_bytes=32 * 1024 * 1024)
 
@@ -50,35 +52,52 @@
     return core * CHIPS * quarter + which * quarter + step % quarter
 
 
-def summary_kernel(starts, key_ref, value_ref, send_ref, keep_ref):
-    core, chip, _, block = place()
+def summarize(starts, key_ref, value_ref, half, out):
+    _, chip, _, block = place()
     rows, width = key_ref.shape
-    half = width // HD // 2
+    steps = width // HD // 2
     begin = block * rows
     last = segment_at(starts, begin + rows - 1)
     positions = begin + lax.broadcasted_iota(jnp.int32, (rows, HD), 0)
     kept = segment_rows(starts, positions) == last
-    for out, which in ((send_ref, 1 - core), (keep_ref, core)):
-        for step in range(half):
-            at = column(head_of(which, chip, step, half // CHIPS))
-            key = jnp.where(kept, key_ref[:, at].astype(F32), 0.0).astype(BF16)
-            out[step * HD:(step + 1) * HD, :] = lax.dot_general(
-                key, value_ref[:, at], (((0,), (0,)), ((), ())), preferred_element_type=F32)
-
-
-def chip_kernel(starts, rows, keep_ref, got_ref, *pieces):
+    for step in range(steps):
+        at = column(head_of(half, chip, step, steps // CHIPS))
+        key = jnp.where(kept, key_ref[:, at].astype(F32), 0.0).astype(BF16)
+        out[step * HD:(step + 1) * HD, :] = lax.dot_general(
+            key, value_ref[:, at], (((0,), (0,)), ((), ())), preferred_element_type=F32)
+
+
+def send_kernel(starts_hbm, key_hbm, value_hbm, send_ref, key_ref, value_ref, starts, sems):
+    copies = [
+        pltpu.make_async_copy(source, target, sems.at[i])
+        for i, (source, target) in enumerate(((starts_hbm, starts), (key_hbm, key_ref), (value_hbm, value_ref)))
+    ]
+    for copy in copies:
+        copy.start()
+    for copy in copies:
+        copy.wait()
+    summarize(starts, key_ref, value_ref, 1 - place()[0], send_ref)
+
+
+def keep_kernel(starts, key_ref, value_ref, keep_ref):
+    summarize(starts, key_ref, value_ref, place()[0], keep_ref)
+
+
+def chip_kernel(part, starts, rows, keep_ref, got_ref, *refs):
+    pieces = refs[-CHIPS:]
     core, _, _, block = place()
     joined = same(starts, rows, block // 2 * 2 + 1, block // 2 * 2)
     mine = jnp.where(core == 0, joined, 1.0)
     other = jnp.where(core == 0, 1.0, joined)
     size = pieces[0].shape[0]
     for k, piece in enumerate(pieces):
-        at = slice(k * size, (k + 1) * size)
+        begin = (k * PARTS + part) * size
+        at = slice(begin, begin + size)
         piece[...] = mine * keep_ref[at, :] + other * got_ref[at, :]
 
 
 def total_kernel(starts, rows, *refs):
-    pieces, out = refs[:-1], refs[-1]
+    pieces, out = refs[:CHIPS], refs[-1]
     _, chip, group, _ = place()
     first = group * 2 * CHIPS
     total = None
@@ -116,28 +135,32 @@
     scale = jnp.where(core == 0, joined, 1.0)
     add = jnp.where(core == 0, 1.0, 0.0)
     size = pieces[0].shape[0]
-    for k, piece in enumerate(pieces):
-        at = slice(k * size, (k + 1) * size)
-        out[at, :] = scale * piece[...] + add * keep_ref[at, :]
-
-
-def intra_kernel(starts, query_ref, key_ref, value_ref, out_ref):
+    for part in range(PARTS):
+        for k in range(CHIPS):
+            begin = (k * PARTS + part) * size
+            at = slice(begin, begin + size)
+            out[at, :] = scale * pieces[part * CHIPS + k][...] + add * keep_ref[at, :]
+
+
+def intra_kernel(heads, starts, query_ref, key_ref, value_ref, *refs):
+    out_ref = refs[-1]
     _, _, _, block = place()
-    rows, width = query_ref.shape
+    rows = query_ref.shape[0]
     begin = block * rows
     late = begin + lax.broadcasted_iota(jnp.int32, (rows, rows), 0)
     early = begin + lax.broadcasted_iota(jnp.int32, (rows, rows), 1)
     allowed = (late >= early) & (segment_rows(starts, late) == segment_rows(starts, early))
-    for head in range(width // HD):
+    for place_out, head in enumerate(heads):
         at = slice(head * HD, (head + 1) * HD)
         scores = lax.dot_general(
             query_ref[:, at], key_ref[:, at], (((1,), (1,)), ((), ())), preferred_element_type=F32)
         weights = jnp.where(allowed, scores, 0.0).astype(BF16)
-        out_ref[:, at] = jnp.dot(weights, value_ref[:, at], preferred_element_type=F32)
-
-
-def final_kernel(starts, query_ref, intra_ref, gain_ref, got_ref, sibling_ref, *refs):
-    pieces, out_ref, mixed = refs[:CHIPS], refs[CHIPS], refs[CHIPS + 1]
+        out_ref[:, place_out * HD:(place_out + 1) * HD] = jnp.dot(
+            weights, value_ref[:, at], preferred_element_type=F32)
+
+
+def final_kernel(starts, query_ref, gain_ref, got_ref, sibling_ref, *refs):
+    intra_refs, pieces, (out_ref, mixed) = refs[:2], refs[2:2 + CHIPS * PARTS], refs[2 + CHIPS * PARTS:]
     core, chip, _, block = place()
     rows, width = query_ref.shape
     half = width // HD // 2
@@ -155,15 +178,19 @@
         for step in range(half):
             at = column(head_of(which, chip, step, quarter))
             if own:
-                part = (step % quarter) * HD
-                state = scale * pieces[step // quarter][part:part + HD, :]
+                size = quarter // PARTS
+                piece = pieces[step % quarter // size * CHIPS + step // quarter]
+                begin = step % size * HD
+                state = scale * piece[begin:begin + HD, :]
                 state = state + add * got_ref[step * HD:(step + 1) * HD, :]
             else:
                 state = sibling_ref[step * HD:(step + 1) * HD, :]
-            inter = jnp.dot(query_ref[:, at], state.astype(BF16), preferred_element_type=F32)
-            both = intra_ref[:, at] + use * inter
-            mixed[:, at] = both
-            squares = squares + both * both
+            mixed[:, at] = use * jnp.dot(query_ref[:, at], state.astype(BF16), preferred_element_type=F32)
+    for head in range(width // HD):
+        at = slice(head * HD, (head + 1) * HD)
+        both = mixed[:, at] + intra_refs[head // half][:, head % half * HD:(head % half + 1) * HD]
+        mixed[:, at] = both
+        squares = squares + both * both
     mean = jnp.sum(squares, axis=-1, keepdims=True) * (1.0 / width)
     norm = jnp.broadcast_to(lax.rsqrt(mean + 1e-05), (rows, HD))
     for head in range(width // HD):
@@ -171,6 +198,10 @@
         out_ref[:, at] = (mixed[:, at] * norm * gain_ref[:, at]).astype(BF16)
 
 
+def in_hbm(array):
+    return pltpu.with_memory_space_constraint(array, pltpu.HBM)
+
+
 def arrays(shape, count, dtype=F32):
     return [jax.ShapeDtypeStruct(shape, dtype)] * count
 
@@ -190,22 +221,45 @@
     def swap(array, bits):
         return lax.ppermute(array, "ctx", [(i, i ^ bits) for i in range(count)])
 
-    send, keep = call(summary_kernel, arrays((tall, HD), 2), key, value)
+    tall_array = arrays((tall, HD), 1)[0]
+    send, key, value = pl.pallas_call(
+        send_kernel, out_shape=[tall_array] + arrays((rows, width), 2, BF16), in_specs=[HB] * 3, out_specs=[VM] * 3,
+        scratch_shapes=[pltpu.SMEM(seg_starts.shape, jnp.int32), pltpu.SemaphoreType.DMA((3,))],
+        compiler_params=PARAMS,
+    )(in_hbm(seg_starts), in_hbm(key), in_hbm(value))
     got = swap(send, 1)
-    intra = call(intra_kernel, arrays((rows, width), 1)[0], query, key, value)
-    lane = (tall // CHIPS, HD)
-    own = call(lambda s, *r: chip_kernel(s, rows, *r), arrays(lane, CHIPS), keep, got)
-    pieces = [own[0]] + [swap(own[k], 2 * k) for k in range(1, CHIPS)]
-    total = call(lambda s, *r: total_kernel(s, rows, *r), arrays(lane, 1)[0], *pieces)
-    before = [
-        lax.ppermute(total, "ctx", [(i, i + shift * 2 * CHIPS) for i in range(count - shift * 2 * CHIPS)])
-        for shift in range(1, groups)
-    ]
-    outs = call(lambda s, *r: carry_kernel(s, rows, groups - 1, *r), arrays(lane, CHIPS), *pieces, *before)
-    states = [outs[0]] + [swap(outs[k], 2 * k) for k in range(1, CHIPS)]
-    sibling = swap(call(lambda s, *r: pair_kernel(s, rows, *r), arrays((tall, HD), 1)[0], keep, *states), 1)
+    keep = call(keep_kernel, tall_array, key, value)
+    lanes = arrays((tall // CHIPS // PARTS, HD), CHIPS)
+    parts, befores, states = [], [], []
+    after = []
+    for part in range(PARTS):
+        own = call(lambda s, *r: chip_kernel(part, s, rows, *r), lanes, keep, got, *after)
+        pieces = [own[0]] + [swap(own[k], 2 * k) for k in range(1, CHIPS)]
+        after = [pieces[1]]
+        parts.append(pieces)
+    heads = width // HD
+
+    def inside(this, *after):
+        span = range(this * heads // 2, (this + 1) * heads // 2)
+        return call(functools.partial(intra_kernel, span), arrays((rows, width // 2), 1)[0], query, key, value, *after)
+
+    after, intra = [], []
+    for pieces in parts:
+        total = call(lambda s, *r: total_kernel(s, rows, *r), lanes[0], *pieces, *after)
+        if not after:
+            intra.append(inside(0, total))
+            after = intra
+        befores.append([
+            lax.ppermute(total, "ctx", [(i, (i + shift * 2 * CHIPS) % count) for i in range(count)])
+            for shift in range(1, groups)
+        ])
+    for pieces, before in zip(parts, befores):
+        outs = call(lambda s, *r: carry_kernel(s, rows, groups - 1, *r), lanes, *pieces, *before)
+        states += [outs[0]] + [swap(outs[k], 2 * k) for k in range(1, CHIPS)]
+    intra.append(inside(1, outs[0]))
+    sibling = swap(call(lambda s, *r: pair_kernel(s, rows, *r), tall_array, keep, *states, intra[1]), 1)
     attended = call(
-        final_kernel, jax.ShapeDtypeStruct((rows, width), BF16), query, intra, norm_gain[None, :], got, sibling,
+        final_kernel, jax.ShapeDtypeStruct((rows, width), BF16), query, norm_gain[None, :], got, sibling, *intra,
         *states, scratch=[pltpu.VMEM((rows, width), F32)])
     return attended[None]
 

time: 63.7 us -> 48.1 us (0.76)
  waiting for transfers between devices: 30.7 us -> 11 us
  Pallas kernels: 11 us -> 14.8 us
  starting transfers between devices: 18.4 us -> 21.4 us
  local copies, waits for them, and re-layouts: 3.35 us -> 0.66 us
    ppermute x8 -> x14, waiting for transfers between devices: 25.9 us -> 9.93 us  [swap(): return lax.ppermute(array, 'ctx', [(i, i ^ bits) for i in range(count)])]
    ppermute x1 -> x2, waiting for transfers between devices: 4.72 us -> 1.04 us  [shards(): lax.ppermute(total, 'ctx', [(i, (i + shift * 2 * CHIPS) % count) for i in...]
    ppermute x8 -> x14, starting transfers between devices: 13.8 us -> 17.1 us  [swap(): return lax.ppermute(array, 'ctx', [(i, i ^ bits) for i in range(count)])]
    unnamed x14 -> x6, local copies, waits for them, and re-layouts: 3.35 us -> 0.66 us
    pallas_call x7 -> x11, Pallas kernels: 11 us -> 13.2 us  [call(): pl.pallas_call(kernel, out_shape=outs, in_specs=[SM] + [VM] * len(args),...]
    pallas_call x0 -> x1, Pallas kernels: none -> 1.58 us  [shards(): pl.pallas_call(send_kernel, out_shape=[tall_array] + arrays((rows, width)...]
    ppermute x1 -> x2, starting transfers between devices: 4.65 us -> 4.26 us  [shards(): lax.ppermute(total, 'ctx', [(i, (i + shift * 2 * CHIPS) % count) for i in...]
  transfers between devices with their start and end apart: 9 -> 16, of which waited for: 7 -> 8; matrix products, arithmetic and copies ran while one was open for 0% -> 0% of each run, Pallas kernels for 8% -> 20%
where the time goes in v2:
time: 48.1 us; the launch traced here: 47.9 us
  starting transfers between devices  21.4 us (44%)
  Pallas kernels  14.8 us (31%)
  waiting for transfers between devices  11 us (23%)
  local copies, waits for them, and re-layouts  0.66 us (1%)
    ppermute x14, starting transfers between devices, swap(): return lax.ppermute(array, 'ctx', [(i, i ^ bits) for i in range(count)])  17.1 us
    pallas_call x11, Pallas kernels, call(): pl.pallas_call(kernel, out_shape=outs, in_specs=[SM] + [VM] * len(args),...  13.2 us
    ppermute x14, waiting for transfers between devices, swap(): return lax.ppermute(array, 'ctx', [(i, i ^ bits) for i in range(count)])  9.93 us
    ppermute x2, starting transfers between devices, shards(): lax.ppermute(total, 'ctx', [(i, (i + shift * 2 * CHIPS) % count) for i in...  4.26 us
    pallas_call x1, Pallas kernels, shards(): pl.pallas_call(send_kernel, out_shape=[tall_array] + arrays((rows, width)...  1.58 us
    ppermute x2, waiting for transfers between devices, shards(): lax.ppermute(total, 'ctx', [(i, (i + shift * 2 * CHIPS) % count) for i in...  1.04 us
  transfers between devices with their start and end apart: 16, of which 8 were waited for; matrix products, arithmetic and copies ran while one was open for 0% of the time, Pallas kernels for 20%

profile of v2, /device:TPU:0, one launch (start us, length us, event | category | flops | bytes accessed | tf_op | source)
XLA Modules:
  0.0 47.9 jit_solution(14028677749645030431)
XLA Ops:
  0.0 1.6 %shard_map.55 = (f32[2048,128]{1,0:T(8,128)S(1)}, bf16[64,4096]{1,0:T(8,128)(2,1)S(1)}, bf16[64,4096]{1,0:T(8,128)(2,1)S(1)}) custom-call(s32[1,4]{1,0:T(1,128)} %starts.7, bf16[64,4096]{1,0:T(8,128)(2,1)} %bitcast.9, bf16[64,4096]{1,0:T(8,128)(2,1)} %bitcast.10), custom_call_target="tpu_custom_call" | custom-call | tf_op jit(solution)/shard_map/pallas_call | solution.py:225
  2.8 0.9 %shard_map.56.r_0_ = f32[2048,128]{1,0:T(8,128)S(1)} custom-call(s32[1,4]{1,0:T(1,128)S(1)} %copy-done.1, bf16[64,4096]{1,0:T(8,128)(2,1)S(1)} %get-tuple-element.25.key_ref, bf16[64,4096]{1,0:T(8,128)(2,1)S(1)} %get-tuple-element.26.value_ref), custom_call_target="tpu_custom_call" | custom-call | tf_op jit(solution)/shard_map/pallas_call | solution.py:216
  3.7 0.7 %collective-permute-done.r_1_.got_ref = f32[2048,128]{1,0:T(8,128)S(1)} collective-permute-done((f32[2048,128]{1,0:T(8,128)S(1)}, f32[2048,128]{1,0:T(8,128)S(1)}, u32[]{:S(2)}, u32[]{:S(2)}) %collective-permute-start) | collective-permute-done | bytes 1048608 | tf_op jit(solution)/shard_map/ppermute | solution.py:222
  5.0 3.0 %collective-permute-start.1 = (f32[256,128]{1,0:T(8,128)S(1)}, f32[256,128]{1,0:T(8,128)S(1)}, u32[]{:S(2)}, u32[]{:S(2)}) collective-permute-start(f32[256,128]{1,0:T(8,128)S(1)} %get-tuple-element.28), channel_id=1, source_target_pairs={{0,2},{1,3},{2,0},{3,1},{4,6},{5,7},{6,4},{7,5},{8,10},{9,11},{10,... | collective-permute-start | bytes 393224 | tf_op jit(solution)/shard_map/ppermute | solution.py:222
  8.0 1.6 %collective-permute-start.2 = (f32[256,128]{1,0:T(8,128)S(1)}, f32[256,128]{1,0:T(8,128)S(1)}, u32[]{:S(2)}, u32[]{:S(2)}) collective-permute-start(f32[256,128]{1,0:T(8,128)S(1)} %get-tuple-element.29), channel_id=1, source_target_pairs={{0,4},{1,5},{2,6},{3,7},{4,0},{5,1},{6,2},{7,3},{8,12},{9,13},{10,... | collective-permute-start | bytes 393224 | tf_op jit(solution)/shard_map/ppermute | solution.py:222
  9.6 2.2 %collective-permute-done.1.r_1_.r_2_ = f32[256,128]{1,0:T(8,128)S(1)} collective-permute-done((f32[256,128]{1,0:T(8,128)S(1)}, f32[256,128]{1,0:T(8,128)S(1)}, u32[]{:S(2)}, u32[]{:S(2)}) %collective-permute-start.1) | collective-permute-done | bytes 131104 | tf_op jit(solution)/shard_map/ppermute | solution.py:222
  12.4 1.8 %collective-permute-start.8 = (f32[256,128]{1,0:T(8,128)S(1)}, f32[256,128]{1,0:T(8,128)S(1)}, u32[]{:S(2)}, u32[]{:S(2)}) collective-permute-start(f32[256,128]{1,0:T(8,128)S(1)} %get-tuple-element.36), channel_id=1, source_target_pairs={{0,2},{1,3},{2,0},{3,1},{4,6},{5,7},{6,4},{7,5},{8,10},{9,11},{10,... | collective-permute-start | bytes 393224 | tf_op jit(solution)/shard_map/ppermute | solution.py:222
  14.2 1.6 %collective-permute-start.9 = (f32[256,128]{1,0:T(8,128)S(1)}, f32[256,128]{1,0:T(8,128)S(1)}, u32[]{:S(2)}, u32[]{:S(2)}) collective-permute-start(f32[256,128]{1,0:T(8,128)S(1)} %get-tuple-element.37), channel_id=1, source_target_pairs={{0,4},{1,5},{2,6},{3,7},{4,0},{5,1},{6,2},{7,3},{8,12},{9,13},{10,... | collective-permute-start | bytes 393224 | tf_op jit(solution)/shard_map/ppermute | solution.py:222
  16.6 2.9 %collective-permute-start.4 = (f32[256,128]{1,0:T(8,128)S(1)}, f32[256,128]{1,0:T(8,128)S(1)}, u32[]{:S(2)}, u32[]{:S(2)}) collective-permute-start(f32[256,128]{1,0:T(8,128)S(1)} %shard_map.58.refs_0_), channel_id=1, source_target_pairs={{0,8},{1,9},{2,10},{3,11},{4,12},{5,13},{6,14},{7,15},{8,0},{9,1},... | collective-permute-start | bytes 393224 | tf_op jit(solution)/shard_map/ppermute | solution.py:253
  19.5 2.8 %shard_map.61.r_4_.refs_0_ = f32[64,2048]{1,0:T(8,128)S(1)} custom-call(s32[1,4]{1,0:T(1,128)S(1)} %copy-done.1, bf16[64,4096]{1,0:T(8,128)(2,1)S(1)} %bitcast.5, bf16[64,4096]{1,0:T(8,128)(2,1)S(1)} %get-tuple-element.25.key_ref, bf16[64,4096]{1,0:T(8,128)(2,1)S(1)} %get-tuple-element.26.value_ref, f32[256,128]{1,0:T(8,128)S(1)} %shard_map.58.refs_0_), custom_call_target="tpu_custom_call" | custom-call | tf_op jit(solution)/shard_map/pallas_call | solution.py:216
  22.3 0.7 %collective-permute-done.9.r_2_ = f32[256,128]{1,0:T(8,128)S(1)} collective-permute-done((f32[256,128]{1,0:T(8,128)S(1)}, f32[256,128]{1,0:T(8,128)S(1)}, u32[]{:S(2)}, u32[]{:S(2)}) %collective-permute-start.9) | collective-permute-done | bytes 131104 | tf_op jit(solution)/shard_map/ppermute | solution.py:222
  23.0 1.5 %collective-permute-done.10.r_3_ = f32[256,128]{1,0:T(8,128)S(1)} collective-permute-done((f32[256,128]{1,0:T(8,128)S(1)}, f32[256,128]{1,0:T(8,128)S(1)}, u32[]{:S(2)}, u32[]{:S(2)}) %collective-permute-start.10) | collective-permute-done | bytes 131104 | tf_op jit(solution)/shard_map/ppermute | solution.py:222
  25.0 1.4 %collective-permute-start.11 = (f32[256,128]{1,0:T(8,128)S(1)}, f32[256,128]{1,0:T(8,128)S(1)}, u32[]{:S(2)}, u32[]{:S(2)}) collective-permute-start(f32[256,128]{1,0:T(8,128)S(1)} %shard_map.62), channel_id=1, source_target_pairs={{0,8},{1,9},{2,10},{3,11},{4,12},{5,13},{6,14},{7,15},{8,0},{9,1},... | collective-permute-start | bytes 393224 | tf_op jit(solution)/shard_map/ppermute | solution.py:253
  26.4 0.7 %shard_map.59 = (f32[256,128]{1,0:T(8,128)S(1)}, f32[256,128]{1,0:T(8,128)S(1)}, f32[256,128]{1,0:T(8,128)S(1)}, f32[256,128]{1,0:T(8,128)S(1)}) custom-call(s32[1,4]{1,0:T(1,128)S(1)} %copy-done.1, f32[256,128]{1,0:T(8,128)S(1)} %get-tuple-element.27.r_0_, f32[256,128]{1,0:T(8,128)S(1)} %collective-permute-done.1.r_1_.r_2_, ...), custom_call_target="tpu_custom_call" | custom-call | tf_op jit(solution)/shard_map/pallas_call | solution.py:216
  27.2 1.5 %collective-permute-start.5 = (f32[256,128]{1,0:T(8,128)S(1)}, f32[256,128]{1,0:T(8,128)S(1)}, u32[]{:S(2)}, u32[]{:S(2)}) collective-permute-start(f32[256,128]{1,0:T(8,128)S(1)} %get-tuple-element.32), channel_id=1, source_target_pairs={{0,2},{1,3},{2,0},{3,1},{4,6},{5,7},{6,4},{7,5},{8,10},{9,11},{10,... | collective-permute-start | bytes 393224 | tf_op jit(solution)/shard_map/ppermute | solution.py:222
  28.6 2.6 %collective-permute-start.6 = (f32[256,128]{1,0:T(8,128)S(1)}, f32[256,128]{1,0:T(8,128)S(1)}, u32[]{:S(2)}, u32[]{:S(2)}) collective-permute-start(f32[256,128]{1,0:T(8,128)S(1)} %get-tuple-element.33), channel_id=1, source_target_pairs={{0,4},{1,5},{2,6},{3,7},{4,0},{5,1},{6,2},{7,3},{8,12},{9,13},{10,... | collective-permute-start | bytes 393224 | tf_op jit(solution)/shard_map/ppermute | solution.py:222
  31.2 1.0 %collective-permute-done.11.r_4_ = f32[256,128]{1,0:T(8,128)S(1)} collective-permute-done((f32[256,128]{1,0:T(8,128)S(1)}, f32[256,128]{1,0:T(8,128)S(1)}, u32[]{:S(2)}, u32[]{:S(2)}) %collective-permute-start.11) | collective-permute-done | bytes 131104 | tf_op jit(solution)/shard_map/ppermute | solution.py:253
  32.2 0.7 %shard_map.63 = (f32[256,128]{1,0:T(8,128)S(1)}, f32[256,128]{1,0:T(8,128)S(1)}, f32[256,128]{1,0:T(8,128)S(1)}, f32[256,128]{1,0:T(8,128)S(1)}) custom-call(s32[1,4]{1,0:T(1,128)S(1)} %copy-done.1, f32[256,128]{1,0:T(8,128)S(1)} %get-tuple-element.35.r_0_, f32[256,128]{1,0:T(8,128)S(1)} %collective-permute-done.8.r_1_, ...), custom_call_target="tpu_custom_call" | custom-call | tf_op jit(solution)/shard_map/pallas_call | solution.py:216
  33.0 1.8 %collective-permute-start.12 = (f32[256,128]{1,0:T(8,128)S(1)}, f32[256,128]{1,0:T(8,128)S(1)}, u32[]{:S(2)}, u32[]{:S(2)}) collective-permute-start(f32[256,128]{1,0:T(8,128)S(1)} %get-tuple-element.40), channel_id=1, source_target_pairs={{0,2},{1,3},{2,0},{3,1},{4,6},{5,7},{6,4},{7,5},{8,10},{9,11},{10,... | collective-permute-start | bytes 393224 | tf_op jit(solution)/shard_map/ppermute | solution.py:222
  35.5 1.9 %collective-permute-start.14 = (f32[256,128]{1,0:T(8,128)S(1)}, f32[256,128]{1,0:T(8,128)S(1)}, u32[]{:S(2)}, u32[]{:S(2)}) collective-permute-start(f32[256,128]{1,0:T(8,128)S(1)} %get-tuple-element.42), channel_id=1, source_target_pairs={{0,6},{1,7},{2,4},{3,5},{4,2},{5,3},{6,0},{7,1},{8,14},{9,15},{10,... | collective-permute-start | bytes 393224 | tf_op jit(solution)/shard_map/ppermute | solution.py:222
  37.4 2.8 %shard_map.64.r_9_.refs_1_ = f32[64,2048]{1,0:T(8,128)S(1)} custom-call(s32[1,4]{1,0:T(1,128)S(1)} %copy-done.1, bf16[64,4096]{1,0:T(8,128)(2,1)S(1)} %bitcast.6, bf16[64,4096]{1,0:T(8,128)(2,1)S(1)} %get-tuple-element.25.key_ref, bf16[64,4096]{1,0:T(8,128)(2,1)S(1)} %get-tuple-element.26.value_ref, f32[256,128]{1,0:T(8,128)S(1)} %get-tuple-element.39.refs_0_.r_5_.refs_6_), custom_call_target="tpu_custom_call" | custom-call | tf_op jit(solution)/shard_map/pallas_call | solution.py:216
  40.6 1.8 %collective-permute-done.14.r_8_.refs_9_ = f32[256,128]{1,0:T(8,128)S(1)} collective-permute-done((f32[256,128]{1,0:T(8,128)S(1)}, f32[256,128]{1,0:T(8,128)S(1)}, u32[]{:S(2)}, u32[]{:S(2)}) %collective-permute-start.14) | collective-permute-done | bytes 131104 | tf_op jit(solution)/shard_map/ppermute | solution.py:222
  43.2 2.6 %collective-permute-done.15.sibling_ref = f32[2048,128]{1,0:T(8,128)S(1)} collective-permute-done((f32[2048,128]{1,0:T(8,128)S(1)}, f32[2048,128]{1,0:T(8,128)S(1)}, u32[]{:S(2)}, u32[]{:S(2)}) %collective-permute-start.15) | collective-permute-done | bytes 1048608 | tf_op jit(solution)/shard_map/ppermute | solution.py:222
  45.8 2.1 %shard_map.66 = bf16[64,4096]{1,0:T(8,128)(2,1)} custom-call(s32[1,4]{1,0:T(1,128)S(1)} %copy-done.1, bf16[64,4096]{1,0:T(8,128)(2,1)S(1)} %bitcast.7, f32[1,4096]{1,0:T(1,128)S(1)} %bitcast.8, f32[2048,128]{1,0:T(8,128)S(1)} %collective-permute-done.r_1_.got_ref, f32[2048,128]{1,0:T(8,128)S(1)} %collective-permute-done.15.sibling_ref, ...), custom_call_target="tpu_custom_call" | custom-call | tf_op jit(solution)/shard_map/pallas_call | solution.py:216
  (26 shorter events, 5.6 us)
Async XLA Ops:
  1.6 2.8 %collective-permute-start = (f32[2048,128]{1,0:T(8,128)S(1)}, f32[2048,128]{1,0:T(8,128)S(1)}, u32[]{:S(2)}, u32[]{:S(2)}) collective-permute-start(f32[2048,128]{1,0:T(8,128)S(1)} %get-tuple-element.24), channel_id=1, source_target_pairs={{0,1},{1,0},{2,3},{3,2},{4,5},{5,4},{6,7},{7,6},{8,9},{9,8},{10,11... | collective-permute-start | bytes 3145736 | tf_op jit(solution)/shard_map/ppermute | solution.py:222
  2.1 0.7 %copy-start.1 = (s32[1,4]{1,0:T(1,128)S(1)}, s32[1,4]{1,0:T(1,128)}, u32[]{:S(2)}) copy-start(s32[1,4]{1,0:T(1,128)} %starts.7) | copy-start | bytes 52
  5.0 6.8 %collective-permute-start.1 = (f32[256,128]{1,0:T(8,128)S(1)}, f32[256,128]{1,0:T(8,128)S(1)}, u32[]{:S(2)}, u32[]{:S(2)}) collective-permute-start(f32[256,128]{1,0:T(8,128)S(1)} %get-tuple-element.28), channel_id=1, source_target_pairs={{0,2},{1,3},{2,0},{3,1},{4,6},{5,7},{6,4},{7,5},{8,10},{9,11},{10,... | collective-permute-start | bytes 393224 | tf_op jit(solution)/shard_map/ppermute | solution.py:222
  8.0 8.0 %collective-permute-start.2 = (f32[256,128]{1,0:T(8,128)S(1)}, f32[256,128]{1,0:T(8,128)S(1)}, u32[]{:S(2)}, u32[]{:S(2)}) collective-permute-start(f32[256,128]{1,0:T(8,128)S(1)} %get-tuple-element.29), channel_id=1, source_target_pairs={{0,4},{1,5},{2,6},{3,7},{4,0},{5,1},{6,2},{7,3},{8,12},{9,13},{10,... | collective-permute-start | bytes 393224 | tf_op jit(solution)/shard_map/ppermute | solution.py:222
  9.6 6.4 %collective-permute-start.3 = (f32[256,128]{1,0:T(8,128)S(1)}, f32[256,128]{1,0:T(8,128)S(1)}, u32[]{:S(2)}, u32[]{:S(2)}) collective-permute-start(f32[256,128]{1,0:T(8,128)S(1)} %get-tuple-element.30), channel_id=1, source_target_pairs={{0,6},{1,7},{2,4},{3,5},{4,2},{5,3},{6,0},{7,1},{8,14},{9,15},{10,... | collective-permute-start | bytes 393224 | tf_op jit(solution)/shard_map/ppermute | solution.py:222
  12.4 7.1 %copy-start = (bf16[1,64,4096]{2,1,0:T(8,128)(2,1)S(1)}, bf16[1,64,4096]{2,1,0:T(8,128)(2,1)}, u32[]{:S(2)}) copy-start(bf16[1,64,4096]{2,1,0:T(8,128)(2,1)} %param.5) | copy-start | bytes 1572868
  12.4 9.9 %collective-permute-start.8 = (f32[256,128]{1,0:T(8,128)S(1)}, f32[256,128]{1,0:T(8,128)S(1)}, u32[]{:S(2)}, u32[]{:S(2)}) collective-permute-start(f32[256,128]{1,0:T(8,128)S(1)} %get-tuple-element.36), channel_id=1, source_target_pairs={{0,2},{1,3},{2,0},{3,1},{4,6},{5,7},{6,4},{7,5},{8,10},{9,11},{10,... | collective-permute-start | bytes 393224 | tf_op jit(solution)/shard_map/ppermute | solution.py:222
  14.2 8.7 %collective-permute-start.9 = (f32[256,128]{1,0:T(8,128)S(1)}, f32[256,128]{1,0:T(8,128)S(1)}, u32[]{:S(2)}, u32[]{:S(2)}) collective-permute-start(f32[256,128]{1,0:T(8,128)S(1)} %get-tuple-element.37), channel_id=1, source_target_pairs={{0,4},{1,5},{2,6},{3,7},{4,0},{5,1},{6,2},{7,3},{8,12},{9,13},{10,... | collective-permute-start | bytes 393224 | tf_op jit(solution)/shard_map/ppermute | solution.py:222
  15.8 8.6 %collective-permute-start.10 = (f32[256,128]{1,0:T(8,128)S(1)}, f32[256,128]{1,0:T(8,128)S(1)}, u32[]{:S(2)}, u32[]{:S(2)}) collective-permute-start(f32[256,128]{1,0:T(8,128)S(1)} %get-tuple-element.38), channel_id=1, source_target_pairs={{0,6},{1,7},{2,4},{3,5},{4,2},{5,3},{6,0},{7,1},{8,14},{9,15},{10,... | collective-permute-start | bytes 393224 | tf_op jit(solution)/shard_map/ppermute | solution.py:222
  16.6 9.8 %collective-permute-start.4 = (f32[256,128]{1,0:T(8,128)S(1)}, f32[256,128]{1,0:T(8,128)S(1)}, u32[]{:S(2)}, u32[]{:S(2)}) collective-permute-start(f32[256,128]{1,0:T(8,128)S(1)} %shard_map.58.refs_0_), channel_id=1, source_target_pairs={{0,8},{1,9},{2,10},{3,11},{4,12},{5,13},{6,14},{7,15},{8,0},{9,1},... | collective-permute-start | bytes 393224 | tf_op jit(solution)/shard_map/ppermute | solution.py:253
  25.0 7.2 %collective-permute-start.11 = (f32[256,128]{1,0:T(8,128)S(1)}, f32[256,128]{1,0:T(8,128)S(1)}, u32[]{:S(2)}, u32[]{:S(2)}) collective-permute-start(f32[256,128]{1,0:T(8,128)S(1)} %shard_map.62), channel_id=1, source_target_pairs={{0,8},{1,9},{2,10},{3,11},{4,12},{5,13},{6,14},{7,15},{8,0},{9,1},... | collective-permute-start | bytes 393224 | tf_op jit(solution)/shard_map/ppermute | solution.py:253
  27.2 8.3 %collective-permute-start.5 = (f32[256,128]{1,0:T(8,128)S(1)}, f32[256,128]{1,0:T(8,128)S(1)}, u32[]{:S(2)}, u32[]{:S(2)}) collective-permute-start(f32[256,128]{1,0:T(8,128)S(1)} %get-tuple-element.32), channel_id=1, source_target_pairs={{0,2},{1,3},{2,0},{3,1},{4,6},{5,7},{6,4},{7,5},{8,10},{9,11},{10,... | collective-permute-start | bytes 393224 | tf_op jit(solution)/shard_map/ppermute | solution.py:222
  28.6 11.6 %collective-permute-start.6 = (f32[256,128]{1,0:T(8,128)S(1)}, f32[256,128]{1,0:T(8,128)S(1)}, u32[]{:S(2)}, u32[]{:S(2)}) collective-permute-start(f32[256,128]{1,0:T(8,128)S(1)} %get-tuple-element.33), channel_id=1, source_target_pairs={{0,4},{1,5},{2,6},{3,7},{4,0},{5,1},{6,2},{7,3},{8,12},{9,13},{10,... | collective-permute-start | bytes 393224 | tf_op jit(solution)/shard_map/ppermute | solution.py:222
  31.2 9.0 %collective-permute-start.7 = (f32[256,128]{1,0:T(8,128)S(1)}, f32[256,128]{1,0:T(8,128)S(1)}, u32[]{:S(2)}, u32[]{:S(2)}) collective-permute-start(f32[256,128]{1,0:T(8,128)S(1)} %get-tuple-element.34), channel_id=1, source_target_pairs={{0,6},{1,7},{2,4},{3,5},{4,2},{5,3},{6,0},{7,1},{8,14},{9,15},{10,... | collective-permute-start | bytes 393224 | tf_op jit(solution)/shard_map/ppermute | solution.py:222
  33.0 7.3 %collective-permute-start.12 = (f32[256,128]{1,0:T(8,128)S(1)}, f32[256,128]{1,0:T(8,128)S(1)}, u32[]{:S(2)}, u32[]{:S(2)}) collective-permute-start(f32[256,128]{1,0:T(8,128)S(1)} %get-tuple-element.40), channel_id=1, source_target_pairs={{0,2},{1,3},{2,0},{3,1},{4,6},{5,7},{6,4},{7,5},{8,10},{9,11},{10,... | collective-permute-start | bytes 393224 | tf_op jit(solution)/shard_map/ppermute | solution.py:222
  34.8 5.8 %collective-permute-start.13 = (f32[256,128]{1,0:T(8,128)S(1)}, f32[256,128]{1,0:T(8,128)S(1)}, u32[]{:S(2)}, u32[]{:S(2)}) collective-permute-start(f32[256,128]{1,0:T(8,128)S(1)} %get-tuple-element.41), channel_id=1, source_target_pairs={{0,4},{1,5},{2,6},{3,7},{4,0},{5,1},{6,2},{7,3},{8,12},{9,13},{10,... | collective-permute-start | bytes 393224 | tf_op jit(solution)/shard_map/ppermute | solution.py:222
  35.5 6.9 %collective-permute-start.14 = (f32[256,128]{1,0:T(8,128)S(1)}, f32[256,128]{1,0:T(8,128)S(1)}, u32[]{:S(2)}, u32[]{:S(2)}) collective-permute-start(f32[256,128]{1,0:T(8,128)S(1)} %get-tuple-element.42), channel_id=1, source_target_pairs={{0,6},{1,7},{2,4},{3,5},{4,2},{5,3},{6,0},{7,1},{8,14},{9,15},{10,... | collective-permute-start | bytes 393224 | tf_op jit(solution)/shard_map/ppermute | solution.py:222
  42.4 3.4 %copy-start.2 = (f32[4096]{0:T(1024)S(1)}, f32[4096]{0:T(1024)}, u32[]{:S(2)}) copy-start(f32[4096]{0:T(1024)} %param.9) | copy-start | bytes 49156
  43.1 2.7 %collective-permute-start.15 = (f32[2048,128]{1,0:T(8,128)S(1)}, f32[2048,128]{1,0:T(8,128)S(1)}, u32[]{:S(2)}, u32[]{:S(2)}) collective-permute-start(f32[2048,128]{1,0:T(8,128)S(1)} %shard_map.65), channel_id=1, source_target_pairs={{0,1},{1,0},{2,3},{3,2},{4,5},{5,4},{6,7},{7,6},{8,9},{9,8},{10,11... | collective-permute-start | bytes 3145736 | tf_op jit(solution)/shard_map/ppermute | solution.py:222

commit v3 on v0

v3 whole, which is shorter than its diff:
```python
import functools

import jax
import jax.numpy as jnp
from jax import lax
from jax.experimental import pallas as pl
from jax.experimental.pallas import tpu as pltpu
from jax.sharding import PartitionSpec as P

HD = 128
CHIPS = 4
SPLIT = (1, 1)
EARLY = (1, 2)
F32 = jnp.float32
BF16 = jnp.bfloat16
HB = pl.BlockSpec(memory_space=pltpu.HBM)
SM = pl.BlockSpec(memory_space=pltpu.SMEM)
VM = pl.BlockSpec(memory_space=pltpu.VMEM)
PARAMS = pltpu.CompilerParams(vmem_limit_bytes=32 * 1024 * 1024)


def place():
    block = lax.axis_index("ctx")
    return block % 2, (block // 2) % CHIPS, block // (2 * CHIPS), block


def segment_at(starts, position):
    count = jnp.int32(0)
    for i in range(starts.shape[1]):
        count = count + (starts[0, i] <= position).astype(jnp.int32)
    return count


def same(starts, rows, late, early):
    one = segment_at(starts, (late + 1) * rows - 1)
    two = segment_at(starts, (early + 1) * rows - 1)
    return (one == two).astype(F32)


def segment_rows(starts, positions):
    count = jnp.zeros(positions.shape, jnp.int32)
    for i in range(starts.shape[1]):
        count = count + (starts[0, i] <= positions).astype(jnp.int32)
    return count


def tile(index):
    return slice(index * HD, (index + 1) * HD)


def sizes(width):
    quarter = width // HD // 2 // CHIPS
    return [quarter * share // sum(SPLIT) for share in SPLIT]


def part_steps(width, part):
    return [(part, k, j) for k in range(CHIPS) for j in range(sizes(width)[part])]


def steps(width):
    return [(own, *step) for own in (True, False) for part in range(len(SPLIT)) for step in part_steps(width, part)]


def column(width, core, chip, own, part, k, j):
    parts = sizes(width)
    quarter = sum(parts)
    half = core if own else 1 - core
    head = (half * CHIPS + lax.bitwise_xor(chip, k)) * quarter + sum(parts[:part]) + j
    return pl.ds(pl.multiple_of(head * HD, HD), HD)


def table_rows(groups):
    names = ["chip_mine", "chip_other", "pair_scale", "pair_add", "mix_scale", "mix_add"]
    names += [("total", k) for k in range(CHIPS)]
    names += [("carry", k, j) for k in range(CHIPS) for j in range(CHIPS)]
    names += [("enter", k) for k in range(CHIPS)]
    names += [("before", s) for s in range(groups - 1)]
    return {name: i for i, name in enumerate(names)}


def weights(starts, rows, groups):
    core, chip, group, block = place()
    same_ = functools.partial(same, starts, rows)
    first = group * 2 * CHIPS
    joined = same_(block // 2 * 2 + 1, block // 2 * 2)
    after, mix = same_(block, block - 1), same_(block - 1, block - 2)
    found = {
        "chip_mine": jnp.where(core == 0, joined, 1.0),
        "chip_other": jnp.where(core == 0, 1.0, joined),
        "pair_scale": jnp.where(core == 0, after, 1.0),
        "pair_add": jnp.where(core == 0, 1.0, 0.0),
        "mix_scale": jnp.where(core == 0, 1.0, mix),
        "mix_add": jnp.where(core == 0, 0.0, 1.0),
    }
    for k in range(CHIPS):
        target = lax.bitwise_xor(chip, k)
        end = first + 2 * target - 1
        found["total", k] = same_(first + 2 * CHIPS - 1, first + 2 * target + 1)
        found["enter", k] = same_(end, first - 1)
        for j in range(CHIPS):
            source = lax.bitwise_xor(chip, j)
            found["carry", k, j] = jnp.where(source < target, same_(end, first + 2 * source + 1), 0.0)
    for s in range(groups - 1):
        block = first - 1 - s * 2 * CHIPS
        found["before", s] = jnp.where(block >= 0, same_(first - 1, block), 0.0)
    return found


def summarize(kept_ref, key_ref, value_ref, own, part, out):
    core, chip, _, _ = place()
    width = key_ref.shape[1]
    kept = kept_ref[...]
    for i, step in enumerate(part_steps(width, part)):
        at = column(width, core, chip, own, *step)
        out[tile(i), :] = lax.dot_general(
            key_ref[:, at] * kept, value_ref[:, at], (((0,), (0,)), ((), ())), preferred_element_type=F32)


def first_kernel(groups, starts_hbm, key_hbm, value_hbm, send_ref, key_ref, value_ref, table_ref, kept_ref, allowed_ref,
                 use_ref, starts, sems):
    copies = [
        pltpu.make_async_copy(source, target, sems.at[i])
        for i, (source, target) in enumerate(((starts_hbm, starts), (key_hbm, key_ref), (value_hbm, value_ref)))
    ]
    for copy in copies:
        copy.start()
    copies[0].wait()
    rows = key_ref.shape[0]
    _, _, _, block = place()
    begin = block * rows
    names = table_rows(groups)
    for name, weight in weights(starts, rows, groups).items():
        table_ref[names[name]:names[name] + 1, :] = jnp.full((1, HD), weight, F32)
    segments = segment_rows(starts, begin + lax.broadcasted_iota(jnp.int32, (rows, HD), 0))
    kept_ref[...] = (segments == segment_at(starts, begin + rows - 1)).astype(F32).astype(BF16)
    use_ref[...] = (segments == segment_at(starts, begin - 1)).astype(F32)
    late = begin + lax.broadcasted_iota(jnp.int32, (rows, rows), 0)
    early = begin + lax.broadcasted_iota(jnp.int32, (rows, rows), 1)
    allowed = (late >= early) & (segment_rows(starts, late) == segment_rows(starts, early))
    allowed_ref[...] = allowed.astype(F32)
    for copy in copies[1:]:
        copy.wait()
    summarize(kept_ref, key_ref, value_ref, False, 0, send_ref)


def summary_kernel(what, kept_ref, key_ref, value_ref, *outs):
    for (own, part), out in zip(what, outs):
        summarize(kept_ref, key_ref, value_ref, own, part, out)


def row(table_ref, groups, *name):
    at = table_rows(groups)[name if len(name) > 1 else name[0]]
    return table_ref[at:at + 1, :]


def chip_kernel(weight, keep_ref, got_ref, *refs):
    pieces = refs[-CHIPS:]
    size = pieces[0].shape[0]
    for k, piece in enumerate(pieces):
        at = slice(k * size, (k + 1) * size)
        piece[...] = weight("chip_mine") * keep_ref[at, :] + weight("chip_other") * got_ref[at, :]


def total_kernel(weight, *refs):
    pieces, out = refs[:CHIPS], refs[-1]
    total = None
    for k, piece in enumerate(pieces):
        term = weight("total", k) * piece[...]
        total = term if total is None else total + term
    out[...] = total


def carry_kernel(shifts, weight, *refs):
    pieces, groups, outs = refs[:CHIPS], refs[CHIPS:CHIPS + shifts], refs[-CHIPS:]
    before = None
    for s, total in enumerate(groups):
        term = weight("before", s) * total[...]
        before = term if before is None else before + term
    for k, out in enumerate(outs):
        state = weight("enter", k) * before
        for j, piece in enumerate(pieces):
            if j != k:
                state = state + weight("carry", k, j) * piece[...]
        out[...] = state


def pair_kernel(weight, keep_ref, *refs):
    pieces, out = refs[:CHIPS], refs[-1]
    size = pieces[0].shape[0]
    for k, piece in enumerate(pieces):
        at = slice(k * size, (k + 1) * size)
        out[at, :] = weight("pair_scale") * piece[...] + weight("pair_add") * keep_ref[at, :]


def intra_kernel(on, span, allowed_ref, query_ref, key_ref, value_ref, *refs):
    out_ref = refs[-1]
    core, chip, _, _ = place()
    width = query_ref.shape[1]

    def body():
        allowed = allowed_ref[...]
        for i, step in enumerate(steps(width)[slice(*span)]):
            at = column(width, core, chip, *step)
            scores = lax.dot_general(
                query_ref[:, at], key_ref[:, at], (((1,), (1,)), ((), ())), preferred_element_type=F32)
            out_ref[:, tile(i)] = jnp.dot(
                (scores * allowed).astype(BF16), value_ref[:, at], preferred_element_type=F32)

    if on is None:
        body()
    else:
        pl.when(core == on)(body)


def from_past(use, query_ref, step, state):
    core, chip, _, _ = place()
    at = column(query_ref.shape[1], core, chip, *step)
    return use * jnp.dot(query_ref[:, at], state.astype(BF16), preferred_element_type=F32)


def mix_kernel(cut, weight, use_ref, query_ref, *refs):
    parts = len(SPLIT)
    intras = refs[:4]
    refs = refs[4:]
    pieces, got_refs, sibling_refs = refs[:CHIPS * parts], refs[CHIPS * parts:][:parts], refs[CHIPS * parts + parts:-2]
    mixed_ref, squares_ref = refs[-2:]
    core, _, _, _ = place()
    rows, width = query_ref.shape
    use = use_ref[...]
    squares = jnp.zeros((rows, HD), F32)
    for i, step in enumerate(steps(width)):
        both = jnp.where(core == 0, intras[2 * (i >= cut)][:, tile(i - cut * (i >= cut))], intras[2 * (i >= cut) + 1][:, tile(i - cut * (i >= cut))])
        own, part, k, j = step
        at = tile(k * sizes(width)[part] + j)
        if own:
            state = weight("mix_scale") * pieces[part * CHIPS + k][tile(j), :] + weight("mix_add") * got_refs[part][at, :]
        elif part < parts - 1:
            state = sibling_refs[part][at, :]
        else:
            mixed_ref[:, tile(i)] = both
            continue
        both = both + from_past(use, query_ref, step, state)
        mixed_ref[:, tile(i)] = both
        squares = squares + both * both
    squares_ref[...] = squares


def norm_kernel(use_ref, query_ref, gain_ref, mixed_ref, squares_ref, sibling_ref, out_ref, last_ref):
    core, chip, _, _ = place()
    rows, width = query_ref.shape
    order = steps(width)
    first = len(order) - sibling_ref.shape[0] // HD
    use = use_ref[...]
    squares = squares_ref[...]
    for i, step in enumerate(order[first:]):
        both = mixed_ref[:, tile(first + i)] + from_past(use, query_ref, step, sibling_ref[tile(i), :])
        last_ref[:, tile(i)] = both
        squares = squares + both * both
    mean = jnp.sum(squares, axis=-1, keepdims=True) * (1.0 / width)
    norm = jnp.broadcast_to(lax.rsqrt(mean + 1e-05), (rows, HD))
    for i, step in enumerate(order):
        at = column(width, core, chip, *step)
        both = mixed_ref[:, tile(i)] if i < first else last_ref[:, tile(i - first)]
        out_ref[:, at] = (both * norm * gain_ref[:, at]).astype(BF16)


def in_hbm(array):
    return pltpu.with_memory_space_constraint(array, pltpu.HBM)


def array(shape, dtype=F32):
    return jax.ShapeDtypeStruct(shape, dtype)


def shards(count, query_rows, key_rows, value_rows, seg_starts, norm_gain):
    query, key, value = query_rows[0], key_rows[0], value_rows[0]
    rows, width = query.shape
    groups = count // (2 * CHIPS)
    parts = range(len(SPLIT))
    heads = len(steps(width))
    lanes = [[array((size * HD, HD))] * CHIPS for size in sizes(width)]
    talls = [array((CHIPS * size * HD, HD)) for size in sizes(width)]

    def call(kernel, outs, *args, scratch=()):
        return pl.pallas_call(
            kernel, out_shape=outs, in_specs=[VM] * len(args), out_specs=jax.tree.map(lambda _: VM, outs),
            scratch_shapes=scratch, compiler_params=PARAMS,
        )(*args)

    def weighted(kernel, outs, *args):
        def body(table_ref, *refs):
            return kernel(functools.partial(row, table_ref, groups), *refs)

        return call(body, outs, table, *args)

    def swap(what, bits):
        return lax.ppermute(what, "ctx", [(i, i ^ bits) for i in range(count)])

    def later(what, shift):
        return lax.ppermute(what, "ctx", [(i, (i + shift * 2 * CHIPS) % count) for i in range(count)])

    def exchange(own):
        return [own[0]] + [swap(own[k], 2 * k) for k in range(1, CHIPS)]

    def intra(on, span, *after):
        out = array((rows, (span[1] - span[0]) * HD))
        return call(functools.partial(intra_kernel, on, span), out, allowed, query, key, value, *after)

    table = array((-(-len(table_rows(groups)) // 8) * 8, HD))
    send, key, value, table, kept, allowed, use = pl.pallas_call(
        functools.partial(first_kernel, groups),
        out_shape=[talls[0]] + [array((rows, width), BF16)] * 2 + [
            table, array((rows, HD), BF16), array((rows, rows)), array((rows, HD))],
        in_specs=[HB] * 3, out_specs=[VM] * 7,
        scratch_shapes=[pltpu.SMEM(seg_starts.shape, jnp.int32), pltpu.SemaphoreType.DMA((3,))],
        compiler_params=PARAMS,
    )(in_hbm(seg_starts), in_hbm(key), in_hbm(value))
    gots, keeps = [], []
    for part in parts:
        gots.append(swap(send, 1))
        what = [(True, part)] + [(False, part + 1)][:len(SPLIT) - 1 - part]
        keep, *send = call(functools.partial(summary_kernel, what), [talls[p] for _, p in what], kept, key, value)
        keeps.append(keep)
        send = send[0] if send else None
    cut = heads * EARLY[0] // EARLY[1]
    zero = intra(0, (0, cut), keeps[0])
    pieces, befores, states, siblings = [], [], [], []
    after = [zero]
    for part in parts:
        own = weighted(chip_kernel, lanes[part], keeps[part], gots[part], *after)
        pieces.append(exchange(own))
        after = [pieces[part][3]]
    after = []
    for part in parts:
        total = weighted(total_kernel, lanes[part][0], *pieces[part], *after)
        if part == 0:
            one = intra(1, (0, cut), total)
            after = [one]
        befores.append([later(total, shift) for shift in range(1, groups)])
    zero_rest = intra(0, (cut, heads), total)
    after = [zero_rest]
    for part in parts:
        outs = weighted(functools.partial(carry_kernel, groups - 1), lanes[part], *pieces[part], *befores[part], *after)
        states.append(exchange(outs))
        if part == 0:
            one_rest = intra(1, (cut, heads), outs[0])
            after = [one_rest]
    for part in parts:
        siblings.append(swap(weighted(pair_kernel, talls[part], keeps[part], *states[part]), 1))
    intras = [zero, one, zero_rest, one_rest]
    mixed, squares = weighted(
        functools.partial(mix_kernel, cut), [array((rows, width)), array((rows, HD))], use, query, *intras,
        *[piece for pieces in states for piece in pieces], *gots, *siblings[:-1])
    attended = call(
        norm_kernel, array((rows, width), BF16), use, query, norm_gain[None, :], mixed, squares, siblings[-1],
        scratch=[pltpu.VMEM((rows, talls[-1].shape[0]), F32)])
    return attended[None]


def solution(mesh):
    placed = (
        P("sess", "ctx", None),
        P("sess", "ctx", None),
        P("sess", "ctx", None),
        P("sess", None),
        P(),
    )
    return jax.shard_map(
        functools.partial(shards, mesh.shape["ctx"]), mesh=mesh, in_specs=placed,
        out_specs=P("sess", "ctx", None), check_vma=False
    )
```

time: 268 us -> 44.6 us (0.17)
  waiting for transfers between devices: 129 us -> 10.6 us
  other arithmetic: 74.5 us -> 0 us
  blocking collectives: 35.8 us -> 0 us
  starting transfers between devices: 0.01 us -> 24.3 us
  between operations: 14.8 us -> 0.12 us
  Pallas kernels: 0 us -> 8.89 us
  matrix products: 6.44 us -> 0 us
  local copies, waits for them, and re-layouts: 6.37 us -> 0.57 us
    all_gather x1 -> x0, waiting for transfers between devices: 129 us -> none  [prefix(): pieces = jax.tree.map(lambda part: lax.all_gather(part, axis), value)]
    select_n x15 -> x0, other arithmetic: 61.4 us -> none  [step(): jnp.where(position < mine, new, old)]
    unnamed x1 -> x0, blocking collectives: 35.8 us -> none
    ppermute x0 -> x18, starting transfers between devices: none -> 24.3 us  [the longest x16 17.1 us: swap(): return lax.ppermute(what, 'ctx', [(i, i ^ bits) for i in range(count)])]
    ppermute x0 -> x18, waiting for transfers between devices: none -> 10.6 us  [the longest x16 10.6 us: swap(): return lax.ppermute(what, 'ctx', [(i, i ^ bits) for i in range(count)])]
    pallas_call x0 -> x17, Pallas kernels: none -> 8.89 us  [the longest x16 7.39 us: call(): pl.pallas_call(kernel, out_shape=outs, in_specs=[VM] * len(args), out_spe...]
    sub x15 -> x0, other arithmetic: 8.78 us -> none  [combine_states(): 1.0 - flag_late[0]]
    dot_general x3 -> x0, matrix products: 6.44 us -> none  [the longest x1 2.7 us: shards(): jnp.einsum('htu,uhe->the', weights, value_heads, preferred_element_type=j...]
  transfers between devices with their start and end apart: 1 -> 18, of which waited for: 1 -> 8; matrix products, arithmetic and copies ran while one was open for 2% -> 0% of each run, Pallas kernels for 0% -> 14%
where the time goes in v3:
time: 44.6 us; the launch traced here: 44.4 us
  starting transfers between devices  24.3 us (54%)
  waiting for transfers between devices  10.6 us (24%)
  Pallas kernels  8.89 us (20%)
  local copies, waits for them, and re-layouts  0.57 us (1%)
    ppermute x16, starting transfers between devices, swap(): return lax.ppermute(what, 'ctx', [(i, i ^ bits) for i in range(count)])  17.1 us
    ppermute x16, waiting for transfers between devices, swap(): return lax.ppermute(what, 'ctx', [(i, i ^ bits) for i in range(count)])  10.6 us
    pallas_call x16, Pallas kernels, call(): pl.pallas_call(kernel, out_shape=outs, in_specs=[VM] * len(args), out_spe...  7.39 us
    ppermute x2, starting transfers between devices, later(): lax.ppermute(what, 'ctx', [(i, (i + shift * 2 * CHIPS) % count) for i in...  7.2 us
    pallas_call x1, Pallas kernels, shards(): pl.pallas_call(functools.partial(first_kernel, groups), out_shape=[talls[...  1.5 us
  transfers between devices with their start and end apart: 18, of which 8 were waited for; matrix products, arithmetic and copies ran while one was open for 0% of the time, Pallas kernels for 14%

profile of v3, /device:TPU:0, one launch (start us, length us, event | category | flops | bytes accessed | tf_op | source)
XLA Modules:
  0.0 44.4 jit_solution(9613907200416626492)
XLA Ops:
  0.0 1.5 %shard_map.55 = (f32[1024,128]{1,0:T(8,128)S(1)}, bf16[64,4096]{1,0:T(8,128)(2,1)S(1)}, bf16[64,4096]{1,0:T(8,128)(2,1)S(1)}, f32[32,128]{1,0:T(8,128)S(1)}, bf1...) custom-call(s32[1,4]{1,0:T(1,128)} %starts_hbm.1, bf16[64,4096]{1,0:T(8,128)(2,1)} %bitcast.12, ...), custom_call_target="tpu_custom_call" | custom-call | tf_op jit(solution)/shard_map/pallas_call | solution.py:310
  1.5 0.5 %collective-permute-start = (f32[1024,128]{1,0:T(8,128)S(1)}, f32[1024,128]{1,0:T(8,128)S(1)}, u32[]{:S(2)}, u32[]{:S(2)}) collective-permute-start(f32[1024,128]{1,0:T(8,128)S(1)} %get-tuple-element.39), channel_id=1, source_target_pairs={{0,1},{1,0},{2,3},{3,2},{4,5},{5,4},{6,7},{7,6},{8,9},{9,8},{10,11... | collective-permute-start | bytes 1572872 | tf_op jit(solution)/shard_map/ppermute | solution.py:297
  2.5 0.6 %copy-done = bf16[1,64,4096]{2,1,0:T(8,128)(2,1)S(1)} copy-done((bf16[1,64,4096]{2,1,0:T(8,128)(2,1)S(1)}, bf16[1,64,4096]{2,1,0:T(8,128)(2,1)}, u32[]{:S(2)}) %copy-start) | copy-done | bytes 524312
  3.1 2.3 %shard_map.57.refs_2_ = f32[64,2048]{1,0:T(8,128)S(1)} custom-call(f32[64,64]{1,0:T(8,128)S(1)} %get-tuple-element.34.allowed_ref, bf16[64,4096]{1,0:T(8,128)(2,1)S(1)} %bitcast.5, bf16[64,4096]{1,0:T(8,128)(2,1)S(1)} %get-tuple-element.35.key_ref, bf16[64,4096]{1,0:T(8,128)(2,1)S(1)} %get-tuple-element.36.value_ref, f32[1024,128]{1,0:T(8,128)S(1)} %get-tuple-element.38.refs_0_), custom_call_target="tpu_custom_call" | custom-call | tf_op jit(solution)/shard_map/pallas_call | solution.py:285
  5.4 3.6 %collective-permute-start.3 = (f32[256,128]{1,0:T(8,128)S(1)}, f32[256,128]{1,0:T(8,128)S(1)}, u32[]{:S(2)}, u32[]{:S(2)}) collective-permute-start(f32[256,128]{1,0:T(8,128)S(1)} %get-tuple-element.43), channel_id=1, source_target_pairs={{0,6},{1,7},{2,4},{3,5},{4,2},{5,3},{6,0},{7,1},{8,14},{9,15},{10,... | collective-permute-start | bytes 393224 | tf_op jit(solution)/shard_map/ppermute | solution.py:297
  9.0 0.5 %collective-permute-start.1 = (f32[256,128]{1,0:T(8,128)S(1)}, f32[256,128]{1,0:T(8,128)S(1)}, u32[]{:S(2)}, u32[]{:S(2)}) collective-permute-start(f32[256,128]{1,0:T(8,128)S(1)} %get-tuple-element.41), channel_id=1, source_target_pairs={{0,2},{1,3},{2,0},{3,1},{4,6},{5,7},{6,4},{7,5},{8,10},{9,11},{10,... | collective-permute-start | bytes 393224 | tf_op jit(solution)/shard_map/ppermute | solution.py:297
  9.9 2.8 %collective-permute-done.3.refs_3_.refs_2_ = f32[256,128]{1,0:T(8,128)S(1)} collective-permute-done((f32[256,128]{1,0:T(8,128)S(1)}, f32[256,128]{1,0:T(8,128)S(1)}, u32[]{:S(2)}, u32[]{:S(2)}) %collective-permute-start.3) | collective-permute-done | bytes 131104 | tf_op jit(solution)/shard_map/ppermute | solution.py:297
  12.8 1.9 %collective-permute-start.5 = (f32[256,128]{1,0:T(8,128)S(1)}, f32[256,128]{1,0:T(8,128)S(1)}, u32[]{:S(2)}, u32[]{:S(2)}) collective-permute-start(f32[256,128]{1,0:T(8,128)S(1)} %get-tuple-element.46), channel_id=1, source_target_pairs={{0,2},{1,3},{2,0},{3,1},{4,6},{5,7},{6,4},{7,5},{8,10},{9,11},{10,... | collective-permute-start | bytes 393224 | tf_op jit(solution)/shard_map/ppermute | solution.py:297
  14.7 1.6 %collective-permute-start.6 = (f32[256,128]{1,0:T(8,128)S(1)}, f32[256,128]{1,0:T(8,128)S(1)}, u32[]{:S(2)}, u32[]{:S(2)}) collective-permute-start(f32[256,128]{1,0:T(8,128)S(1)} %get-tuple-element.47), channel_id=1, source_target_pairs={{0,4},{1,5},{2,6},{3,7},{4,0},{5,1},{6,2},{7,3},{8,12},{9,13},{10,... | collective-permute-start | bytes 393224 | tf_op jit(solution)/shard_map/ppermute | solution.py:297
  16.4 3.4 %collective-permute-start.8 = (f32[256,128]{1,0:T(8,128)S(1)}, f32[256,128]{1,0:T(8,128)S(1)}, u32[]{:S(2)}, u32[]{:S(2)}) collective-permute-start(f32[256,128]{1,0:T(8,128)S(1)} %shard_map.59.refs_0_), channel_id=1, source_target_pairs={{0,8},{1,9},{2,10},{3,11},{4,12},{5,13},{6,14},{7,15},{8,0},{9,1},... | collective-permute-start | bytes 393224 | tf_op jit(solution)/shard_map/ppermute | solution.py:300
  20.1 2.1 %collective-permute-done.7.refs_3_ = f32[256,128]{1,0:T(8,128)S(1)} collective-permute-done((f32[256,128]{1,0:T(8,128)S(1)}, f32[256,128]{1,0:T(8,128)S(1)}, u32[]{:S(2)}, u32[]{:S(2)}) %collective-permute-start.7) | collective-permute-done | bytes 131104 | tf_op jit(solution)/shard_map/ppermute | solution.py:297
  22.2 3.8 %collective-permute-start.12 = (f32[256,128]{1,0:T(8,128)S(1)}, f32[256,128]{1,0:T(8,128)S(1)}, u32[]{:S(2)}, u32[]{:S(2)}) collective-permute-start(f32[256,128]{1,0:T(8,128)S(1)} %shard_map.63.refs_0_), channel_id=1, source_target_pairs={{0,8},{1,9},{2,10},{3,11},{4,12},{5,13},{6,14},{7,15},{8,0},{9,1},... | collective-permute-start | bytes 393224 | tf_op jit(solution)/shard_map/ppermute | solution.py:300
  26.1 2.3 %shard_map.64.refs_5_.refs_4_ = f32[64,2048]{1,0:T(8,128)S(1)} custom-call(f32[64,64]{1,0:T(8,128)S(1)} %get-tuple-element.34.allowed_ref, bf16[64,4096]{1,0:T(8,128)(2,1)S(1)} %bitcast.7, bf16[64,4096]{1,0:T(8,128)(2,1)S(1)} %get-tuple-element.35.key_ref, bf16[64,4096]{1,0:T(8,128)(2,1)S(1)} %get-tuple-element.36.value_ref, f32[256,128]{1,0:T(8,128)S(1)} %shard_map.63.refs_0_), custom_call_target="tpu_custom_call" | custom-call | tf_op jit(solution)/shard_map/pallas_call | solution.py:285
  28.5 0.6 %collective-permute-start.9 = (f32[256,128]{1,0:T(8,128)S(1)}, f32[256,128]{1,0:T(8,128)S(1)}, u32[]{:S(2)}, u32[]{:S(2)}) collective-permute-start(f32[256,128]{1,0:T(8,128)S(1)} %get-tuple-element.50), channel_id=1, source_target_pairs={{0,2},{1,3},{2,0},{3,1},{4,6},{5,7},{6,4},{7,5},{8,10},{9,11},{10,... | collective-permute-start | bytes 393224 | tf_op jit(solution)/shard_map/ppermute | solution.py:297
  29.0 2.4 %collective-permute-start.10 = (f32[256,128]{1,0:T(8,128)S(1)}, f32[256,128]{1,0:T(8,128)S(1)}, u32[]{:S(2)}, u32[]{:S(2)}) collective-permute-start(f32[256,128]{1,0:T(8,128)S(1)} %get-tuple-element.51), channel_id=1, source_target_pairs={{0,4},{1,5},{2,6},{3,7},{4,0},{5,1},{6,2},{7,3},{8,12},{9,13},{10,... | collective-permute-start | bytes 393224 | tf_op jit(solution)/shard_map/ppermute | solution.py:297
  31.4 0.6 %collective-permute-start.11 = (f32[256,128]{1,0:T(8,128)S(1)}, f32[256,128]{1,0:T(8,128)S(1)}, u32[]{:S(2)}, u32[]{:S(2)}) collective-permute-start(f32[256,128]{1,0:T(8,128)S(1)} %get-tuple-element.52), channel_id=1, source_target_pairs={{0,6},{1,7},{2,4},{3,5},{4,2},{5,3},{6,0},{7,1},{8,14},{9,15},{10,... | collective-permute-start | bytes 393224 | tf_op jit(solution)/shard_map/ppermute | solution.py:297
  32.2 1.0 %collective-permute-start.13 = (f32[256,128]{1,0:T(8,128)S(1)}, f32[256,128]{1,0:T(8,128)S(1)}, u32[]{:S(2)}, u32[]{:S(2)}) collective-permute-start(f32[256,128]{1,0:T(8,128)S(1)} %get-tuple-element.54), channel_id=1, source_target_pairs={{0,2},{1,3},{2,0},{3,1},{4,6},{5,7},{6,4},{7,5},{8,10},{9,11},{10,... | collective-permute-start | bytes 393224 | tf_op jit(solution)/shard_map/ppermute | solution.py:297
  33.1 2.0 %collective-permute-start.14 = (f32[256,128]{1,0:T(8,128)S(1)}, f32[256,128]{1,0:T(8,128)S(1)}, u32[]{:S(2)}, u32[]{:S(2)}) collective-permute-start(f32[256,128]{1,0:T(8,128)S(1)} %get-tuple-element.55), channel_id=1, source_target_pairs={{0,4},{1,5},{2,6},{3,7},{4,0},{5,1},{6,2},{7,3},{8,12},{9,13},{10,... | collective-permute-start | bytes 393224 | tf_op jit(solution)/shard_map/ppermute | solution.py:297
  35.3 2.0 %collective-permute-start.15 = (f32[256,128]{1,0:T(8,128)S(1)}, f32[256,128]{1,0:T(8,128)S(1)}, u32[]{:S(2)}, u32[]{:S(2)}) collective-permute-start(f32[256,128]{1,0:T(8,128)S(1)} %get-tuple-element.56), channel_id=1, source_target_pairs={{0,6},{1,7},{2,4},{3,5},{4,2},{5,3},{6,0},{7,1},{8,14},{9,15},{10,... | collective-permute-start | bytes 393224 | tf_op jit(solution)/shard_map/ppermute | solution.py:297
  37.6 1.0 %collective-permute-done.13.refs_11_.refs_2_ = f32[256,128]{1,0:T(8,128)S(1)} collective-permute-done((f32[256,128]{1,0:T(8,128)S(1)}, f32[256,128]{1,0:T(8,128)S(1)}, u32[]{:S(2)}, u32[]{:S(2)}) %collective-permute-start.13) | collective-permute-done | bytes 131104 | tf_op jit(solution)/shard_map/ppermute | solution.py:297
  38.6 2.6 %collective-permute-done.15.refs_13_.refs_4_ = f32[256,128]{1,0:T(8,128)S(1)} collective-permute-done((f32[256,128]{1,0:T(8,128)S(1)}, f32[256,128]{1,0:T(8,128)S(1)}, u32[]{:S(2)}, u32[]{:S(2)}) %collective-permute-start.15) | collective-permute-done | bytes 131104 | tf_op jit(solution)/shard_map/ppermute | solution.py:297
  41.3 0.4 shard_map.69
  41.7 1.4 %collective-permute-done.17.sibling_ref = f32[1024,128]{1,0:T(8,128)S(1)} collective-permute-done((f32[1024,128]{1,0:T(8,128)S(1)}, f32[1024,128]{1,0:T(8,128)S(1)}, u32[]{:S(2)}, u32[]{:S(2)}) %collective-permute-start.17) | collective-permute-done | bytes 524320 | tf_op jit(solution)/shard_map/ppermute | solution.py:297
  43.2 1.2 %shard_map.71 = bf16[64,4096]{1,0:T(8,128)(2,1)} custom-call(f32[64,128]{1,0:T(8,128)S(1)} %get-tuple-element.32.refs_0_.use_ref, bf16[64,4096]{1,0:T(8,128)(2,1)S(1)} %bitcast.10, f32[1,4096]{1,0:T(1,128)S(1)} %bitcast.11, f32[64,4096]{1,0:T(8,128)S(1)} %get-tuple-element.57.mixed_ref, f32[64,128]{1,0:T(8,128)S(1)} %get-tuple-element.58.squares_ref, ...), custom_call_target="tpu_custom_call" | custom-call | tf_op jit(solution)/shard_map/pallas_call | solution.py:285
  (33 shorter events, 2.4 us)
Async XLA Ops:
  1.5 3.8 %collective-permute-start = (f32[1024,128]{1,0:T(8,128)S(1)}, f32[1024,128]{1,0:T(8,128)S(1)}, u32[]{:S(2)}, u32[]{:S(2)}) collective-permute-start(f32[1024,128]{1,0:T(8,128)S(1)} %get-tuple-element.39), channel_id=1, source_target_pairs={{0,1},{1,0},{2,3},{3,2},{4,5},{5,4},{6,7},{7,6},{8,9},{9,8},{10,11... | collective-permute-start | bytes 1572872 | tf_op jit(solution)/shard_map/ppermute | solution.py:297
  2.0 1.0 %copy-start = (bf16[1,64,4096]{2,1,0:T(8,128)(2,1)S(1)}, bf16[1,64,4096]{2,1,0:T(8,128)(2,1)}, u32[]{:S(2)}) copy-start(bf16[1,64,4096]{2,1,0:T(8,128)(2,1)} %param.5) | copy-start | bytes 1572868
  2.4 7.5 %collective-permute-start.4 = (f32[1024,128]{1,0:T(8,128)S(1)}, f32[1024,128]{1,0:T(8,128)S(1)}, u32[]{:S(2)}, u32[]{:S(2)}) collective-permute-start(f32[1024,128]{1,0:T(8,128)S(1)} %get-tuple-element.44), channel_id=1, source_target_pairs={{0,1},{1,0},{2,3},{3,2},{4,5},{5,4},{6,7},{7,6},{8,9},{9,8},{10,11... | collective-permute-start | bytes 1572872 | tf_op jit(solution)/shard_map/ppermute | solution.py:297
  5.4 7.4 %collective-permute-start.3 = (f32[256,128]{1,0:T(8,128)S(1)}, f32[256,128]{1,0:T(8,128)S(1)}, u32[]{:S(2)}, u32[]{:S(2)}) collective-permute-start(f32[256,128]{1,0:T(8,128)S(1)} %get-tuple-element.43), channel_id=1, source_target_pairs={{0,6},{1,7},{2,4},{3,5},{4,2},{5,3},{6,0},{7,1},{8,14},{9,15},{10,... | collective-permute-start | bytes 393224 | tf_op jit(solution)/shard_map/ppermute | solution.py:297
  9.0 7.4 %collective-permute-start.1 = (f32[256,128]{1,0:T(8,128)S(1)}, f32[256,128]{1,0:T(8,128)S(1)}, u32[]{:S(2)}, u32[]{:S(2)}) collective-permute-start(f32[256,128]{1,0:T(8,128)S(1)} %get-tuple-element.41), channel_id=1, source_target_pairs={{0,2},{1,3},{2,0},{3,1},{4,6},{5,7},{6,4},{7,5},{8,10},{9,11},{10,... | collective-permute-start | bytes 393224 | tf_op jit(solution)/shard_map/ppermute | solution.py:297
  9.5 6.9 %collective-permute-start.2 = (f32[256,128]{1,0:T(8,128)S(1)}, f32[256,128]{1,0:T(8,128)S(1)}, u32[]{:S(2)}, u32[]{:S(2)}) collective-permute-start(f32[256,128]{1,0:T(8,128)S(1)} %get-tuple-element.42), channel_id=1, source_target_pairs={{0,4},{1,5},{2,6},{3,7},{4,0},{5,1},{6,2},{7,3},{8,12},{9,13},{10,... | collective-permute-start | bytes 393224 | tf_op jit(solution)/shard_map/ppermute | solution.py:297
  12.8 7.0 %collective-permute-start.5 = (f32[256,128]{1,0:T(8,128)S(1)}, f32[256,128]{1,0:T(8,128)S(1)}, u32[]{:S(2)}, u32[]{:S(2)}) collective-permute-start(f32[256,128]{1,0:T(8,128)S(1)} %get-tuple-element.46), channel_id=1, source_target_pairs={{0,2},{1,3},{2,0},{3,1},{4,6},{5,7},{6,4},{7,5},{8,10},{9,11},{10,... | collective-permute-start | bytes 393224 | tf_op jit(solution)/shard_map/ppermute | solution.py:297
  14.7 5.4 %collective-permute-start.6 = (f32[256,128]{1,0:T(8,128)S(1)}, f32[256,128]{1,0:T(8,128)S(1)}, u32[]{:S(2)}, u32[]{:S(2)}) collective-permute-start(f32[256,128]{1,0:T(8,128)S(1)} %get-tuple-element.47), channel_id=1, source_target_pairs={{0,4},{1,5},{2,6},{3,7},{4,0},{5,1},{6,2},{7,3},{8,12},{9,13},{10,... | collective-permute-start | bytes 393224 | tf_op jit(solution)/shard_map/ppermute | solution.py:297
  16.3 5.9 %collective-permute-start.7 = (f32[256,128]{1,0:T(8,128)S(1)}, f32[256,128]{1,0:T(8,128)S(1)}, u32[]{:S(2)}, u32[]{:S(2)}) collective-permute-start(f32[256,128]{1,0:T(8,128)S(1)} %get-tuple-element.48), channel_id=1, source_target_pairs={{0,6},{1,7},{2,4},{3,5},{4,2},{5,3},{6,0},{7,1},{8,14},{9,15},{10,... | collective-permute-start | bytes 393224 | tf_op jit(solution)/shard_map/ppermute | solution.py:297
  16.4 11.9 %collective-permute-start.8 = (f32[256,128]{1,0:T(8,128)S(1)}, f32[256,128]{1,0:T(8,128)S(1)}, u32[]{:S(2)}, u32[]{:S(2)}) collective-permute-start(f32[256,128]{1,0:T(8,128)S(1)} %shard_map.59.refs_0_), channel_id=1, source_target_pairs={{0,8},{1,9},{2,10},{3,11},{4,12},{5,13},{6,14},{7,15},{8,0},{9,1},... | collective-permute-start | bytes 393224 | tf_op jit(solution)/shard_map/ppermute | solution.py:300
  22.2 9.8 %collective-permute-start.12 = (f32[256,128]{1,0:T(8,128)S(1)}, f32[256,128]{1,0:T(8,128)S(1)}, u32[]{:S(2)}, u32[]{:S(2)}) collective-permute-start(f32[256,128]{1,0:T(8,128)S(1)} %shard_map.63.refs_0_), channel_id=1, source_target_pairs={{0,8},{1,9},{2,10},{3,11},{4,12},{5,13},{6,14},{7,15},{8,0},{9,1},... | collective-permute-start | bytes 393224 | tf_op jit(solution)/shard_map/ppermute | solution.py:300
  28.5 6.8 %collective-permute-start.9 = (f32[256,128]{1,0:T(8,128)S(1)}, f32[256,128]{1,0:T(8,128)S(1)}, u32[]{:S(2)}, u32[]{:S(2)}) collective-permute-start(f32[256,128]{1,0:T(8,128)S(1)} %get-tuple-element.50), channel_id=1, source_target_pairs={{0,2},{1,3},{2,0},{3,1},{4,6},{5,7},{6,4},{7,5},{8,10},{9,11},{10,... | collective-permute-start | bytes 393224 | tf_op jit(solution)/shard_map/ppermute | solution.py:297
  29.0 8.2 %collective-permute-start.10 = (f32[256,128]{1,0:T(8,128)S(1)}, f32[256,128]{1,0:T(8,128)S(1)}, u32[]{:S(2)}, u32[]{:S(2)}) collective-permute-start(f32[256,128]{1,0:T(8,128)S(1)} %get-tuple-element.51), channel_id=1, source_target_pairs={{0,4},{1,5},{2,6},{3,7},{4,0},{5,1},{6,2},{7,3},{8,12},{9,13},{10,... | collective-permute-start | bytes 393224 | tf_op jit(solution)/shard_map/ppermute | solution.py:297
  31.4 6.0 %collective-permute-start.11 = (f32[256,128]{1,0:T(8,128)S(1)}, f32[256,128]{1,0:T(8,128)S(1)}, u32[]{:S(2)}, u32[]{:S(2)}) collective-permute-start(f32[256,128]{1,0:T(8,128)S(1)} %get-tuple-element.52), channel_id=1, source_target_pairs={{0,6},{1,7},{2,4},{3,5},{4,2},{5,3},{6,0},{7,1},{8,14},{9,15},{10,... | collective-permute-start | bytes 393224 | tf_op jit(solution)/shard_map/ppermute | solution.py:297
  32.2 6.4 %collective-permute-start.13 = (f32[256,128]{1,0:T(8,128)S(1)}, f32[256,128]{1,0:T(8,128)S(1)}, u32[]{:S(2)}, u32[]{:S(2)}) collective-permute-start(f32[256,128]{1,0:T(8,128)S(1)} %get-tuple-element.54), channel_id=1, source_target_pairs={{0,2},{1,3},{2,0},{3,1},{4,6},{5,7},{6,4},{7,5},{8,10},{9,11},{10,... | collective-permute-start | bytes 393224 | tf_op jit(solution)/shard_map/ppermute | solution.py:297
  33.1 5.5 %collective-permute-start.14 = (f32[256,128]{1,0:T(8,128)S(1)}, f32[256,128]{1,0:T(8,128)S(1)}, u32[]{:S(2)}, u32[]{:S(2)}) collective-permute-start(f32[256,128]{1,0:T(8,128)S(1)} %get-tuple-element.55), channel_id=1, source_target_pairs={{0,4},{1,5},{2,6},{3,7},{4,0},{5,1},{6,2},{7,3},{8,12},{9,13},{10,... | collective-permute-start | bytes 393224 | tf_op jit(solution)/shard_map/ppermute | solution.py:297
  35.3 5.9 %collective-permute-start.15 = (f32[256,128]{1,0:T(8,128)S(1)}, f32[256,128]{1,0:T(8,128)S(1)}, u32[]{:S(2)}, u32[]{:S(2)}) collective-permute-start(f32[256,128]{1,0:T(8,128)S(1)} %get-tuple-element.56), channel_id=1, source_target_pairs={{0,6},{1,7},{2,4},{3,5},{4,2},{5,3},{6,0},{7,1},{8,14},{9,15},{10,... | collective-permute-start | bytes 393224 | tf_op jit(solution)/shard_map/ppermute | solution.py:297
  37.5 3.8 %collective-permute-start.16 = (f32[1024,128]{1,0:T(8,128)S(1)}, f32[1024,128]{1,0:T(8,128)S(1)}, u32[]{:S(2)}, u32[]{:S(2)}) collective-permute-start(f32[1024,128]{1,0:T(8,128)S(1)} %shard_map.68), channel_id=1, source_target_pairs={{0,1},{1,0},{2,3},{3,2},{4,5},{5,4},{6,7},{7,6},{8,9},{9,8},{10,11... | collective-permute-start | bytes 1572872 | tf_op jit(solution)/shard_map/ppermute | solution.py:297
  41.2 2.0 %collective-permute-start.17 = (f32[1024,128]{1,0:T(8,128)S(1)}, f32[1024,128]{1,0:T(8,128)S(1)}, u32[]{:S(2)}, u32[]{:S(2)}) collective-permute-start(f32[1024,128]{1,0:T(8,128)S(1)} %shard_map.70), channel_id=1, source_target_pairs={{0,1},{1,0},{2,3},{3,2},{4,5},{5,4},{6,7},{7,6},{8,9},{9,8},{10,11... | collective-permute-start | bytes 1572872 | tf_op jit(solution)/shard_map/ppermute | solution.py:297
  41.3 1.9 %copy-start.1 = (f32[4096]{0:T(1024)S(1)}, f32[4096]{0:T(1024)}, u32[]{:S(2)}) copy-start(f32[4096]{0:T(1024)} %param.9) | copy-start | bytes 49156

commit v4 on v3

v4 whole, which is shorter than its diff:
```python
import functools

import jax
import jax.numpy as jnp
from jax import lax
from jax.experimental import pallas as pl
from jax.experimental.pallas import tpu as pltpu
from jax.sharding import PartitionSpec as P

HD = 128
CHIPS = 4
QUARTERS = (0, 3, 2, 1)
FRONT = (((0, 1, 2, 3),), ((0, 1, 2, 3),))
BACK = (((0, 1, 2, 3),), ((0, 1, 2, 3),))
SPLIT = (1, 1)
SLOTS = {"start": [(0, (0, 16))], "between1": [(0, (16, 32))], "enter1": [(1, (0, 32))]}
F32 = jnp.float32
BF16 = jnp.bfloat16
HB = pl.BlockSpec(memory_space=pltpu.HBM)
SM = pl.BlockSpec(memory_space=pltpu.SMEM)
VM = pl.BlockSpec(memory_space=pltpu.VMEM)
PARAMS = pltpu.CompilerParams(vmem_limit_bytes=32 * 1024 * 1024)


def place():
    block = lax.axis_index("ctx")
    return block % 2, (block // 2) % CHIPS, block // (2 * CHIPS), block


def segment_at(starts, position):
    count = jnp.int32(0)
    for i in range(starts.shape[1]):
        count = count + (starts[0, i] <= position).astype(jnp.int32)
    return count


def same(starts, rows, late, early):
    one = segment_at(starts, (late + 1) * rows - 1)
    two = segment_at(starts, (early + 1) * rows - 1)
    return (one == two).astype(F32)


def segment_rows(starts, positions):
    count = jnp.zeros(positions.shape, jnp.int32)
    for i in range(starts.shape[1]):
        count = count + (starts[0, i] <= positions).astype(jnp.int32)
    return count


def tile(index):
    return slice(index * HD, (index + 1) * HD)


def sizes(width):
    quarter = width // HD // 2 // CHIPS
    return [quarter * share // sum(SPLIT) for share in SPLIT]


def part_steps(width, part, spots=range(CHIPS)):
    return [(part, QUARTERS[spot], j) for spot in spots for j in range(sizes(width)[part])]


def steps(width):
    return [
        (own, *step) for own in (True, False) for part in range(len(SPLIT)) for spots in BACK[part]
        for step in part_steps(width, part, spots)]


def found_in(groups, spot):
    return next((i, group.index(spot)) for i, group in enumerate(groups) if spot in group)


def column(width, core, chip, own, part, k, j):
    parts = sizes(width)
    quarter = sum(parts)
    half = core if own else 1 - core
    head = (half * CHIPS + lax.bitwise_xor(chip, k)) * quarter + sum(parts[:part]) + j
    return pl.ds(pl.multiple_of(head * HD, HD), HD)


def table_rows(groups):
    names = ["chip_mine", "chip_other", "pair_scale", "pair_add", "mix_scale", "mix_add"]
    names += [("total", k) for k in range(CHIPS)]
    names += [("carry", k, j) for k in range(CHIPS) for j in range(CHIPS)]
    names += [("enter", k) for k in range(CHIPS)]
    names += [("before", s) for s in range(groups - 1)]
    return {name: i for i, name in enumerate(names)}


def weights(starts, rows, groups):
    core, chip, group, block = place()
    same_ = functools.partial(same, starts, rows)
    mine, first = block // 2 * 2, group * 2 * CHIPS
    joined = same_(mine + 1, mine)
    after, mix = same_(block, block - 1), same_(block - 1, block - 2)
    found = {
        "chip_mine": jnp.where(core == 0, joined, 1.0),
        "chip_other": jnp.where(core == 0, 1.0, joined),
        "pair_scale": jnp.where(core == 0, after, 1.0),
        "pair_add": jnp.where(core == 0, 1.0, 0.0),
        "mix_scale": jnp.where(core == 0, 1.0, mix),
        "mix_add": jnp.where(core == 0, 0.0, 1.0),
    }
    for k in range(CHIPS):
        target = lax.bitwise_xor(chip, k)
        end = first + 2 * target - 1
        found["total", k] = same_(first + 7, first + 2 * target + 1)
        found["enter", k] = same_(end, first - 1)
        for j in range(CHIPS):
            source = lax.bitwise_xor(chip, j)
            found["carry", k, j] = jnp.where(source < target, same_(end, first + 2 * source + 1), 0.0)
    for s in range(groups - 1):
        end = first - 1 - s * 2 * CHIPS
        found["before", s] = jnp.where(end >= 0, same_(first - 1, end), 0.0)
    return found


def summarize(kept_ref, key_ref, value_ref, own, part, spots, out):
    core, chip, _, _ = place()
    width = key_ref.shape[1]
    kept = kept_ref[...]
    for i, step in enumerate(part_steps(width, part, spots)):
        at = column(width, core, chip, own, *step)
        out[tile(i), :] = lax.dot_general(
            key_ref[:, at] * kept, value_ref[:, at], (((0,), (0,)), ((), ())), preferred_element_type=F32)


def first_kernel(groups, starts_hbm, key_hbm, value_hbm, key_ref, value_ref, table_ref, kept_ref, allowed_ref, use_ref, *refs):
    *sends, starts, sems = refs
    copies = [
        pltpu.make_async_copy(source, target, sems.at[i])
        for i, (source, target) in enumerate(((starts_hbm, starts), (key_hbm, key_ref), (value_hbm, value_ref)))
    ]
    for copy in copies:
        copy.start()
    copies[0].wait()
    rows = key_ref.shape[0]
    begin = place()[3] * rows
    names = table_rows(groups)
    for name, weight in weights(starts, rows, groups).items():
        table_ref[names[name]:names[name] + 1, :] = jnp.full((1, HD), weight, F32)
    segments = segment_rows(starts, begin + lax.broadcasted_iota(jnp.int32, (rows, HD), 0))
    kept_ref[...] = (segments == segment_at(starts, begin + rows - 1)).astype(F32).astype(BF16)
    use_ref[...] = (segments == segment_at(starts, begin - 1)).astype(F32)
    late = begin + lax.broadcasted_iota(jnp.int32, (rows, rows), 0)
    early = begin + lax.broadcasted_iota(jnp.int32, (rows, rows), 1)
    allowed = (late >= early) & (segment_rows(starts, late) == segment_rows(starts, early))
    allowed_ref[...] = allowed.astype(F32)
    for copy in copies[1:]:
        copy.wait()
    for spots, send_ref in zip(FRONT[0], sends):
        summarize(kept_ref, key_ref, value_ref, False, 0, spots, send_ref)


def summary_kernel(what, kept_ref, key_ref, value_ref, *refs):
    for (own, part, spots), out in zip(what, refs[-len(what):]):
        summarize(kept_ref, key_ref, value_ref, own, part, spots, out)


def row(table_ref, groups, *name):
    at = table_rows(groups)[name if len(name) > 1 else name[0]]
    return table_ref[at:at + 1, :]


def chip_kernel(count, weight, keep_ref, got_ref, *refs):
    size = refs[-1].shape[0]
    for i, out in enumerate(refs[-count:]):
        at = slice(i * size, (i + 1) * size)
        out[...] = weight("chip_mine") * keep_ref[at, :] + weight("chip_other") * got_ref[at, :]


def total_kernel(weight, *refs):
    total = None
    for k, piece in zip(QUARTERS, refs[:CHIPS]):
        term = weight("total", k) * piece[...]
        total = term if total is None else total + term
    refs[-1][...] = total


def straight_kernel(shifts, weight, *refs):
    pieces, outs = refs[:CHIPS], refs[-CHIPS:]
    before = entered(weight, refs[CHIPS:CHIPS + shifts])
    for k, out in zip(QUARTERS, outs):
        state = weight("enter", k) * before
        for j, piece in zip(QUARTERS, pieces):
            if j != k:
                state = state + weight("carry", k, j) * piece[...]
        out[...] = state


def entered(weight, totals):
    before = None
    for s, total in enumerate(totals):
        term = weight("before", s) * total[...]
        before = term if before is None else before + term
    return before


def pair_kernel(part, spots, weight, *refs):
    keeps, pieces, out = refs[:len(FRONT[part])], refs[len(FRONT[part]):][:len(spots)], refs[-1]
    size = pieces[0].shape[0]
    for i, (spot, piece) in enumerate(zip(spots, pieces)):
        which, place_in = found_in(FRONT[part], spot)
        keep = keeps[which][place_in * size:(place_in + 1) * size, :]
        out[i * size:(i + 1) * size, :] = weight("pair_scale") * piece[...] + weight("pair_add") * keep


def intra_kernel(on, span, allowed_ref, query_ref, key_ref, value_ref, *refs):
    out_ref = refs[-1]
    core, chip, _, _ = place()
    width = query_ref.shape[1]

    def body():
        allowed = allowed_ref[...]
        for i, step in enumerate(steps(width)[slice(*span)]):
            at = column(width, core, chip, *step)
            scores = lax.dot_general(
                query_ref[:, at], key_ref[:, at], (((1,), (1,)), ((), ())), preferred_element_type=F32)
            out_ref[:, tile(i)] = jnp.dot(
                (scores * allowed).astype(BF16), value_ref[:, at], preferred_element_type=F32)

    if on is None:
        body()
    else:
        pl.when(core == on)(body)


def from_past(use, query_ref, step, state):
    core, chip, _, _ = place()
    at = column(query_ref.shape[1], core, chip, *step)
    return use * jnp.dot(query_ref[:, at], state.astype(BF16), preferred_element_type=F32)


def mix_kernel(sources, count, weight, use_ref, query_ref, gain_ref, *refs):
    parts = len(SPLIT)
    intras, refs = refs[:count], refs[count:]
    states = [refs[part * CHIPS:(part + 1) * CHIPS] for part in range(parts)]
    refs = refs[parts * CHIPS:]
    gots, siblings = [], []
    for part in range(parts):
        gots.append(refs[:len(FRONT[part])])
        refs = refs[len(FRONT[part]):]
    for part in range(parts):
        siblings.append(refs[:len(BACK[part])])
        refs = refs[len(siblings[part]):] if part < parts - 1 else refs
    mixed_ref, squares_ref = refs[-2:]
    core, chip, _, _ = place()
    rows, width = query_ref.shape
    use = use_ref[...]
    squares = jnp.zeros((rows, HD), F32)
    order = steps(width)
    first = len(order) - len(part_steps(width, parts - 1, BACK[-1][-1]))
    for i, step in enumerate(order):
        found = [intras[which][:, tile(at)] for which, at in sources[i]]
        both = found[0] if sources[i][0] == sources[i][1] else jnp.where(core == 0, *found)
        own, part, k, j = step
        size = sizes(width)[part]
        spot = QUARTERS.index(k)
        if own:
            which, at = found_in(FRONT[part], spot)
            state = weight("mix_scale") * states[part][spot][tile(j), :]
            state = state + weight("mix_add") * gots[part][which][tile(at * size + j), :]
        elif i < first:
            which, at = found_in(BACK[part], spot)
            state = siblings[part][which][tile(at * size + j), :]
        else:
            mixed_ref[:, tile(i)] = both
            continue
        both = both + from_past(use, query_ref, step, state)
        squares = squares + both * both
        mixed_ref[:, tile(i)] = both * gain_ref[:, column(width, core, chip, *step)]
    squares_ref[...] = squares


def norm_kernel(use_ref, query_ref, gain_ref, mixed_ref, squares_ref, sibling_ref, out_hbm, out_ref, sems):
    core, chip, _, _ = place()
    rows, width = query_ref.shape
    order = steps(width)
    first = len(order) - sibling_ref.shape[0] // HD
    use = use_ref[...]
    squares = squares_ref[...]
    late = []
    for i, step in enumerate(order[first:]):
        both = mixed_ref[:, tile(first + i)] + from_past(use, query_ref, step, sibling_ref[tile(i), :])
        squares = squares + both * both
        late.append(both * gain_ref[:, column(width, core, chip, *step)])
    mean = jnp.sum(squares, axis=-1, keepdims=True) * (1.0 / width)
    norm = jnp.broadcast_to(lax.rsqrt(mean + 1e-05), (rows, HD))
    for i, step in enumerate(order):
        both = mixed_ref[:, tile(i)] if i < first else late[i - first]
        out_ref[:, column(width, core, chip, *step)] = (both * norm).astype(BF16)
    copies = []
    for i in range(sems.shape[0]):
        at = slice(i * rows // sems.shape[0], (i + 1) * rows // sems.shape[0])
        copies.append(pltpu.make_async_copy(out_ref.at[at, :], out_hbm.at[at, :], sems.at[i]))
        copies[-1].start()
    for copy in copies:
        copy.wait()


def in_hbm(array):
    return pltpu.with_memory_space_constraint(array, pltpu.HBM)


def array(shape, dtype=F32):
    return jax.ShapeDtypeStruct(shape, dtype)


def shards(count, query_rows, key_rows, value_rows, seg_starts, norm_gain):
    query, key, value = query_rows[0], key_rows[0], value_rows[0]
    rows, width = query.shape
    groups = count // (2 * CHIPS)
    parts = range(len(SPLIT))
    heads = len(steps(width))
    lanes = [array((size * HD, HD)) for size in sizes(width)]

    def tall(part, spots):
        return array((len(part_steps(width, part, spots)) * HD, HD))

    def call(kernel, outs, *args, scratch=()):
        return pl.pallas_call(
            kernel, out_shape=outs, in_specs=[VM] * len(args), out_specs=jax.tree.map(lambda _: VM, outs),
            scratch_shapes=scratch, compiler_params=PARAMS,
        )(*args)

    def weighted(kernel, outs, *args):
        def body(table_ref, *refs):
            return kernel(functools.partial(row, table_ref, groups), *refs)

        return call(body, outs, table, *args)

    def swap(what, bits):
        return lax.ppermute(what, "ctx", [(i, i ^ bits) for i in range(count)])

    def later(what, shift):
        return lax.ppermute(what, "ctx", [(i, (i + shift * 2 * CHIPS) % count) for i in range(count)])

    def intra(on, span, *after):
        out = array((rows, (span[1] - span[0]) * HD))
        return call(functools.partial(intra_kernel, on, span), out, allowed, query, key, value, *after)

    def summary(what, *after):
        outs = [tall(*step[1:]) for step in what]
        return call(functools.partial(summary_kernel, what), outs, kept, key, value, *after)

    key, value, table, kept, allowed, use, *sends = pl.pallas_call(
        functools.partial(first_kernel, groups),
        out_shape=[array((rows, width), BF16)] * 2 + [
            array((-(-len(table_rows(groups)) // 8) * 8, HD)), array((rows, HD), BF16), array((rows, rows)),
            array((rows, HD))] + [tall(0, spots) for spots in FRONT[0]],
        in_specs=[HB] * 3, out_specs=[VM] * (6 + len(FRONT[0])),
        scratch_shapes=[pltpu.SMEM(seg_starts.shape, jnp.int32), pltpu.SemaphoreType.DMA((3,))],
        compiler_params=PARAMS,
    )(in_hbm(seg_starts), in_hbm(key), in_hbm(value))
    gots, keeps = [], []
    for part in parts:
        gots.append([swap(send, 1) for send in sends])
        keep = [(True, part, spots) for spots in FRONT[part]]
        send = [(False, part + 1, spots) for spots in FRONT[part + 1]] if part + 1 < len(SPLIT) else []
        outs = summary(keep + send)
        keeps.append(outs[:len(keep)])
        sends = outs[len(keep):]
    done = [[None] * heads, [None] * heads]
    intras = []

    def inside(slot, *after):
        new = []
        for on, span in SLOTS.get(slot, ()):
            span = tuple(heads * at // 32 for at in span)
            for core in range(2) if on is None else (on,):
                done[core][slice(*span)] = [(len(intras), i) for i in range(span[1] - span[0])]
            intras.append(intra(on, span, *after))
            new.append(intras[-1])
        return new

    chips, totals, states, siblings = [{} for _ in range(4)]

    def begin(part, *after):
        own = {}
        for spots, keep, got in zip(FRONT[part], keeps[part], gots[part]):
            outs = weighted(
                functools.partial(chip_kernel, len(spots)), [lanes[part]] * len(spots), keep, got, *after)
            own.update(zip(spots, outs))
        chips[part] = {spot: swap(own[spot], 2 * QUARTERS[spot]) if QUARTERS[spot] else own[spot] for spot in own}
        return chips[part]

    def between(part, *after):
        total = weighted(total_kernel, lanes[part], *[chips[part][spot] for spot in range(CHIPS)], *after)
        totals[part] = [later(total, shift) for shift in range(1, groups)]
        return [total]

    def enter(part, *after):
        outs = weighted(
            functools.partial(straight_kernel, groups - 1), [lanes[part]] * CHIPS,
            *[chips[part][spot] for spot in range(CHIPS)], *totals[part], *after)
        states[part] = [swap(out, 2 * k) if k else out for out, k in zip(outs, QUARTERS)]
        return [outs[0]]

    def share(part, *after):
        siblings[part] = []
        for spots in BACK[part]:
            siblings[part].append(swap(weighted(
                functools.partial(pair_kernel, part, spots), tall(part, spots), *keeps[part],
                *[states[part][spot] for spot in spots], *after), 1))
        return siblings[part][:1]

    a = begin(0, *inside("start", keeps[0][0]))
    b = begin(1, a[1])
    a = between(0, *inside("begin", b[0]))
    b = between(1, *inside("between", a[0]))
    a = enter(0, *inside("between1", b[0]))
    b = enter(1, *inside("enter", a[0]))
    a = share(0, *inside("enter1", b[0]))
    b = share(1, *inside("share", a[0]))
    siblings, states = [siblings[part] for part in parts], [states[part] for part in parts]
    gain = norm_gain[None, :]
    mixed, squares = weighted(
        functools.partial(mix_kernel, list(zip(*done)), len(intras)), [array((rows, width)), array((rows, HD))], use, query, gain,
        *intras, *[piece for state in states for piece in state], *[got for group in gots for got in group],
        *[sibling for group in siblings for sibling in group][:-1])
    attended = pl.pallas_call(
        norm_kernel, out_shape=array((rows, width), BF16), in_specs=[VM] * 6, out_specs=HB,
        scratch_shapes=[pltpu.VMEM((rows, width), BF16), pltpu.SemaphoreType.DMA((2,))], compiler_params=PARAMS,
    )(use, query, gain, mixed, squares, siblings[-1][-1])
    return attended[None]


def solution(mesh):
    placed = (
        P("sess", "ctx", None),
        P("sess", "ctx", None),
        P("sess", "ctx", None),
        P("sess", None),
        P(),
    )
    return jax.shard_map(
        functools.partial(shards, mesh.shape["ctx"]), mesh=mesh, in_specs=placed,
        out_specs=P("sess", "ctx", None), check_vma=False
    )
```

time: 44.6 us -> 42.6 us (0.955)
  starting transfers between devices: 24.3 us -> 20.6 us
  waiting for transfers between devices: 10.6 us -> 12.2 us
    ppermute x16, starting transfers between devices: 17.1 us -> 14.6 us  [swap(): return lax.ppermute(what, 'ctx', [(i, i ^ bits) for i in range(count)])]
    ppermute x16, waiting for transfers between devices: 10.6 us -> 12.2 us  [swap(): return lax.ppermute(what, 'ctx', [(i, i ^ bits) for i in range(count)])]
    pallas_call x16 -> x14, Pallas kernels: 7.39 us -> 6.16 us  [call(): pl.pallas_call(kernel, out_shape=outs, in_specs=[VM] * len(args), out_spe...]
    ppermute x2, starting transfers between devices: 7.2 us -> 5.98 us  [later(): lax.ppermute(what, 'ctx', [(i, (i + shift * 2 * CHIPS) % count) for i in...]
    pallas_call x1 -> x2, Pallas kernels: 1.5 us -> 2.69 us  [the longest x1 1.5 us: shards(): pl.pallas_call(functools.partial(first_kernel, groups), out_shape=[array(...]
  transfers between devices with their start and end apart: 18 -> 18, of which waited for: 8 -> 9; matrix products, arithmetic and copies ran while one was open for 0% -> 0% of each run, Pallas kernels for 14% -> 15%
where the time goes in v4:
time: 42.6 us; the launch traced here: 42.4 us
  starting transfers between devices  20.6 us (48%)
  waiting for transfers between devices  12.2 us (29%)
  Pallas kernels  8.85 us (21%)
  local copies, waits for them, and re-layouts  0.57 us (1%)
    ppermute x16, starting transfers between devices, swap(): return lax.ppermute(what, 'ctx', [(i, i ^ bits) for i in range(count)])  14.6 us
    ppermute x16, waiting for transfers between devices, swap(): return lax.ppermute(what, 'ctx', [(i, i ^ bits) for i in range(count)])  12.2 us
    pallas_call x14, Pallas kernels, call(): pl.pallas_call(kernel, out_shape=outs, in_specs=[VM] * len(args), out_spe...  6.16 us
    ppermute x2, starting transfers between devices, later(): lax.ppermute(what, 'ctx', [(i, (i + shift * 2 * CHIPS) % count) for i in...  5.98 us
    pallas_call x1, Pallas kernels, shards(): pl.pallas_call(functools.partial(first_kernel, groups), out_shape=[array(...  1.5 us
    pallas_call x1, Pallas kernels, shards(): pl.pallas_call(norm_kernel, out_shape=array((rows, width), BF16), in_spec...  1.19 us
  transfers between devices with their start and end apart: 18, of which 9 were waited for; matrix products, arithmetic and copies ran while one was open for 0% of the time, Pallas kernels for 15%

profile of v4, /device:TPU:0, one launch (start us, length us, event | category | flops | bytes accessed | tf_op | source)
XLA Modules:
  0.0 42.4 jit_solution(15228478407216828888)
XLA Ops:
  0.0 1.5 %shard_map.55 = (bf16[64,4096]{1,0:T(8,128)(2,1)S(1)}, bf16[64,4096]{1,0:T(8,128)(2,1)S(1)}, f32[32,128]{1,0:T(8,128)S(1)}, bf16[64,128]{1,0:T(8,128)(2,1)S(1)},...) custom-call(s32[1,4]{1,0:T(1,128)} %starts_hbm.1, bf16[64,4096]{1,0:T(8,128)(2,1)} %bitcast.12, ...), custom_call_target="tpu_custom_call" | custom-call | tf_op jit(solution)/shard_map/pallas_call | solution.py:346
  1.5 0.5 %collective-permute-start.1 = (f32[1024,128]{1,0:T(8,128)S(1)}, f32[1024,128]{1,0:T(8,128)S(1)}, u32[]{:S(2)}, u32[]{:S(2)}) collective-permute-start(f32[1024,128]{1,0:T(8,128)S(1)} %get-tuple-element.40), channel_id=1, source_target_pairs={{0,1},{1,0},{2,3},{3,2},{4,5},{5,4},{6,7},{7,6},{8,9},{9,8},{10,11... | collective-permute-start | bytes 1572872 | tf_op jit(solution)/shard_map/ppermute | solution.py:333
  2.5 0.6 %copy-done = bf16[1,64,4096]{2,1,0:T(8,128)(2,1)S(1)} copy-done((bf16[1,64,4096]{2,1,0:T(8,128)(2,1)S(1)}, bf16[1,64,4096]{2,1,0:T(8,128)(2,1)}, u32[]{:S(2)}) %copy-start) | copy-done | bytes 524312
  3.1 2.3 %shard_map.57.refs_2_.refs_3_ = f32[64,2048]{1,0:T(8,128)S(1)} custom-call(f32[64,64]{1,0:T(8,128)S(1)} %get-tuple-element.34.allowed_ref, bf16[64,4096]{1,0:T(8,128)(2,1)S(1)} %bitcast.5, bf16[64,4096]{1,0:T(8,128)(2,1)S(1)} %get-tuple-element.35.key_ref, bf16[64,4096]{1,0:T(8,128)(2,1)S(1)} %get-tuple-element.36.value_ref, ...), custom_call_target="tpu_custom_call" | custom-call | tf_op jit(solution)/shard_map/pallas_call | solution.py:321
  5.4 3.6 %collective-permute-start.2 = (f32[256,128]{1,0:T(8,128)S(1)}, f32[256,128]{1,0:T(8,128)S(1)}, u32[]{:S(2)}, u32[]{:S(2)}) collective-permute-start(f32[256,128]{1,0:T(8,128)S(1)} %get-tuple-element.41), channel_id=1, source_target_pairs={{0,6},{1,7},{2,4},{3,5},{4,2},{5,3},{6,0},{7,1},{8,14},{9,15},{10,... | collective-permute-start | bytes 393224 | tf_op jit(solution)/shard_map/ppermute | solution.py:333
  9.9 3.0 %collective-permute-done.2.refs_2_.refs_1_ = f32[256,128]{1,0:T(8,128)S(1)} collective-permute-done((f32[256,128]{1,0:T(8,128)S(1)}, f32[256,128]{1,0:T(8,128)S(1)}, u32[]{:S(2)}, u32[]{:S(2)}) %collective-permute-start.2) | collective-permute-done | bytes 131104 | tf_op jit(solution)/shard_map/ppermute | solution.py:333
  13.0 2.7 %collective-permute-start.3 = (f32[256,128]{1,0:T(8,128)S(1)}, f32[256,128]{1,0:T(8,128)S(1)}, u32[]{:S(2)}, u32[]{:S(2)}) collective-permute-start(f32[256,128]{1,0:T(8,128)S(1)} %get-tuple-element.43), channel_id=1, source_target_pairs={{0,6},{1,7},{2,4},{3,5},{4,2},{5,3},{6,0},{7,1},{8,14},{9,15},{10,... | collective-permute-start | bytes 393224 | tf_op jit(solution)/shard_map/ppermute | solution.py:333
  15.7 0.5 %collective-permute-start.4 = (f32[256,128]{1,0:T(8,128)S(1)}, f32[256,128]{1,0:T(8,128)S(1)}, u32[]{:S(2)}, u32[]{:S(2)}) collective-permute-start(f32[256,128]{1,0:T(8,128)S(1)} %get-tuple-element.44), channel_id=1, source_target_pairs={{0,4},{1,5},{2,6},{3,7},{4,0},{5,1},{6,2},{7,3},{8,12},{9,13},{10,... | collective-permute-start | bytes 393224 | tf_op jit(solution)/shard_map/ppermute | solution.py:333
  16.6 2.8 %collective-permute-start.9 = (f32[256,128]{1,0:T(8,128)S(1)}, f32[256,128]{1,0:T(8,128)S(1)}, u32[]{:S(2)}, u32[]{:S(2)}) collective-permute-start(f32[256,128]{1,0:T(8,128)S(1)} %shard_map.65), channel_id=1, source_target_pairs={{0,8},{1,9},{2,10},{3,11},{4,12},{5,13},{6,14},{7,15},{8,0},{9,1},... | collective-permute-start | bytes 393224 | tf_op jit(solution)/shard_map/ppermute | solution.py:336
  19.3 0.9 %collective-permute-done.3.refs_1_ = f32[256,128]{1,0:T(8,128)S(1)} collective-permute-done((f32[256,128]{1,0:T(8,128)S(1)}, f32[256,128]{1,0:T(8,128)S(1)}, u32[]{:S(2)}, u32[]{:S(2)}) %collective-permute-start.3) | collective-permute-done | bytes 131104 | tf_op jit(solution)/shard_map/ppermute | solution.py:333
  20.2 2.0 %collective-permute-done.4.refs_2_ = f32[256,128]{1,0:T(8,128)S(1)} collective-permute-done((f32[256,128]{1,0:T(8,128)S(1)}, f32[256,128]{1,0:T(8,128)S(1)}, u32[]{:S(2)}, u32[]{:S(2)}) %collective-permute-start.4) | collective-permute-done | bytes 131104 | tf_op jit(solution)/shard_map/ppermute | solution.py:333
  22.3 3.2 %collective-permute-start.6 = (f32[256,128]{1,0:T(8,128)S(1)}, f32[256,128]{1,0:T(8,128)S(1)}, u32[]{:S(2)}, u32[]{:S(2)}) collective-permute-start(f32[256,128]{1,0:T(8,128)S(1)} %shard_map.61.refs_0_), channel_id=1, source_target_pairs={{0,8},{1,9},{2,10},{3,11},{4,12},{5,13},{6,14},{7,15},{8,0},{9,1},... | collective-permute-start | bytes 393224 | tf_op jit(solution)/shard_map/ppermute | solution.py:336
  25.5 2.3 %shard_map.62.refs_5_.refs_4_ = f32[64,2048]{1,0:T(8,128)S(1)} custom-call(f32[64,64]{1,0:T(8,128)S(1)} %get-tuple-element.34.allowed_ref, bf16[64,4096]{1,0:T(8,128)(2,1)S(1)} %bitcast.6, bf16[64,4096]{1,0:T(8,128)(2,1)S(1)} %get-tuple-element.35.key_ref, bf16[64,4096]{1,0:T(8,128)(2,1)S(1)} %get-tuple-element.36.value_ref, f32[256,128]{1,0:T(8,128)S(1)} %shard_map.61.refs_0_), custom_call_target="tpu_custom_call" | custom-call | tf_op jit(solution)/shard_map/pallas_call | solution.py:321
  27.9 0.7 %collective-permute-start.10 = (f32[256,128]{1,0:T(8,128)S(1)}, f32[256,128]{1,0:T(8,128)S(1)}, u32[]{:S(2)}, u32[]{:S(2)}) collective-permute-start(f32[256,128]{1,0:T(8,128)S(1)} %get-tuple-element.51), channel_id=1, source_target_pairs={{0,6},{1,7},{2,4},{3,5},{4,2},{5,3},{6,0},{7,1},{8,14},{9,15},{10,... | collective-permute-start | bytes 393224 | tf_op jit(solution)/shard_map/ppermute | solution.py:333
  28.6 0.8 %collective-permute-start.11 = (f32[256,128]{1,0:T(8,128)S(1)}, f32[256,128]{1,0:T(8,128)S(1)}, u32[]{:S(2)}, u32[]{:S(2)}) collective-permute-start(f32[256,128]{1,0:T(8,128)S(1)} %get-tuple-element.52), channel_id=1, source_target_pairs={{0,4},{1,5},{2,6},{3,7},{4,0},{5,1},{6,2},{7,3},{8,12},{9,13},{10,... | collective-permute-start | bytes 393224 | tf_op jit(solution)/shard_map/ppermute | solution.py:333
  29.5 2.0 %collective-permute-start.12 = (f32[256,128]{1,0:T(8,128)S(1)}, f32[256,128]{1,0:T(8,128)S(1)}, u32[]{:S(2)}, u32[]{:S(2)}) collective-permute-start(f32[256,128]{1,0:T(8,128)S(1)} %get-tuple-element.53), channel_id=1, source_target_pairs={{0,2},{1,3},{2,0},{3,1},{4,6},{5,7},{6,4},{7,5},{8,10},{9,11},{10,... | collective-permute-start | bytes 393224 | tf_op jit(solution)/shard_map/ppermute | solution.py:333
  31.6 0.7 %collective-permute-start.13 = (f32[256,128]{1,0:T(8,128)S(1)}, f32[256,128]{1,0:T(8,128)S(1)}, u32[]{:S(2)}, u32[]{:S(2)}) collective-permute-start(f32[256,128]{1,0:T(8,128)S(1)} %get-tuple-element.54), channel_id=1, source_target_pairs={{0,6},{1,7},{2,4},{3,5},{4,2},{5,3},{6,0},{7,1},{8,14},{9,15},{10,... | collective-permute-start | bytes 393224 | tf_op jit(solution)/shard_map/ppermute | solution.py:333
  32.3 0.8 %collective-permute-start.14 = (f32[256,128]{1,0:T(8,128)S(1)}, f32[256,128]{1,0:T(8,128)S(1)}, u32[]{:S(2)}, u32[]{:S(2)}) collective-permute-start(f32[256,128]{1,0:T(8,128)S(1)} %get-tuple-element.55), channel_id=1, source_target_pairs={{0,4},{1,5},{2,6},{3,7},{4,0},{5,1},{6,2},{7,3},{8,12},{9,13},{10,... | collective-permute-start | bytes 393224 | tf_op jit(solution)/shard_map/ppermute | solution.py:333
  33.1 1.1 %collective-permute-done.10.refs_2_.refs_7_ = f32[256,128]{1,0:T(8,128)S(1)} collective-permute-done((f32[256,128]{1,0:T(8,128)S(1)}, f32[256,128]{1,0:T(8,128)S(1)}, u32[]{:S(2)}, u32[]{:S(2)}) %collective-permute-start.10) | collective-permute-done | bytes 131104 | tf_op jit(solution)/shard_map/ppermute | solution.py:333
  34.2 1.0 %collective-permute-start.15 = (f32[256,128]{1,0:T(8,128)S(1)}, f32[256,128]{1,0:T(8,128)S(1)}, u32[]{:S(2)}, u32[]{:S(2)}) collective-permute-start(f32[256,128]{1,0:T(8,128)S(1)} %get-tuple-element.56), channel_id=1, source_target_pairs={{0,2},{1,3},{2,0},{3,1},{4,6},{5,7},{6,4},{7,5},{8,10},{9,11},{10,... | collective-permute-start | bytes 393224 | tf_op jit(solution)/shard_map/ppermute | solution.py:333
  35.7 1.9 %collective-permute-done.13.refs_11_.refs_2_ = f32[256,128]{1,0:T(8,128)S(1)} collective-permute-done((f32[256,128]{1,0:T(8,128)S(1)}, f32[256,128]{1,0:T(8,128)S(1)}, u32[]{:S(2)}, u32[]{:S(2)}) %collective-permute-start.13) | collective-permute-done | bytes 131104 | tf_op jit(solution)/shard_map/ppermute | solution.py:333
  37.7 1.4 %collective-permute-done.15.refs_13_.refs_4_ = f32[256,128]{1,0:T(8,128)S(1)} collective-permute-done((f32[256,128]{1,0:T(8,128)S(1)}, f32[256,128]{1,0:T(8,128)S(1)}, u32[]{:S(2)}, u32[]{:S(2)}) %collective-permute-start.15) | collective-permute-done | bytes 131104 | tf_op jit(solution)/shard_map/ppermute | solution.py:333
  39.8 1.4 %collective-permute-done.17.sibling_ref = f32[1024,128]{1,0:T(8,128)S(1)} collective-permute-done((f32[1024,128]{1,0:T(8,128)S(1)}, f32[1024,128]{1,0:T(8,128)S(1)}, u32[]{:S(2)}, u32[]{:S(2)}) %collective-permute-start.17) | collective-permute-done | bytes 524320 | tf_op jit(solution)/shard_map/ppermute | solution.py:333
  41.2 1.2 %shard_map.70 = bf16[64,4096]{1,0:T(8,128)(2,1)} custom-call(f32[64,128]{1,0:T(8,128)S(1)} %get-tuple-element.32.refs_0_.use_ref, bf16[64,4096]{1,0:T(8,128)(2,1)S(1)} %bitcast.9, f32[1,4096]{1,0:T(1,128)S(1)} %bitcast.11, f32[64,4096]{1,0:T(8,128)S(1)} %get-tuple-element.57.mixed_ref, f32[64,128]{1,0:T(8,128)S(1)} %get-tuple-element.58.squares_ref, ...), custom_call_target="tpu_custom_call" | custom-call | tf_op jit(solution)/shard_map/pallas_call | solution.py:421
  (32 shorter events, 3.5 us)
Async XLA Ops:
  1.5 3.8 %collective-permute-start.1 = (f32[1024,128]{1,0:T(8,128)S(1)}, f32[1024,128]{1,0:T(8,128)S(1)}, u32[]{:S(2)}, u32[]{:S(2)}) collective-permute-start(f32[1024,128]{1,0:T(8,128)S(1)} %get-tuple-element.40), channel_id=1, source_target_pairs={{0,1},{1,0},{2,3},{3,2},{4,5},{5,4},{6,7},{7,6},{8,9},{9,8},{10,11... | collective-permute-start | bytes 1572872 | tf_op jit(solution)/shard_map/ppermute | solution.py:333
  2.0 1.0 %copy-start = (bf16[1,64,4096]{2,1,0:T(8,128)(2,1)S(1)}, bf16[1,64,4096]{2,1,0:T(8,128)(2,1)}, u32[]{:S(2)}) copy-start(bf16[1,64,4096]{2,1,0:T(8,128)(2,1)} %param.5) | copy-start | bytes 1572868
  2.4 7.5 %collective-permute-start = (f32[1024,128]{1,0:T(8,128)S(1)}, f32[1024,128]{1,0:T(8,128)S(1)}, u32[]{:S(2)}, u32[]{:S(2)}) collective-permute-start(f32[1024,128]{1,0:T(8,128)S(1)} %get-tuple-element.39), channel_id=1, source_target_pairs={{0,1},{1,0},{2,3},{3,2},{4,5},{5,4},{6,7},{7,6},{8,9},{9,8},{10,11... | collective-permute-start | bytes 1572872 | tf_op jit(solution)/shard_map/ppermute | solution.py:333
  5.4 7.5 %collective-permute-start.2 = (f32[256,128]{1,0:T(8,128)S(1)}, f32[256,128]{1,0:T(8,128)S(1)}, u32[]{:S(2)}, u32[]{:S(2)}) collective-permute-start(f32[256,128]{1,0:T(8,128)S(1)} %get-tuple-element.41), channel_id=1, source_target_pairs={{0,6},{1,7},{2,4},{3,5},{4,2},{5,3},{6,0},{7,1},{8,14},{9,15},{10,... | collective-permute-start | bytes 393224 | tf_op jit(solution)/shard_map/ppermute | solution.py:333
  9.0 7.5 %collective-permute-start.7 = (f32[256,128]{1,0:T(8,128)S(1)}, f32[256,128]{1,0:T(8,128)S(1)}, u32[]{:S(2)}, u32[]{:S(2)}) collective-permute-start(f32[256,128]{1,0:T(8,128)S(1)} %get-tuple-element.48), channel_id=1, source_target_pairs={{0,4},{1,5},{2,6},{3,7},{4,0},{5,1},{6,2},{7,3},{8,12},{9,13},{10,... | collective-permute-start | bytes 393224 | tf_op jit(solution)/shard_map/ppermute | solution.py:333
  9.5 7.1 %collective-permute-start.8 = (f32[256,128]{1,0:T(8,128)S(1)}, f32[256,128]{1,0:T(8,128)S(1)}, u32[]{:S(2)}, u32[]{:S(2)}) collective-permute-start(f32[256,128]{1,0:T(8,128)S(1)} %get-tuple-element.49), channel_id=1, source_target_pairs={{0,2},{1,3},{2,0},{3,1},{4,6},{5,7},{6,4},{7,5},{8,10},{9,11},{10,... | collective-permute-start | bytes 393224 | tf_op jit(solution)/shard_map/ppermute | solution.py:333
  13.0 7.2 %collective-permute-start.3 = (f32[256,128]{1,0:T(8,128)S(1)}, f32[256,128]{1,0:T(8,128)S(1)}, u32[]{:S(2)}, u32[]{:S(2)}) collective-permute-start(f32[256,128]{1,0:T(8,128)S(1)} %get-tuple-element.43), channel_id=1, source_target_pairs={{0,6},{1,7},{2,4},{3,5},{4,2},{5,3},{6,0},{7,1},{8,14},{9,15},{10,... | collective-permute-start | bytes 393224 | tf_op jit(solution)/shard_map/ppermute | solution.py:333
  15.7 6.6 %collective-permute-start.4 = (f32[256,128]{1,0:T(8,128)S(1)}, f32[256,128]{1,0:T(8,128)S(1)}, u32[]{:S(2)}, u32[]{:S(2)}) collective-permute-start(f32[256,128]{1,0:T(8,128)S(1)} %get-tuple-element.44), channel_id=1, source_target_pairs={{0,4},{1,5},{2,6},{3,7},{4,0},{5,1},{6,2},{7,3},{8,12},{9,13},{10,... | collective-permute-start | bytes 393224 | tf_op jit(solution)/shard_map/ppermute | solution.py:333
  16.1 6.1 %collective-permute-start.5 = (f32[256,128]{1,0:T(8,128)S(1)}, f32[256,128]{1,0:T(8,128)S(1)}, u32[]{:S(2)}, u32[]{:S(2)}) collective-permute-start(f32[256,128]{1,0:T(8,128)S(1)} %get-tuple-element.45), channel_id=1, source_target_pairs={{0,2},{1,3},{2,0},{3,1},{4,6},{5,7},{6,4},{7,5},{8,10},{9,11},{10,... | collective-permute-start | bytes 393224 | tf_op jit(solution)/shard_map/ppermute | solution.py:333
  16.6 11.2 %collective-permute-start.9 = (f32[256,128]{1,0:T(8,128)S(1)}, f32[256,128]{1,0:T(8,128)S(1)}, u32[]{:S(2)}, u32[]{:S(2)}) collective-permute-start(f32[256,128]{1,0:T(8,128)S(1)} %shard_map.65), channel_id=1, source_target_pairs={{0,8},{1,9},{2,10},{3,11},{4,12},{5,13},{6,14},{7,15},{8,0},{9,1},... | collective-permute-start | bytes 393224 | tf_op jit(solution)/shard_map/ppermute | solution.py:336
  22.3 9.2 %collective-permute-start.6 = (f32[256,128]{1,0:T(8,128)S(1)}, f32[256,128]{1,0:T(8,128)S(1)}, u32[]{:S(2)}, u32[]{:S(2)}) collective-permute-start(f32[256,128]{1,0:T(8,128)S(1)} %shard_map.61.refs_0_), channel_id=1, source_target_pairs={{0,8},{1,9},{2,10},{3,11},{4,12},{5,13},{6,14},{7,15},{8,0},{9,1},... | collective-permute-start | bytes 393224 | tf_op jit(solution)/shard_map/ppermute | solution.py:336
  27.9 6.3 %collective-permute-start.10 = (f32[256,128]{1,0:T(8,128)S(1)}, f32[256,128]{1,0:T(8,128)S(1)}, u32[]{:S(2)}, u32[]{:S(2)}) collective-permute-start(f32[256,128]{1,0:T(8,128)S(1)} %get-tuple-element.51), channel_id=1, source_target_pairs={{0,6},{1,7},{2,4},{3,5},{4,2},{5,3},{6,0},{7,1},{8,14},{9,15},{10,... | collective-permute-start | bytes 393224 | tf_op jit(solution)/shard_map/ppermute | solution.py:333
  28.6 6.5 %collective-permute-start.11 = (f32[256,128]{1,0:T(8,128)S(1)}, f32[256,128]{1,0:T(8,128)S(1)}, u32[]{:S(2)}, u32[]{:S(2)}) collective-permute-start(f32[256,128]{1,0:T(8,128)S(1)} %get-tuple-element.52), channel_id=1, source_target_pairs={{0,4},{1,5},{2,6},{3,7},{4,0},{5,1},{6,2},{7,3},{8,12},{9,13},{10,... | collective-permute-start | bytes 393224 | tf_op jit(solution)/shard_map/ppermute | solution.py:333
  29.5 6.0 %collective-permute-start.12 = (f32[256,128]{1,0:T(8,128)S(1)}, f32[256,128]{1,0:T(8,128)S(1)}, u32[]{:S(2)}, u32[]{:S(2)}) collective-permute-start(f32[256,128]{1,0:T(8,128)S(1)} %get-tuple-element.53), channel_id=1, source_target_pairs={{0,2},{1,3},{2,0},{3,1},{4,6},{5,7},{6,4},{7,5},{8,10},{9,11},{10,... | collective-permute-start | bytes 393224 | tf_op jit(solution)/shard_map/ppermute | solution.py:333
  31.6 5.9 %collective-permute-start.13 = (f32[256,128]{1,0:T(8,128)S(1)}, f32[256,128]{1,0:T(8,128)S(1)}, u32[]{:S(2)}, u32[]{:S(2)}) collective-permute-start(f32[256,128]{1,0:T(8,128)S(1)} %get-tuple-element.54), channel_id=1, source_target_pairs={{0,6},{1,7},{2,4},{3,5},{4,2},{5,3},{6,0},{7,1},{8,14},{9,15},{10,... | collective-permute-start | bytes 393224 | tf_op jit(solution)/shard_map/ppermute | solution.py:333
  32.3 5.4 %collective-permute-start.14 = (f32[256,128]{1,0:T(8,128)S(1)}, f32[256,128]{1,0:T(8,128)S(1)}, u32[]{:S(2)}, u32[]{:S(2)}) collective-permute-start(f32[256,128]{1,0:T(8,128)S(1)} %get-tuple-element.55), channel_id=1, source_target_pairs={{0,4},{1,5},{2,6},{3,7},{4,0},{5,1},{6,2},{7,3},{8,12},{9,13},{10,... | collective-permute-start | bytes 393224 | tf_op jit(solution)/shard_map/ppermute | solution.py:333
  34.2 5.0 %collective-permute-start.15 = (f32[256,128]{1,0:T(8,128)S(1)}, f32[256,128]{1,0:T(8,128)S(1)}, u32[]{:S(2)}, u32[]{:S(2)}) collective-permute-start(f32[256,128]{1,0:T(8,128)S(1)} %get-tuple-element.56), channel_id=1, source_target_pairs={{0,2},{1,3},{2,0},{3,1},{4,6},{5,7},{6,4},{7,5},{8,10},{9,11},{10,... | collective-permute-start | bytes 393224 | tf_op jit(solution)/shard_map/ppermute | solution.py:333
  35.6 3.8 %copy-start.1 = (f32[4096]{0:T(1024)S(1)}, f32[4096]{0:T(1024)}, u32[]{:S(2)}) copy-start(f32[4096]{0:T(1024)} %param.9) | copy-start | bytes 49156
  35.6 3.7 %collective-permute-start.16 = (f32[1024,128]{1,0:T(8,128)S(1)}, f32[1024,128]{1,0:T(8,128)S(1)}, u32[]{:S(2)}, u32[]{:S(2)}) collective-permute-start(f32[1024,128]{1,0:T(8,128)S(1)} %shard_map.67), channel_id=1, source_target_pairs={{0,1},{1,0},{2,3},{3,2},{4,5},{5,4},{6,7},{7,6},{8,9},{9,8},{10,11... | collective-permute-start | bytes 1572872 | tf_op jit(solution)/shard_map/ppermute | solution.py:333
  39.2 2.0 %collective-permute-start.17 = (f32[1024,128]{1,0:T(8,128)S(1)}, f32[1024,128]{1,0:T(8,128)S(1)}, u32[]{:S(2)}, u32[]{:S(2)}) collective-permute-start(f32[1024,128]{1,0:T(8,128)S(1)} %shard_map.69), channel_id=1, source_target_pairs={{0,1},{1,0},{2,3},{3,2},{4,5},{5,4},{6,7},{7,6},{8,9},{9,8},{10,11... | collective-permute-start | bytes 1572872 | tf_op jit(solution)/shard_map/ppermute | solution.py:333

commit v5 on v4

--- a/solution.py
+++ b/solution.py
@@ -196,13 +196,28 @@
     return before
 
 
+def query_kernel(query_ref, *refs):
+    core, chip, _, _ = place()
+    width = query_ref.shape[1]
+    order = steps(width)
+    half = len(order) // 2
+    for i, step in enumerate(order[half:]):
+        refs[-1][:, tile(i)] = query_ref[:, column(width, core, chip, *step)].astype(F32)
+
+
 def pair_kernel(part, spots, weight, *refs):
-    keeps, pieces, out = refs[:len(FRONT[part])], refs[len(FRONT[part]):][:len(spots)], refs[-1]
+    keeps, pieces = refs[:len(FRONT[part])], refs[len(FRONT[part]):][:len(spots)]
+    query_ref, out = refs[len(keeps) + len(spots)], refs[-1]
+    width = 2 * query_ref.shape[1]
+    order = steps(width)
     size = pieces[0].shape[0]
     for i, (spot, piece) in enumerate(zip(spots, pieces)):
         which, place_in = found_in(FRONT[part], spot)
         keep = keeps[which][place_in * size:(place_in + 1) * size, :]
-        out[i * size:(i + 1) * size, :] = weight("pair_scale") * piece[...] + weight("pair_add") * keep
+        state = (weight("pair_scale") * piece[...] + weight("pair_add") * keep).astype(BF16)
+        for j in range(size // HD):
+            query = query_ref[:, tile(order.index((True, part, QUARTERS[spot], j)))].astype(BF16)
+            out[:, tile(i * (size // HD) + j)] = jnp.dot(query, state[tile(j), :], preferred_element_type=F32)
 
 
 def intra_kernel(on, span, allowed_ref, query_ref, key_ref, value_ref, *refs):
@@ -260,39 +275,41 @@
             which, at = found_in(FRONT[part], spot)
             state = weight("mix_scale") * states[part][spot][tile(j), :]
             state = state + weight("mix_add") * gots[part][which][tile(at * size + j), :]
+            past = from_past(use, query_ref, step, state)
         elif i < first:
             which, at = found_in(BACK[part], spot)
-            state = siblings[part][which][tile(at * size + j), :]
+            past = use * siblings[part][which][:, tile(at * size + j)]
         else:
             mixed_ref[:, tile(i)] = both
             continue
-        both = both + from_past(use, query_ref, step, state)
+        both = both + past
         squares = squares + both * both
         mixed_ref[:, tile(i)] = both * gain_ref[:, column(width, core, chip, *step)]
     squares_ref[...] = squares
 
 
-def norm_kernel(use_ref, query_ref, gain_ref, mixed_ref, squares_ref, sibling_ref, out_hbm, out_ref, sems):
-    core, chip, _, _ = place()
-    rows, width = query_ref.shape
+def norm_kernel(use_ref, gain_ref, mixed_ref, squares_ref, sibling_ref, out_hbm, out_ref, sems):
+    core, chip, _, _ = place()
+    rows, width = out_ref.shape
     order = steps(width)
-    first = len(order) - sibling_ref.shape[0] // HD
+    first = len(order) - sibling_ref.shape[1] // HD
     use = use_ref[...]
     squares = squares_ref[...]
     late = []
     for i, step in enumerate(order[first:]):
-        both = mixed_ref[:, tile(first + i)] + from_past(use, query_ref, step, sibling_ref[tile(i), :])
+        both = mixed_ref[:, tile(first + i)] + use * sibling_ref[:, tile(i)]
         squares = squares + both * both
         late.append(both * gain_ref[:, column(width, core, chip, *step)])
     mean = jnp.sum(squares, axis=-1, keepdims=True) * (1.0 / width)
     norm = jnp.broadcast_to(lax.rsqrt(mean + 1e-05), (rows, HD))
-    for i, step in enumerate(order):
-        both = mixed_ref[:, tile(i)] if i < first else late[i - first]
-        out_ref[:, column(width, core, chip, *step)] = (both * norm).astype(BF16)
     copies = []
-    for i in range(sems.shape[0]):
-        at = slice(i * rows // sems.shape[0], (i + 1) * rows // sems.shape[0])
-        copies.append(pltpu.make_async_copy(out_ref.at[at, :], out_hbm.at[at, :], sems.at[i]))
+    number = sems.shape[0]
+    for part in range(number):
+        at = slice(part * rows // number, (part + 1) * rows // number)
+        for i, step in enumerate(order):
+            both = mixed_ref[at, tile(i)] if i < first else late[i - first][at, :]
+            out_ref[at, column(width, core, chip, *step)] = (both * norm[at, :]).astype(BF16)
+        copies.append(pltpu.make_async_copy(out_ref.at[at, :], out_hbm.at[at, :], sems.at[part]))
         copies[-1].start()
     for copy in copies:
         copy.wait()
@@ -400,12 +417,13 @@
         siblings[part] = []
         for spots in BACK[part]:
             siblings[part].append(swap(weighted(
-                functools.partial(pair_kernel, part, spots), tall(part, spots), *keeps[part],
-                *[states[part][spot] for spot in spots], *after), 1))
+                functools.partial(pair_kernel, part, spots), array((rows, tall(part, spots).shape[0])), *keeps[part],
+                *[states[part][spot] for spot in spots], asked, *after), 1))
         return siblings[part][:1]
 
+    asked = swap(call(query_kernel, array((rows, width // 2)), query), 1)
     a = begin(0, *inside("start", keeps[0][0]))
-    b = begin(1, a[1])
+    b = begin(1, a[1], asked)
     a = between(0, *inside("begin", b[0]))
     b = between(1, *inside("between", a[0]))
     a = enter(0, *inside("between1", b[0]))
@@ -419,9 +437,9 @@
         *intras, *[piece for state in states for piece in state], *[got for group in gots for got in group],
         *[sibling for group in siblings for sibling in group][:-1])
     attended = pl.pallas_call(
-        norm_kernel, out_shape=array((rows, width), BF16), in_specs=[VM] * 6, out_specs=HB,
+        norm_kernel, out_shape=array((rows, width), BF16), in_specs=[VM] * 5, out_specs=HB,
         scratch_shapes=[pltpu.VMEM((rows, width), BF16), pltpu.SemaphoreType.DMA((2,))], compiler_params=PARAMS,
-    )(use, query, gain, mixed, squares, siblings[-1][-1])
+    )(use, gain, mixed, squares, siblings[-1][-1])
     return attended[None]
 
 

time: 42.6 us -> 42.1 us (0.988)
  local copies, waits for them, and re-layouts: 0.57 us -> 0.01 us
  starting transfers between devices: 20.6 us -> 21.1 us
  waiting for transfers between devices: 12.2 us -> 11.7 us
    ppermute x16 -> x17, starting transfers between devices: 14.6 us -> 15.2 us  [swap(): return lax.ppermute(what, 'ctx', [(i, i ^ bits) for i in range(count)])]
    unnamed x4, local copies, waits for them, and re-layouts: 0.57 us -> 0.01 us
    ppermute x16 -> x17, waiting for transfers between devices: 12.2 us -> 11.7 us  [swap(): return lax.ppermute(what, 'ctx', [(i, i ^ bits) for i in range(count)])]
    pallas_call x14 -> x15, Pallas kernels: 6.16 us -> 6.47 us  [call(): pl.pallas_call(kernel, out_shape=outs, in_specs=[VM] * len(args), out_spe...]
  transfers between devices with their start and end apart: 18 -> 19, of which waited for: 9 -> 9; matrix products, arithmetic and copies ran while one was open for 0% -> 0% of each run, Pallas kernels for 15% -> 15%
where the time goes in v5:
time: 42.1 us; the launch traced here: 41.9 us
  starting transfers between devices  21.1 us (50%)
  waiting for transfers between devices  11.7 us (28%)
  Pallas kernels  8.98 us (21%)
    ppermute x17, starting transfers between devices, swap(): return lax.ppermute(what, 'ctx', [(i, i ^ bits) for i in range(count)])  15.2 us
    ppermute x17, waiting for transfers between devices, swap(): return lax.ppermute(what, 'ctx', [(i, i ^ bits) for i in range(count)])  11.7 us
    pallas_call x15, Pallas kernels, call(): pl.pallas_call(kernel, out_shape=outs, in_specs=[VM] * len(args), out_spe...  6.47 us
    ppermute x2, starting transfers between devices, later(): lax.ppermute(what, 'ctx', [(i, (i + shift * 2 * CHIPS) % count) for i in...  5.91 us
    pallas_call x1, Pallas kernels, shards(): pl.pallas_call(functools.partial(first_kernel, groups), out_shape=[array(...  1.56 us
    pallas_call x1, Pallas kernels, shards(): pl.pallas_call(norm_kernel, out_shape=array((rows, width), BF16), in_spec...  0.95 us
  transfers between devices with their start and end apart: 19, of which 9 were waited for; matrix products, arithmetic and copies ran while one was open for 0% of the time, Pallas kernels for 15%

profile of v5, /device:TPU:0, one launch (start us, length us, event | category | flops | bytes accessed | tf_op | source)
XLA Modules:
  0.0 41.9 jit_solution(4982937312927292103)
XLA Ops:
  0.0 1.6 %shard_map.55 = (bf16[64,4096]{1,0:T(8,128)(2,1)S(1)}, bf16[64,4096]{1,0:T(8,128)(2,1)S(1)}, f32[32,128]{1,0:T(8,128)S(1)}, bf16[64,128]{1,0:T(8,128)(2,1)S(1)},...) custom-call(s32[1,4]{1,0:T(1,128)} %starts_hbm.1, bf16[64,4096]{1,0:T(8,128)(2,1)} %bitcast.12, ...), custom_call_target="tpu_custom_call" | custom-call | tf_op jit(solution)/shard_map/pallas_call | solution.py:363
  1.6 0.5 %collective-permute-start.1 = (f32[1024,128]{1,0:T(8,128)S(1)}, f32[1024,128]{1,0:T(8,128)S(1)}, u32[]{:S(2)}, u32[]{:S(2)}) collective-permute-start(f32[1024,128]{1,0:T(8,128)S(1)} %get-tuple-element.40), channel_id=1, source_target_pairs={{0,1},{1,0},{2,3},{3,2},{4,5},{5,4},{6,7},{7,6},{8,9},{9,8},{10,11... | collective-permute-start | bytes 1572872 | tf_op jit(solution)/shard_map/ppermute | solution.py:350
  2.6 0.5 %collective-permute-start = (f32[1024,128]{1,0:T(8,128)S(1)}, f32[1024,128]{1,0:T(8,128)S(1)}, u32[]{:S(2)}, u32[]{:S(2)}) collective-permute-start(f32[1024,128]{1,0:T(8,128)S(1)} %get-tuple-element.39), channel_id=1, source_target_pairs={{0,1},{1,0},{2,3},{3,2},{4,5},{5,4},{6,7},{7,6},{8,9},{9,8},{10,11... | collective-permute-start | bytes 1572872 | tf_op jit(solution)/shard_map/ppermute | solution.py:350
  3.2 2.3 %shard_map.57.refs_2_.refs_3_ = f32[64,2048]{1,0:T(8,128)S(1)} custom-call(f32[64,64]{1,0:T(8,128)S(1)} %get-tuple-element.34.allowed_ref, bf16[64,4096]{1,0:T(8,128)(2,1)S(1)} %bitcast.6, bf16[64,4096]{1,0:T(8,128)(2,1)S(1)} %get-tuple-element.35.key_ref, bf16[64,4096]{1,0:T(8,128)(2,1)S(1)} %get-tuple-element.36.value_ref, ...), custom_call_target="tpu_custom_call" | custom-call | tf_op jit(solution)/shard_map/pallas_call | solution.py:338
  5.5 3.6 %collective-permute-start.2 = (f32[256,128]{1,0:T(8,128)S(1)}, f32[256,128]{1,0:T(8,128)S(1)}, u32[]{:S(2)}, u32[]{:S(2)}) collective-permute-start(f32[256,128]{1,0:T(8,128)S(1)} %get-tuple-element.41), channel_id=1, source_target_pairs={{0,6},{1,7},{2,4},{3,5},{4,2},{5,3},{6,0},{7,1},{8,14},{9,15},{10,... | collective-permute-start | bytes 393224 | tf_op jit(solution)/shard_map/ppermute | solution.py:350
  10.1 2.8 %collective-permute-done.2.refs_2_.refs_1_ = f32[256,128]{1,0:T(8,128)S(1)} collective-permute-done((f32[256,128]{1,0:T(8,128)S(1)}, f32[256,128]{1,0:T(8,128)S(1)}, u32[]{:S(2)}, u32[]{:S(2)}) %collective-permute-start.2) | collective-permute-done | bytes 131104 | tf_op jit(solution)/shard_map/ppermute | solution.py:350
  13.0 2.7 %collective-permute-start.4 = (f32[256,128]{1,0:T(8,128)S(1)}, f32[256,128]{1,0:T(8,128)S(1)}, u32[]{:S(2)}, u32[]{:S(2)}) collective-permute-start(f32[256,128]{1,0:T(8,128)S(1)} %get-tuple-element.43), channel_id=1, source_target_pairs={{0,6},{1,7},{2,4},{3,5},{4,2},{5,3},{6,0},{7,1},{8,14},{9,15},{10,... | collective-permute-start | bytes 393224 | tf_op jit(solution)/shard_map/ppermute | solution.py:350
  15.7 0.5 %collective-permute-start.5 = (f32[256,128]{1,0:T(8,128)S(1)}, f32[256,128]{1,0:T(8,128)S(1)}, u32[]{:S(2)}, u32[]{:S(2)}) collective-permute-start(f32[256,128]{1,0:T(8,128)S(1)} %get-tuple-element.44), channel_id=1, source_target_pairs={{0,4},{1,5},{2,6},{3,7},{4,0},{5,1},{6,2},{7,3},{8,12},{9,13},{10,... | collective-permute-start | bytes 393224 | tf_op jit(solution)/shard_map/ppermute | solution.py:350
  16.6 2.8 %collective-permute-start.10 = (f32[256,128]{1,0:T(8,128)S(1)}, f32[256,128]{1,0:T(8,128)S(1)}, u32[]{:S(2)}, u32[]{:S(2)}) collective-permute-start(f32[256,128]{1,0:T(8,128)S(1)} %shard_map.66), channel_id=1, source_target_pairs={{0,8},{1,9},{2,10},{3,11},{4,12},{5,13},{6,14},{7,15},{8,0},{9,1},... | collective-permute-start | bytes 393224 | tf_op jit(solution)/shard_map/ppermute | solution.py:353
  19.4 0.9 %collective-permute-done.4.refs_1_ = f32[256,128]{1,0:T(8,128)S(1)} collective-permute-done((f32[256,128]{1,0:T(8,128)S(1)}, f32[256,128]{1,0:T(8,128)S(1)}, u32[]{:S(2)}, u32[]{:S(2)}) %collective-permute-start.4) | collective-permute-done | bytes 131104 | tf_op jit(solution)/shard_map/ppermute | solution.py:350
  20.3 2.1 %collective-permute-done.5.refs_2_ = f32[256,128]{1,0:T(8,128)S(1)} collective-permute-done((f32[256,128]{1,0:T(8,128)S(1)}, f32[256,128]{1,0:T(8,128)S(1)}, u32[]{:S(2)}, u32[]{:S(2)}) %collective-permute-start.5) | collective-permute-done | bytes 131104 | tf_op jit(solution)/shard_map/ppermute | solution.py:350
  22.5 3.1 %collective-permute-start.7 = (f32[256,128]{1,0:T(8,128)S(1)}, f32[256,128]{1,0:T(8,128)S(1)}, u32[]{:S(2)}, u32[]{:S(2)}) collective-permute-start(f32[256,128]{1,0:T(8,128)S(1)} %shard_map.62.refs_0_), channel_id=1, source_target_pairs={{0,8},{1,9},{2,10},{3,11},{4,12},{5,13},{6,14},{7,15},{8,0},{9,1},... | collective-permute-start | bytes 393224 | tf_op jit(solution)/shard_map/ppermute | solution.py:353
  25.6 2.3 %shard_map.63.refs_5_.refs_4_ = f32[64,2048]{1,0:T(8,128)S(1)} custom-call(f32[64,64]{1,0:T(8,128)S(1)} %get-tuple-element.34.allowed_ref, bf16[64,4096]{1,0:T(8,128)(2,1)S(1)} %bitcast.7, bf16[64,4096]{1,0:T(8,128)(2,1)S(1)} %get-tuple-element.35.key_ref, bf16[64,4096]{1,0:T(8,128)(2,1)S(1)} %get-tuple-element.36.value_ref, f32[256,128]{1,0:T(8,128)S(1)} %shard_map.62.refs_0_), custom_call_target="tpu_custom_call" | custom-call | tf_op jit(solution)/shard_map/pallas_call | solution.py:338
  28.0 0.7 %collective-permute-start.11 = (f32[256,128]{1,0:T(8,128)S(1)}, f32[256,128]{1,0:T(8,128)S(1)}, u32[]{:S(2)}, u32[]{:S(2)}) collective-permute-start(f32[256,128]{1,0:T(8,128)S(1)} %get-tuple-element.51), channel_id=1, source_target_pairs={{0,6},{1,7},{2,4},{3,5},{4,2},{5,3},{6,0},{7,1},{8,14},{9,15},{10,... | collective-permute-start | bytes 393224 | tf_op jit(solution)/shard_map/ppermute | solution.py:350
  28.7 0.8 %collective-permute-start.12 = (f32[256,128]{1,0:T(8,128)S(1)}, f32[256,128]{1,0:T(8,128)S(1)}, u32[]{:S(2)}, u32[]{:S(2)}) collective-permute-start(f32[256,128]{1,0:T(8,128)S(1)} %get-tuple-element.52), channel_id=1, source_target_pairs={{0,4},{1,5},{2,6},{3,7},{4,0},{5,1},{6,2},{7,3},{8,12},{9,13},{10,... | collective-permute-start | bytes 393224 | tf_op jit(solution)/shard_map/ppermute | solution.py:350
  29.5 2.0 %collective-permute-start.13 = (f32[256,128]{1,0:T(8,128)S(1)}, f32[256,128]{1,0:T(8,128)S(1)}, u32[]{:S(2)}, u32[]{:S(2)}) collective-permute-start(f32[256,128]{1,0:T(8,128)S(1)} %get-tuple-element.53), channel_id=1, source_target_pairs={{0,2},{1,3},{2,0},{3,1},{4,6},{5,7},{6,4},{7,5},{8,10},{9,11},{10,... | collective-permute-start | bytes 393224 | tf_op jit(solution)/shard_map/ppermute | solution.py:350
  31.7 0.7 %collective-permute-start.14 = (f32[256,128]{1,0:T(8,128)S(1)}, f32[256,128]{1,0:T(8,128)S(1)}, u32[]{:S(2)}, u32[]{:S(2)}) collective-permute-start(f32[256,128]{1,0:T(8,128)S(1)} %get-tuple-element.54), channel_id=1, source_target_pairs={{0,6},{1,7},{2,4},{3,5},{4,2},{5,3},{6,0},{7,1},{8,14},{9,15},{10,... | collective-permute-start | bytes 393224 | tf_op jit(solution)/shard_map/ppermute | solution.py:350
  32.4 0.8 %collective-permute-start.15 = (f32[256,128]{1,0:T(8,128)S(1)}, f32[256,128]{1,0:T(8,128)S(1)}, u32[]{:S(2)}, u32[]{:S(2)}) collective-permute-start(f32[256,128]{1,0:T(8,128)S(1)} %get-tuple-element.55), channel_id=1, source_target_pairs={{0,4},{1,5},{2,6},{3,7},{4,0},{5,1},{6,2},{7,3},{8,12},{9,13},{10,... | collective-permute-start | bytes 393224 | tf_op jit(solution)/shard_map/ppermute | solution.py:350
  33.2 1.0 %collective-permute-done.11.refs_2_.refs_7_ = f32[256,128]{1,0:T(8,128)S(1)} collective-permute-done((f32[256,128]{1,0:T(8,128)S(1)}, f32[256,128]{1,0:T(8,128)S(1)}, u32[]{:S(2)}, u32[]{:S(2)}) %collective-permute-start.11) | collective-permute-done | bytes 131104 | tf_op jit(solution)/shard_map/ppermute | solution.py:350
  34.2 1.0 %collective-permute-start.16 = (f32[256,128]{1,0:T(8,128)S(1)}, f32[256,128]{1,0:T(8,128)S(1)}, u32[]{:S(2)}, u32[]{:S(2)}) collective-permute-start(f32[256,128]{1,0:T(8,128)S(1)} %get-tuple-element.56), channel_id=1, source_target_pairs={{0,2},{1,3},{2,0},{3,1},{4,6},{5,7},{6,4},{7,5},{8,10},{9,11},{10,... | collective-permute-start | bytes 393224 | tf_op jit(solution)/shard_map/ppermute | solution.py:350
  35.8 1.8 %collective-permute-done.14.refs_11_.refs_2_ = f32[256,128]{1,0:T(8,128)S(1)} collective-permute-done((f32[256,128]{1,0:T(8,128)S(1)}, f32[256,128]{1,0:T(8,128)S(1)}, u32[]{:S(2)}, u32[]{:S(2)}) %collective-permute-start.14) | collective-permute-done | bytes 131104 | tf_op jit(solution)/shard_map/ppermute | solution.py:350
  37.8 1.4 %collective-permute-done.16.refs_13_.refs_4_ = f32[256,128]{1,0:T(8,128)S(1)} collective-permute-done((f32[256,128]{1,0:T(8,128)S(1)}, f32[256,128]{1,0:T(8,128)S(1)}, u32[]{:S(2)}, u32[]{:S(2)}) %collective-permute-start.16) | collective-permute-done | bytes 131104 | tf_op jit(solution)/shard_map/ppermute | solution.py:350
  39.9 1.1 %collective-permute-done.18.sibling_ref = f32[64,1024]{1,0:T(8,128)S(1)} collective-permute-done((f32[64,1024]{1,0:T(8,128)S(1)}, f32[64,1024]{1,0:T(8,128)S(1)}, u32[]{:S(2)}, u32[]{:S(2)}) %collective-permute-start.18) | collective-permute-done | bytes 262176 | tf_op jit(solution)/shard_map/ppermute | solution.py:350
  41.0 1.0 %shard_map.71 = bf16[64,4096]{1,0:T(8,128)(2,1)} custom-call(f32[64,128]{1,0:T(8,128)S(1)} %get-tuple-element.32.refs_0_.use_ref, f32[1,4096]{1,0:T(1,128)S(1)} %bitcast.11, f32[64,4096]{1,0:T(8,128)S(1)} %get-tuple-element.57.mixed_ref, f32[64,128]{1,0:T(8,128)S(1)} %get-tuple-element.58.squares_ref, f32[64,1024]{1,0:T(8,128)S(1)} %collective-permute-done.18.sibling_ref), custom_call_target="tpu_custom_call" | custom-call | tf_op jit(solution)/shard_map/pallas_call | solution.py:439
  (35 shorter events, 3.7 us)
Async XLA Ops:
  0.0 2.1 %copy-start = (bf16[1,64,4096]{2,1,0:T(8,128)(2,1)S(1)}, bf16[1,64,4096]{2,1,0:T(8,128)(2,1)}, u32[]{:S(2)}) copy-start(bf16[1,64,4096]{2,1,0:T(8,128)(2,1)} %param.5) | copy-start | bytes 1572868
  1.6 3.9 %collective-permute-start.1 = (f32[1024,128]{1,0:T(8,128)S(1)}, f32[1024,128]{1,0:T(8,128)S(1)}, u32[]{:S(2)}, u32[]{:S(2)}) collective-permute-start(f32[1024,128]{1,0:T(8,128)S(1)} %get-tuple-element.40), channel_id=1, source_target_pairs={{0,1},{1,0},{2,3},{3,2},{4,5},{5,4},{6,7},{7,6},{8,9},{9,8},{10,11... | collective-permute-start | bytes 1572872 | tf_op jit(solution)/shard_map/ppermute | solution.py:350
  2.2 7.9 %collective-permute-start.3 = (f32[64,2048]{1,0:T(8,128)S(1)}, f32[64,2048]{1,0:T(8,128)S(1)}, u32[]{:S(2)}, u32[]{:S(2)}) collective-permute-start(f32[64,2048]{1,0:T(8,128)S(1)} %shard_map.60), channel_id=1, source_target_pairs={{0,1},{1,0},{2,3},{3,2},{4,5},{5,4},{6,7},{7,6},{8,9},{9,8},{10,11... | collective-permute-start | bytes 1572872 | tf_op jit(solution)/shard_map/ppermute | solution.py:350
  2.6 7.4 %collective-permute-start = (f32[1024,128]{1,0:T(8,128)S(1)}, f32[1024,128]{1,0:T(8,128)S(1)}, u32[]{:S(2)}, u32[]{:S(2)}) collective-permute-start(f32[1024,128]{1,0:T(8,128)S(1)} %get-tuple-element.39), channel_id=1, source_target_pairs={{0,1},{1,0},{2,3},{3,2},{4,5},{5,4},{6,7},{7,6},{8,9},{9,8},{10,11... | collective-permute-start | bytes 1572872 | tf_op jit(solution)/shard_map/ppermute | solution.py:350
  5.5 7.4 %collective-permute-start.2 = (f32[256,128]{1,0:T(8,128)S(1)}, f32[256,128]{1,0:T(8,128)S(1)}, u32[]{:S(2)}, u32[]{:S(2)}) collective-permute-start(f32[256,128]{1,0:T(8,128)S(1)} %get-tuple-element.41), channel_id=1, source_target_pairs={{0,6},{1,7},{2,4},{3,5},{4,2},{5,3},{6,0},{7,1},{8,14},{9,15},{10,... | collective-permute-start | bytes 393224 | tf_op jit(solution)/shard_map/ppermute | solution.py:350
  9.1 7.4 %collective-permute-start.8 = (f32[256,128]{1,0:T(8,128)S(1)}, f32[256,128]{1,0:T(8,128)S(1)}, u32[]{:S(2)}, u32[]{:S(2)}) collective-permute-start(f32[256,128]{1,0:T(8,128)S(1)} %get-tuple-element.48), channel_id=1, source_target_pairs={{0,4},{1,5},{2,6},{3,7},{4,0},{5,1},{6,2},{7,3},{8,12},{9,13},{10,... | collective-permute-start | bytes 393224 | tf_op jit(solution)/shard_map/ppermute | solution.py:350
  9.6 7.0 %collective-permute-start.9 = (f32[256,128]{1,0:T(8,128)S(1)}, f32[256,128]{1,0:T(8,128)S(1)}, u32[]{:S(2)}, u32[]{:S(2)}) collective-permute-start(f32[256,128]{1,0:T(8,128)S(1)} %get-tuple-element.49), channel_id=1, source_target_pairs={{0,2},{1,3},{2,0},{3,1},{4,6},{5,7},{6,4},{7,5},{8,10},{9,11},{10,... | collective-permute-start | bytes 393224 | tf_op jit(solution)/shard_map/ppermute | solution.py:350
  13.0 7.3 %collective-permute-start.4 = (f32[256,128]{1,0:T(8,128)S(1)}, f32[256,128]{1,0:T(8,128)S(1)}, u32[]{:S(2)}, u32[]{:S(2)}) collective-permute-start(f32[256,128]{1,0:T(8,128)S(1)} %get-tuple-element.43), channel_id=1, source_target_pairs={{0,6},{1,7},{2,4},{3,5},{4,2},{5,3},{6,0},{7,1},{8,14},{9,15},{10,... | collective-permute-start | bytes 393224 | tf_op jit(solution)/shard_map/ppermute | solution.py:350
  15.7 6.7 %collective-permute-start.5 = (f32[256,128]{1,0:T(8,128)S(1)}, f32[256,128]{1,0:T(8,128)S(1)}, u32[]{:S(2)}, u32[]{:S(2)}) collective-permute-start(f32[256,128]{1,0:T(8,128)S(1)} %get-tuple-element.44), channel_id=1, source_target_pairs={{0,4},{1,5},{2,6},{3,7},{4,0},{5,1},{6,2},{7,3},{8,12},{9,13},{10,... | collective-permute-start | bytes 393224 | tf_op jit(solution)/shard_map/ppermute | solution.py:350
  16.2 6.2 %collective-permute-start.6 = (f32[256,128]{1,0:T(8,128)S(1)}, f32[256,128]{1,0:T(8,128)S(1)}, u32[]{:S(2)}, u32[]{:S(2)}) collective-permute-start(f32[256,128]{1,0:T(8,128)S(1)} %get-tuple-element.45), channel_id=1, source_target_pairs={{0,2},{1,3},{2,0},{3,1},{4,6},{5,7},{6,4},{7,5},{8,10},{9,11},{10,... | collective-permute-start | bytes 393224 | tf_op jit(solution)/shard_map/ppermute | solution.py:350
  16.6 11.2 %collective-permute-start.10 = (f32[256,128]{1,0:T(8,128)S(1)}, f32[256,128]{1,0:T(8,128)S(1)}, u32[]{:S(2)}, u32[]{:S(2)}) collective-permute-start(f32[256,128]{1,0:T(8,128)S(1)} %shard_map.66), channel_id=1, source_target_pairs={{0,8},{1,9},{2,10},{3,11},{4,12},{5,13},{6,14},{7,15},{8,0},{9,1},... | collective-permute-start | bytes 393224 | tf_op jit(solution)/shard_map/ppermute | solution.py:353
  22.5 9.1 %collective-permute-start.7 = (f32[256,128]{1,0:T(8,128)S(1)}, f32[256,128]{1,0:T(8,128)S(1)}, u32[]{:S(2)}, u32[]{:S(2)}) collective-permute-start(f32[256,128]{1,0:T(8,128)S(1)} %shard_map.62.refs_0_), channel_id=1, source_target_pairs={{0,8},{1,9},{2,10},{3,11},{4,12},{5,13},{6,14},{7,15},{8,0},{9,1},... | collective-permute-start | bytes 393224 | tf_op jit(solution)/shard_map/ppermute | solution.py:353
  28.0 6.3 %collective-permute-start.11 = (f32[256,128]{1,0:T(8,128)S(1)}, f32[256,128]{1,0:T(8,128)S(1)}, u32[]{:S(2)}, u32[]{:S(2)}) collective-permute-start(f32[256,128]{1,0:T(8,128)S(1)} %get-tuple-element.51), channel_id=1, source_target_pairs={{0,6},{1,7},{2,4},{3,5},{4,2},{5,3},{6,0},{7,1},{8,14},{9,15},{10,... | collective-permute-start | bytes 393224 | tf_op jit(solution)/shard_map/ppermute | solution.py:350
  28.7 6.5 %collective-permute-start.12 = (f32[256,128]{1,0:T(8,128)S(1)}, f32[256,128]{1,0:T(8,128)S(1)}, u32[]{:S(2)}, u32[]{:S(2)}) collective-permute-start(f32[256,128]{1,0:T(8,128)S(1)} %get-tuple-element.52), channel_id=1, source_target_pairs={{0,4},{1,5},{2,6},{3,7},{4,0},{5,1},{6,2},{7,3},{8,12},{9,13},{10,... | collective-permute-start | bytes 393224 | tf_op jit(solution)/shard_map/ppermute | solution.py:350
  29.5 6.0 %collective-permute-start.13 = (f32[256,128]{1,0:T(8,128)S(1)}, f32[256,128]{1,0:T(8,128)S(1)}, u32[]{:S(2)}, u32[]{:S(2)}) collective-permute-start(f32[256,128]{1,0:T(8,128)S(1)} %get-tuple-element.53), channel_id=1, source_target_pairs={{0,2},{1,3},{2,0},{3,1},{4,6},{5,7},{6,4},{7,5},{8,10},{9,11},{10,... | collective-permute-start | bytes 393224 | tf_op jit(solution)/shard_map/ppermute | solution.py:350
  31.7 5.9 %collective-permute-start.14 = (f32[256,128]{1,0:T(8,128)S(1)}, f32[256,128]{1,0:T(8,128)S(1)}, u32[]{:S(2)}, u32[]{:S(2)}) collective-permute-start(f32[256,128]{1,0:T(8,128)S(1)} %get-tuple-element.54), channel_id=1, source_target_pairs={{0,6},{1,7},{2,4},{3,5},{4,2},{5,3},{6,0},{7,1},{8,14},{9,15},{10,... | collective-permute-start | bytes 393224 | tf_op jit(solution)/shard_map/ppermute | solution.py:350
  32.4 5.4 %collective-permute-start.15 = (f32[256,128]{1,0:T(8,128)S(1)}, f32[256,128]{1,0:T(8,128)S(1)}, u32[]{:S(2)}, u32[]{:S(2)}) collective-permute-start(f32[256,128]{1,0:T(8,128)S(1)} %get-tuple-element.55), channel_id=1, source_target_pairs={{0,4},{1,5},{2,6},{3,7},{4,0},{5,1},{6,2},{7,3},{8,12},{9,13},{10,... | collective-permute-start | bytes 393224 | tf_op jit(solution)/shard_map/ppermute | solution.py:350
  34.2 5.0 %collective-permute-start.16 = (f32[256,128]{1,0:T(8,128)S(1)}, f32[256,128]{1,0:T(8,128)S(1)}, u32[]{:S(2)}, u32[]{:S(2)}) collective-permute-start(f32[256,128]{1,0:T(8,128)S(1)} %get-tuple-element.56), channel_id=1, source_target_pairs={{0,2},{1,3},{2,0},{3,1},{4,6},{5,7},{6,4},{7,5},{8,10},{9,11},{10,... | collective-permute-start | bytes 393224 | tf_op jit(solution)/shard_map/ppermute | solution.py:350
  35.7 3.8 %copy-start.1 = (f32[4096]{0:T(1024)S(1)}, f32[4096]{0:T(1024)}, u32[]{:S(2)}) copy-start(f32[4096]{0:T(1024)} %param.9) | copy-start | bytes 49156
  35.7 3.7 %collective-permute-start.17 = (f32[64,1024]{1,0:T(8,128)S(1)}, f32[64,1024]{1,0:T(8,128)S(1)}, u32[]{:S(2)}, u32[]{:S(2)}) collective-permute-start(f32[64,1024]{1,0:T(8,128)S(1)} %shard_map.68), channel_id=1, source_target_pairs={{0,1},{1,0},{2,3},{3,2},{4,5},{5,4},{6,7},{7,6},{8,9},{9,8},{10,11... | collective-permute-start | bytes 786440 | tf_op jit(solution)/shard_map/ppermute | solution.py:350
  39.4 1.6 %collective-permute-start.18 = (f32[64,1024]{1,0:T(8,128)S(1)}, f32[64,1024]{1,0:T(8,128)S(1)}, u32[]{:S(2)}, u32[]{:S(2)}) collective-permute-start(f32[64,1024]{1,0:T(8,128)S(1)} %shard_map.70), channel_id=1, source_target_pairs={{0,1},{1,0},{2,3},{3,2},{4,5},{5,4},{6,7},{7,6},{8,9},{9,8},{10,11... | collective-permute-start | bytes 786440 | tf_op jit(solution)/shard_map/ppermute | solution.py:350

commit v6 on v5

--- a/solution.py
+++ b/solution.py
@@ -13,7 +13,7 @@
 FRONT = (((0, 1, 2, 3),), ((0, 1, 2, 3),))
 BACK = (((0, 1, 2, 3),), ((0, 1, 2, 3),))
 SPLIT = (1, 1)
-SLOTS = {"start": [(0, (0, 16))], "between1": [(0, (16, 32))], "enter1": [(1, (0, 32))]}
+SLOTS = {'start': [(0, (0, 16))], 'enter1': [(0, (16, 32)), (1, (0, 32))]}
 F32 = jnp.float32
 BF16 = jnp.bfloat16
 HB = pl.BlockSpec(memory_space=pltpu.HBM)
@@ -438,7 +438,7 @@
         *[sibling for group in siblings for sibling in group][:-1])
     attended = pl.pallas_call(
         norm_kernel, out_shape=array((rows, width), BF16), in_specs=[VM] * 5, out_specs=HB,
-        scratch_shapes=[pltpu.VMEM((rows, width), BF16), pltpu.SemaphoreType.DMA((2,))], compiler_params=PARAMS,
+        scratch_shapes=[pltpu.VMEM((rows, width), BF16), pltpu.SemaphoreType.DMA((4,))], compiler_params=PARAMS,
     )(use, gain, mixed, squares, siblings[-1][-1])
     return attended[None]
 

time: 42.1 us -> 41.3 us (0.981)
  waiting for transfers between devices: 11.7 us -> 7.81 us
  starting transfers between devices: 21.1 us -> 24.2 us
    ppermute x17, waiting for transfers between devices: 11.7 us -> 7.73 us  [swap(): return lax.ppermute(what, 'ctx', [(i, i ^ bits) for i in range(count)])]
    ppermute x17, starting transfers between devices: 15.2 us -> 18.3 us  [swap(): return lax.ppermute(what, 'ctx', [(i, i ^ bits) for i in range(count)])]
  transfers between devices with their start and end apart: 19 -> 19, of which waited for: 9 -> 8; matrix products, arithmetic and copies ran while one was open for 0% -> 0% of each run, Pallas kernels for 15% -> 16%
where the time goes in v6:
time: 41.3 us; the launch traced here: 41.1 us
  starting transfers between devices  24.2 us (59%)
  Pallas kernels  8.95 us (22%)
  waiting for transfers between devices  7.81 us (19%)
    ppermute x17, starting transfers between devices, swap(): return lax.ppermute(what, 'ctx', [(i, i ^ bits) for i in range(count)])  18.3 us
    ppermute x17, waiting for transfers between devices, swap(): return lax.ppermute(what, 'ctx', [(i, i ^ bits) for i in range(count)])  7.73 us
    pallas_call x15, Pallas kernels, call(): pl.pallas_call(kernel, out_shape=outs, in_specs=[VM] * len(args), out_spe...  6.45 us
    ppermute x2, starting transfers between devices, later(): lax.ppermute(what, 'ctx', [(i, (i + shift * 2 * CHIPS) % count) for i in...  5.91 us
    pallas_call x1, Pallas kernels, shards(): pl.pallas_call(functools.partial(first_kernel, groups), out_shape=[array(...  1.56 us
    pallas_call x1, Pallas kernels, shards(): pl.pallas_call(norm_kernel, out_shape=array((rows, width), BF16), in_spec...  0.94 us
  transfers between devices with their start and end apart: 19, of which 8 were waited for; matrix products, arithmetic and copies ran while one was open for 0% of the time, Pallas kernels for 16%

profile of v6, /device:TPU:0, one launch (start us, length us, event | category | flops | bytes accessed | tf_op | source)
XLA Modules:
  0.0 41.1 jit_solution(1125706627095257322)
XLA Ops:
  0.0 1.6 %shard_map.55 = (bf16[64,4096]{1,0:T(8,128)(2,1)S(1)}, bf16[64,4096]{1,0:T(8,128)(2,1)S(1)}, f32[32,128]{1,0:T(8,128)S(1)}, bf16[64,128]{1,0:T(8,128)(2,1)S(1)},...) custom-call(s32[1,4]{1,0:T(1,128)} %starts_hbm.1, bf16[64,4096]{1,0:T(8,128)(2,1)} %bitcast.12, ...), custom_call_target="tpu_custom_call" | custom-call | tf_op jit(solution)/shard_map/pallas_call | solution.py:363
  1.6 0.5 %collective-permute-start.1 = (f32[1024,128]{1,0:T(8,128)S(1)}, f32[1024,128]{1,0:T(8,128)S(1)}, u32[]{:S(2)}, u32[]{:S(2)}) collective-permute-start(f32[1024,128]{1,0:T(8,128)S(1)} %get-tuple-element.40), channel_id=1, source_target_pairs={{0,1},{1,0},{2,3},{3,2},{4,5},{5,4},{6,7},{7,6},{8,9},{9,8},{10,11... | collective-permute-start | bytes 1572872 | tf_op jit(solution)/shard_map/ppermute | solution.py:350
  2.6 0.5 %collective-permute-start = (f32[1024,128]{1,0:T(8,128)S(1)}, f32[1024,128]{1,0:T(8,128)S(1)}, u32[]{:S(2)}, u32[]{:S(2)}) collective-permute-start(f32[1024,128]{1,0:T(8,128)S(1)} %get-tuple-element.39), channel_id=1, source_target_pairs={{0,1},{1,0},{2,3},{3,2},{4,5},{5,4},{6,7},{7,6},{8,9},{9,8},{10,11... | collective-permute-start | bytes 1572872 | tf_op jit(solution)/shard_map/ppermute | solution.py:350
  3.2 2.3 %shard_map.57.refs_2_.refs_3_ = f32[64,2048]{1,0:T(8,128)S(1)} custom-call(f32[64,64]{1,0:T(8,128)S(1)} %get-tuple-element.34.allowed_ref, bf16[64,4096]{1,0:T(8,128)(2,1)S(1)} %bitcast.6, bf16[64,4096]{1,0:T(8,128)(2,1)S(1)} %get-tuple-element.35.key_ref, bf16[64,4096]{1,0:T(8,128)(2,1)S(1)} %get-tuple-element.36.value_ref, ...), custom_call_target="tpu_custom_call" | custom-call | tf_op jit(solution)/shard_map/pallas_call | solution.py:338
  5.5 3.6 %collective-permute-start.2 = (f32[256,128]{1,0:T(8,128)S(1)}, f32[256,128]{1,0:T(8,128)S(1)}, u32[]{:S(2)}, u32[]{:S(2)}) collective-permute-start(f32[256,128]{1,0:T(8,128)S(1)} %get-tuple-element.41), channel_id=1, source_target_pairs={{0,6},{1,7},{2,4},{3,5},{4,2},{5,3},{6,0},{7,1},{8,14},{9,15},{10,... | collective-permute-start | bytes 393224 | tf_op jit(solution)/shard_map/ppermute | solution.py:350
  9.1 0.4 %collective-permute-start.8 = (f32[256,128]{1,0:T(8,128)S(1)}, f32[256,128]{1,0:T(8,128)S(1)}, u32[]{:S(2)}, u32[]{:S(2)}) collective-permute-start(f32[256,128]{1,0:T(8,128)S(1)} %get-tuple-element.48), channel_id=1, source_target_pairs={{0,4},{1,5},{2,6},{3,7},{4,0},{5,1},{6,2},{7,3},{8,12},{9,13},{10,... | collective-permute-start | bytes 393224 | tf_op jit(solution)/shard_map/ppermute | solution.py:350
  10.1 2.8 %collective-permute-done.2.refs_2_.refs_1_ = f32[256,128]{1,0:T(8,128)S(1)} collective-permute-done((f32[256,128]{1,0:T(8,128)S(1)}, f32[256,128]{1,0:T(8,128)S(1)}, u32[]{:S(2)}, u32[]{:S(2)}) %collective-permute-start.2) | collective-permute-done | bytes 131104 | tf_op jit(solution)/shard_map/ppermute | solution.py:350
  13.0 2.7 %collective-permute-start.4 = (f32[256,128]{1,0:T(8,128)S(1)}, f32[256,128]{1,0:T(8,128)S(1)}, u32[]{:S(2)}, u32[]{:S(2)}) collective-permute-start(f32[256,128]{1,0:T(8,128)S(1)} %get-tuple-element.43), channel_id=1, source_target_pairs={{0,6},{1,7},{2,4},{3,5},{4,2},{5,3},{6,0},{7,1},{8,14},{9,15},{10,... | collective-permute-start | bytes 393224 | tf_op jit(solution)/shard_map/ppermute | solution.py:350
  15.7 0.5 %collective-permute-start.5 = (f32[256,128]{1,0:T(8,128)S(1)}, f32[256,128]{1,0:T(8,128)S(1)}, u32[]{:S(2)}, u32[]{:S(2)}) collective-permute-start(f32[256,128]{1,0:T(8,128)S(1)} %get-tuple-element.44), channel_id=1, source_target_pairs={{0,4},{1,5},{2,6},{3,7},{4,0},{5,1},{6,2},{7,3},{8,12},{9,13},{10,... | collective-permute-start | bytes 393224 | tf_op jit(solution)/shard_map/ppermute | solution.py:350
  16.6 2.8 %collective-permute-start.10 = (f32[256,128]{1,0:T(8,128)S(1)}, f32[256,128]{1,0:T(8,128)S(1)}, u32[]{:S(2)}, u32[]{:S(2)}) collective-permute-start(f32[256,128]{1,0:T(8,128)S(1)} %shard_map.66), channel_id=1, source_target_pairs={{0,8},{1,9},{2,10},{3,11},{4,12},{5,13},{6,14},{7,15},{8,0},{9,1},... | collective-permute-start | bytes 393224 | tf_op jit(solution)/shard_map/ppermute | solution.py:353
  19.4 0.9 %collective-permute-done.4.refs_1_ = f32[256,128]{1,0:T(8,128)S(1)} collective-permute-done((f32[256,128]{1,0:T(8,128)S(1)}, f32[256,128]{1,0:T(8,128)S(1)}, u32[]{:S(2)}, u32[]{:S(2)}) %collective-permute-start.4) | collective-permute-done | bytes 131104 | tf_op jit(solution)/shard_map/ppermute | solution.py:350
  20.3 2.1 %collective-permute-done.5.refs_2_ = f32[256,128]{1,0:T(8,128)S(1)} collective-permute-done((f32[256,128]{1,0:T(8,128)S(1)}, f32[256,128]{1,0:T(8,128)S(1)}, u32[]{:S(2)}, u32[]{:S(2)}) %collective-permute-start.5) | collective-permute-done | bytes 131104 | tf_op jit(solution)/shard_map/ppermute | solution.py:350
  22.5 3.1 %collective-permute-start.7 = (f32[256,128]{1,0:T(8,128)S(1)}, f32[256,128]{1,0:T(8,128)S(1)}, u32[]{:S(2)}, u32[]{:S(2)}) collective-permute-start(f32[256,128]{1,0:T(8,128)S(1)} %shard_map.62), channel_id=1, source_target_pairs={{0,8},{1,9},{2,10},{3,11},{4,12},{5,13},{6,14},{7,15},{8,0},{9,1},... | collective-permute-start | bytes 393224 | tf_op jit(solution)/shard_map/ppermute | solution.py:353
  25.7 2.7 %collective-permute-start.11 = (f32[256,128]{1,0:T(8,128)S(1)}, f32[256,128]{1,0:T(8,128)S(1)}, u32[]{:S(2)}, u32[]{:S(2)}) collective-permute-start(f32[256,128]{1,0:T(8,128)S(1)} %get-tuple-element.51), channel_id=1, source_target_pairs={{0,6},{1,7},{2,4},{3,5},{4,2},{5,3},{6,0},{7,1},{8,14},{9,15},{10,... | collective-permute-start | bytes 393224 | tf_op jit(solution)/shard_map/ppermute | solution.py:350
  28.4 1.1 %collective-permute-start.12 = (f32[256,128]{1,0:T(8,128)S(1)}, f32[256,128]{1,0:T(8,128)S(1)}, u32[]{:S(2)}, u32[]{:S(2)}) collective-permute-start(f32[256,128]{1,0:T(8,128)S(1)} %get-tuple-element.52), channel_id=1, source_target_pairs={{0,4},{1,5},{2,6},{3,7},{4,0},{5,1},{6,2},{7,3},{8,12},{9,13},{10,... | collective-permute-start | bytes 393224 | tf_op jit(solution)/shard_map/ppermute | solution.py:350
  30.0 2.1 %collective-permute-start.14 = (f32[256,128]{1,0:T(8,128)S(1)}, f32[256,128]{1,0:T(8,128)S(1)}, u32[]{:S(2)}, u32[]{:S(2)}) collective-permute-start(f32[256,128]{1,0:T(8,128)S(1)} %get-tuple-element.54), channel_id=1, source_target_pairs={{0,6},{1,7},{2,4},{3,5},{4,2},{5,3},{6,0},{7,1},{8,14},{9,15},{10,... | collective-permute-start | bytes 393224 | tf_op jit(solution)/shard_map/ppermute | solution.py:350
  32.1 1.1 %collective-permute-start.15 = (f32[256,128]{1,0:T(8,128)S(1)}, f32[256,128]{1,0:T(8,128)S(1)}, u32[]{:S(2)}, u32[]{:S(2)}) collective-permute-start(f32[256,128]{1,0:T(8,128)S(1)} %get-tuple-element.55), channel_id=1, source_target_pairs={{0,4},{1,5},{2,6},{3,7},{4,0},{5,1},{6,2},{7,3},{8,12},{9,13},{10,... | collective-permute-start | bytes 393224 | tf_op jit(solution)/shard_map/ppermute | solution.py:350
  33.2 1.9 %collective-permute-start.16 = (f32[256,128]{1,0:T(8,128)S(1)}, f32[256,128]{1,0:T(8,128)S(1)}, u32[]{:S(2)}, u32[]{:S(2)}) collective-permute-start(f32[256,128]{1,0:T(8,128)S(1)} %get-tuple-element.56), channel_id=1, source_target_pairs={{0,2},{1,3},{2,0},{3,1},{4,6},{5,7},{6,4},{7,5},{8,10},{9,11},{10,... | collective-permute-start | bytes 393224 | tf_op jit(solution)/shard_map/ppermute | solution.py:350
  35.1 2.3 %shard_map.64.refs_6_.refs_4_ = f32[64,2048]{1,0:T(8,128)S(1)} custom-call(f32[64,64]{1,0:T(8,128)S(1)} %get-tuple-element.34.allowed_ref, bf16[64,4096]{1,0:T(8,128)(2,1)S(1)} %bitcast.7, bf16[64,4096]{1,0:T(8,128)(2,1)S(1)} %get-tuple-element.35.key_ref, bf16[64,4096]{1,0:T(8,128)(2,1)S(1)} %get-tuple-element.36.value_ref, ...), custom_call_target="tpu_custom_call" | custom-call | tf_op jit(solution)/shard_map/pallas_call | solution.py:338
  37.8 0.6 %collective-permute-done.16.refs_13_.refs_4_ = f32[256,128]{1,0:T(8,128)S(1)} collective-permute-done((f32[256,128]{1,0:T(8,128)S(1)}, f32[256,128]{1,0:T(8,128)S(1)}, u32[]{:S(2)}, u32[]{:S(2)}) %collective-permute-start.16) | collective-permute-done | bytes 131104 | tf_op jit(solution)/shard_map/ppermute | solution.py:350
  38.6 0.5 %collective-permute-done.17.refs_16_ = f32[64,1024]{1,0:T(8,128)S(1)} collective-permute-done((f32[64,1024]{1,0:T(8,128)S(1)}, f32[64,1024]{1,0:T(8,128)S(1)}, u32[]{:S(2)}, u32[]{:S(2)}) %collective-permute-start.17) | collective-permute-done | bytes 262176 | tf_op jit(solution)/shard_map/ppermute | solution.py:350
  39.2 0.4 shard_map.69
  39.6 0.6 %collective-permute-done.18.sibling_ref = f32[64,1024]{1,0:T(8,128)S(1)} collective-permute-done((f32[64,1024]{1,0:T(8,128)S(1)}, f32[64,1024]{1,0:T(8,128)S(1)}, u32[]{:S(2)}, u32[]{:S(2)}) %collective-permute-start.18) | collective-permute-done | bytes 262176 | tf_op jit(solution)/shard_map/ppermute | solution.py:350
  40.2 0.9 %shard_map.71 = bf16[64,4096]{1,0:T(8,128)(2,1)} custom-call(f32[64,128]{1,0:T(8,128)S(1)} %get-tuple-element.32.refs_0_.use_ref, f32[1,4096]{1,0:T(1,128)S(1)} %bitcast.11, f32[64,4096]{1,0:T(8,128)S(1)} %get-tuple-element.57.mixed_ref, f32[64,128]{1,0:T(8,128)S(1)} %get-tuple-element.58.squares_ref, f32[64,1024]{1,0:T(8,128)S(1)} %collective-permute-done.18.sibling_ref), custom_call_target="tpu_custom_call" | custom-call | tf_op jit(solution)/shard_map/pallas_call | solution.py:439
  (35 shorter events, 2.8 us)
Async XLA Ops:
  0.0 2.1 %copy-start = (bf16[1,64,4096]{2,1,0:T(8,128)(2,1)S(1)}, bf16[1,64,4096]{2,1,0:T(8,128)(2,1)}, u32[]{:S(2)}) copy-start(bf16[1,64,4096]{2,1,0:T(8,128)(2,1)} %param.5) | copy-start | bytes 1572868
  1.6 3.9 %collective-permute-start.1 = (f32[1024,128]{1,0:T(8,128)S(1)}, f32[1024,128]{1,0:T(8,128)S(1)}, u32[]{:S(2)}, u32[]{:S(2)}) collective-permute-start(f32[1024,128]{1,0:T(8,128)S(1)} %get-tuple-element.40), channel_id=1, source_target_pairs={{0,1},{1,0},{2,3},{3,2},{4,5},{5,4},{6,7},{7,6},{8,9},{9,8},{10,11... | collective-permute-start | bytes 1572872 | tf_op jit(solution)/shard_map/ppermute | solution.py:350
  2.2 7.9 %collective-permute-start.3 = (f32[64,2048]{1,0:T(8,128)S(1)}, f32[64,2048]{1,0:T(8,128)S(1)}, u32[]{:S(2)}, u32[]{:S(2)}) collective-permute-start(f32[64,2048]{1,0:T(8,128)S(1)} %shard_map.60), channel_id=1, source_target_pairs={{0,1},{1,0},{2,3},{3,2},{4,5},{5,4},{6,7},{7,6},{8,9},{9,8},{10,11... | collective-permute-start | bytes 1572872 | tf_op jit(solution)/shard_map/ppermute | solution.py:350
  2.6 7.4 %collective-permute-start = (f32[1024,128]{1,0:T(8,128)S(1)}, f32[1024,128]{1,0:T(8,128)S(1)}, u32[]{:S(2)}, u32[]{:S(2)}) collective-permute-start(f32[1024,128]{1,0:T(8,128)S(1)} %get-tuple-element.39), channel_id=1, source_target_pairs={{0,1},{1,0},{2,3},{3,2},{4,5},{5,4},{6,7},{7,6},{8,9},{9,8},{10,11... | collective-permute-start | bytes 1572872 | tf_op jit(solution)/shard_map/ppermute | solution.py:350
  5.5 7.4 %collective-permute-start.2 = (f32[256,128]{1,0:T(8,128)S(1)}, f32[256,128]{1,0:T(8,128)S(1)}, u32[]{:S(2)}, u32[]{:S(2)}) collective-permute-start(f32[256,128]{1,0:T(8,128)S(1)} %get-tuple-element.41), channel_id=1, source_target_pairs={{0,6},{1,7},{2,4},{3,5},{4,2},{5,3},{6,0},{7,1},{8,14},{9,15},{10,... | collective-permute-start | bytes 393224 | tf_op jit(solution)/shard_map/ppermute | solution.py:350
  9.1 7.4 %collective-permute-start.8 = (f32[256,128]{1,0:T(8,128)S(1)}, f32[256,128]{1,0:T(8,128)S(1)}, u32[]{:S(2)}, u32[]{:S(2)}) collective-permute-start(f32[256,128]{1,0:T(8,128)S(1)} %get-tuple-element.48), channel_id=1, source_target_pairs={{0,4},{1,5},{2,6},{3,7},{4,0},{5,1},{6,2},{7,3},{8,12},{9,13},{10,... | collective-permute-start | bytes 393224 | tf_op jit(solution)/shard_map/ppermute | solution.py:350
  9.6 7.0 %collective-permute-start.9 = (f32[256,128]{1,0:T(8,128)S(1)}, f32[256,128]{1,0:T(8,128)S(1)}, u32[]{:S(2)}, u32[]{:S(2)}) collective-permute-start(f32[256,128]{1,0:T(8,128)S(1)} %get-tuple-element.49), channel_id=1, source_target_pairs={{0,2},{1,3},{2,0},{3,1},{4,6},{5,7},{6,4},{7,5},{8,10},{9,11},{10,... | collective-permute-start | bytes 393224 | tf_op jit(solution)/shard_map/ppermute | solution.py:350
  13.0 7.3 %collective-permute-start.4 = (f32[256,128]{1,0:T(8,128)S(1)}, f32[256,128]{1,0:T(8,128)S(1)}, u32[]{:S(2)}, u32[]{:S(2)}) collective-permute-start(f32[256,128]{1,0:T(8,128)S(1)} %get-tuple-element.43), channel_id=1, source_target_pairs={{0,6},{1,7},{2,4},{3,5},{4,2},{5,3},{6,0},{7,1},{8,14},{9,15},{10,... | collective-permute-start | bytes 393224 | tf_op jit(solution)/shard_map/ppermute | solution.py:350
  15.7 6.7 %collective-permute-start.5 = (f32[256,128]{1,0:T(8,128)S(1)}, f32[256,128]{1,0:T(8,128)S(1)}, u32[]{:S(2)}, u32[]{:S(2)}) collective-permute-start(f32[256,128]{1,0:T(8,128)S(1)} %get-tuple-element.44), channel_id=1, source_target_pairs={{0,4},{1,5},{2,6},{3,7},{4,0},{5,1},{6,2},{7,3},{8,12},{9,13},{10,... | collective-permute-start | bytes 393224 | tf_op jit(solution)/shard_map/ppermute | solution.py:350
  16.2 6.2 %collective-permute-start.6 = (f32[256,128]{1,0:T(8,128)S(1)}, f32[256,128]{1,0:T(8,128)S(1)}, u32[]{:S(2)}, u32[]{:S(2)}) collective-permute-start(f32[256,128]{1,0:T(8,128)S(1)} %get-tuple-element.45), channel_id=1, source_target_pairs={{0,2},{1,3},{2,0},{3,1},{4,6},{5,7},{6,4},{7,5},{8,10},{9,11},{10,... | collective-permute-start | bytes 393224 | tf_op jit(solution)/shard_map/ppermute | solution.py:350
  16.6 9.0 %collective-permute-start.10 = (f32[256,128]{1,0:T(8,128)S(1)}, f32[256,128]{1,0:T(8,128)S(1)}, u32[]{:S(2)}, u32[]{:S(2)}) collective-permute-start(f32[256,128]{1,0:T(8,128)S(1)} %shard_map.66), channel_id=1, source_target_pairs={{0,8},{1,9},{2,10},{3,11},{4,12},{5,13},{6,14},{7,15},{8,0},{9,1},... | collective-permute-start | bytes 393224 | tf_op jit(solution)/shard_map/ppermute | solution.py:353
  22.5 7.4 %collective-permute-start.7 = (f32[256,128]{1,0:T(8,128)S(1)}, f32[256,128]{1,0:T(8,128)S(1)}, u32[]{:S(2)}, u32[]{:S(2)}) collective-permute-start(f32[256,128]{1,0:T(8,128)S(1)} %shard_map.62), channel_id=1, source_target_pairs={{0,8},{1,9},{2,10},{3,11},{4,12},{5,13},{6,14},{7,15},{8,0},{9,1},... | collective-permute-start | bytes 393224 | tf_op jit(solution)/shard_map/ppermute | solution.py:353
  25.7 7.5 %collective-permute-start.11 = (f32[256,128]{1,0:T(8,128)S(1)}, f32[256,128]{1,0:T(8,128)S(1)}, u32[]{:S(2)}, u32[]{:S(2)}) collective-permute-start(f32[256,128]{1,0:T(8,128)S(1)} %get-tuple-element.51), channel_id=1, source_target_pairs={{0,6},{1,7},{2,4},{3,5},{4,2},{5,3},{6,0},{7,1},{8,14},{9,15},{10,... | collective-permute-start | bytes 393224 | tf_op jit(solution)/shard_map/ppermute | solution.py:350
  28.4 8.9 %collective-permute-start.12 = (f32[256,128]{1,0:T(8,128)S(1)}, f32[256,128]{1,0:T(8,128)S(1)}, u32[]{:S(2)}, u32[]{:S(2)}) collective-permute-start(f32[256,128]{1,0:T(8,128)S(1)} %get-tuple-element.52), channel_id=1, source_target_pairs={{0,4},{1,5},{2,6},{3,7},{4,0},{5,1},{6,2},{7,3},{8,12},{9,13},{10,... | collective-permute-start | bytes 393224 | tf_op jit(solution)/shard_map/ppermute | solution.py:350
  29.5 7.8 %collective-permute-start.13 = (f32[256,128]{1,0:T(8,128)S(1)}, f32[256,128]{1,0:T(8,128)S(1)}, u32[]{:S(2)}, u32[]{:S(2)}) collective-permute-start(f32[256,128]{1,0:T(8,128)S(1)} %get-tuple-element.53), channel_id=1, source_target_pairs={{0,2},{1,3},{2,0},{3,1},{4,6},{5,7},{6,4},{7,5},{8,10},{9,11},{10,... | collective-permute-start | bytes 393224 | tf_op jit(solution)/shard_map/ppermute | solution.py:350
  30.0 7.7 %collective-permute-start.14 = (f32[256,128]{1,0:T(8,128)S(1)}, f32[256,128]{1,0:T(8,128)S(1)}, u32[]{:S(2)}, u32[]{:S(2)}) collective-permute-start(f32[256,128]{1,0:T(8,128)S(1)} %get-tuple-element.54), channel_id=1, source_target_pairs={{0,6},{1,7},{2,4},{3,5},{4,2},{5,3},{6,0},{7,1},{8,14},{9,15},{10,... | collective-permute-start | bytes 393224 | tf_op jit(solution)/shard_map/ppermute | solution.py:350
  32.1 5.7 %collective-permute-start.15 = (f32[256,128]{1,0:T(8,128)S(1)}, f32[256,128]{1,0:T(8,128)S(1)}, u32[]{:S(2)}, u32[]{:S(2)}) collective-permute-start(f32[256,128]{1,0:T(8,128)S(1)} %get-tuple-element.55), channel_id=1, source_target_pairs={{0,4},{1,5},{2,6},{3,7},{4,0},{5,1},{6,2},{7,3},{8,12},{9,13},{10,... | collective-permute-start | bytes 393224 | tf_op jit(solution)/shard_map/ppermute | solution.py:350
  33.2 5.2 %collective-permute-start.16 = (f32[256,128]{1,0:T(8,128)S(1)}, f32[256,128]{1,0:T(8,128)S(1)}, u32[]{:S(2)}, u32[]{:S(2)}) collective-permute-start(f32[256,128]{1,0:T(8,128)S(1)} %get-tuple-element.56), channel_id=1, source_target_pairs={{0,2},{1,3},{2,0},{3,1},{4,6},{5,7},{6,4},{7,5},{8,10},{9,11},{10,... | collective-permute-start | bytes 393224 | tf_op jit(solution)/shard_map/ppermute | solution.py:350
  37.5 1.6 %copy-start.1 = (f32[4096]{0:T(1024)S(1)}, f32[4096]{0:T(1024)}, u32[]{:S(2)}) copy-start(f32[4096]{0:T(1024)} %param.9) | copy-start | bytes 49156
  37.6 1.6 %collective-permute-start.17 = (f32[64,1024]{1,0:T(8,128)S(1)}, f32[64,1024]{1,0:T(8,128)S(1)}, u32[]{:S(2)}, u32[]{:S(2)}) collective-permute-start(f32[64,1024]{1,0:T(8,128)S(1)} %shard_map.68), channel_id=1, source_target_pairs={{0,1},{1,0},{2,3},{3,2},{4,5},{5,4},{6,7},{7,6},{8,9},{9,8},{10,11... | collective-permute-start | bytes 786440 | tf_op jit(solution)/shard_map/ppermute | solution.py:350
  38.6 1.6 %collective-permute-start.18 = (f32[64,1024]{1,0:T(8,128)S(1)}, f32[64,1024]{1,0:T(8,128)S(1)}, u32[]{:S(2)}, u32[]{:S(2)}) collective-permute-start(f32[64,1024]{1,0:T(8,128)S(1)} %shard_map.70), channel_id=1, source_target_pairs={{0,1},{1,0},{2,3},{3,2},{4,5},{5,4},{6,7},{7,6},{8,9},{9,8},{10,11... | collective-permute-start | bytes 786440 | tf_op jit(solution)/shard_map/ppermute | solution.py:350

commit v7 on v6

--- a/solution.py
+++ b/solution.py
@@ -13,7 +13,7 @@
 FRONT = (((0, 1, 2, 3),), ((0, 1, 2, 3),))
 BACK = (((0, 1, 2, 3),), ((0, 1, 2, 3),))
 SPLIT = (1, 1)
-SLOTS = {'start': [(0, (0, 16))], 'enter1': [(0, (16, 32)), (1, (0, 32))]}
+SLOTS = {'start': [(0, (0, 12))], 'enter1': [(0, (12, 32)), (1, (0, 32))]}
 F32 = jnp.float32
 BF16 = jnp.bfloat16
 HB = pl.BlockSpec(memory_space=pltpu.HBM)
@@ -125,22 +125,28 @@
             key_ref[:, at] * kept, value_ref[:, at], (((0,), (0,)), ((), ())), preferred_element_type=F32)
 
 
-def first_kernel(groups, starts_hbm, key_hbm, value_hbm, key_ref, value_ref, table_ref, kept_ref, allowed_ref, use_ref, *refs):
-    *sends, starts, sems = refs
-    copies = [
-        pltpu.make_async_copy(source, target, sems.at[i])
-        for i, (source, target) in enumerate(((starts_hbm, starts), (key_hbm, key_ref), (value_hbm, value_ref)))
-    ]
+def first_kernel(groups, starts_hbm, key_hbm, value_hbm, table_ref, kept_ref, allowed_ref, use_ref, send_ref, starts,
+                 key_ref, value_ref, sems):
+    core, chip, _, block = place()
+    rows, width = key_hbm.shape
+    copies = [pltpu.make_async_copy(starts_hbm, starts, sems.at[0])]
+    todo = part_steps(width, 0)
+    size = sizes(width)[0]
+    for i, step in enumerate(todo[::size]):
+        at = pl.ds(column(width, core, chip, False, *step).start, size * HD)
+        to = slice(i * size * HD, (i + 1) * size * HD)
+        for source, target in ((key_hbm, key_ref), (value_hbm, value_ref)):
+            copies.append(pltpu.make_async_copy(source.at[:, at], target.at[:, to], sems.at[len(copies)]))
     for copy in copies:
         copy.start()
     copies[0].wait()
-    rows = key_ref.shape[0]
-    begin = place()[3] * rows
+    begin = block * rows
     names = table_rows(groups)
     for name, weight in weights(starts, rows, groups).items():
         table_ref[names[name]:names[name] + 1, :] = jnp.full((1, HD), weight, F32)
     segments = segment_rows(starts, begin + lax.broadcasted_iota(jnp.int32, (rows, HD), 0))
-    kept_ref[...] = (segments == segment_at(starts, begin + rows - 1)).astype(F32).astype(BF16)
+    kept = (segments == segment_at(starts, begin + rows - 1)).astype(F32).astype(BF16)
+    kept_ref[...] = kept
     use_ref[...] = (segments == segment_at(starts, begin - 1)).astype(F32)
     late = begin + lax.broadcasted_iota(jnp.int32, (rows, rows), 0)
     early = begin + lax.broadcasted_iota(jnp.int32, (rows, rows), 1)
@@ -148,8 +154,9 @@
     allowed_ref[...] = allowed.astype(F32)
     for copy in copies[1:]:
         copy.wait()
-    for spots, send_ref in zip(FRONT[0], sends):
-        summarize(kept_ref, key_ref, value_ref, False, 0, spots, send_ref)
+    for i in range(len(todo)):
+        send_ref[tile(i), :] = lax.dot_general(
+            key_ref[:, tile(i)] * kept, value_ref[:, tile(i)], (((0,), (0,)), ((), ())), preferred_element_type=F32)
 
 
 def summary_kernel(what, kept_ref, key_ref, value_ref, *refs):
@@ -360,13 +367,15 @@
         outs = [tall(*step[1:]) for step in what]
         return call(functools.partial(summary_kernel, what), outs, kept, key, value, *after)
 
-    key, value, table, kept, allowed, use, *sends = pl.pallas_call(
+    some = pltpu.VMEM((rows, sizes(width)[0] * CHIPS * HD), BF16)
+    table, kept, allowed, use, *sends = pl.pallas_call(
         functools.partial(first_kernel, groups),
-        out_shape=[array((rows, width), BF16)] * 2 + [
+        out_shape=[
             array((-(-len(table_rows(groups)) // 8) * 8, HD)), array((rows, HD), BF16), array((rows, rows)),
-            array((rows, HD))] + [tall(0, spots) for spots in FRONT[0]],
-        in_specs=[HB] * 3, out_specs=[VM] * (6 + len(FRONT[0])),
-        scratch_shapes=[pltpu.SMEM(seg_starts.shape, jnp.int32), pltpu.SemaphoreType.DMA((3,))],
+            array((rows, HD)), tall(0, range(CHIPS))],
+        in_specs=[HB] * 3, out_specs=[VM] * 5,
+        scratch_shapes=[
+            pltpu.SMEM(seg_starts.shape, jnp.int32), some, some, pltpu.SemaphoreType.DMA((1 + 2 * CHIPS,))],
         compiler_params=PARAMS,
     )(in_hbm(seg_starts), in_hbm(key), in_hbm(value))
     gots, keeps = [], []

time: 41.3 us -> 41.1 us (level)
  waiting for transfers between devices: 7.81 us -> 6.07 us
  local copies, waits for them, and re-layouts: 0.01 us -> 1 us
  starting transfers between devices: 24.2 us -> 25.1 us
    ppermute x17, waiting for transfers between devices: 7.73 us -> 5.89 us  [swap(): return lax.ppermute(what, 'ctx', [(i, i ^ bits) for i in range(count)])]
    unnamed x4 -> x8, local copies, waits for them, and re-layouts: 0.01 us -> 1 us
    ppermute x17, starting transfers between devices: 18.3 us -> 19 us  [swap(): return lax.ppermute(what, 'ctx', [(i, i ^ bits) for i in range(count)])]
  transfers between devices with their start and end apart: 19 -> 19, of which waited for: 8 -> 7; matrix products, arithmetic and copies ran while one was open for 0% -> 0% of each run, Pallas kernels for 16% -> 16%
where the time goes in v7:
time: 41.1 us; the launch traced here: 41 us
  starting transfers between devices  25.1 us (61%)
  Pallas kernels  8.69 us (21%)
  waiting for transfers between devices  6.07 us (15%)
  local copies, waits for them, and re-layouts  1 us (2%)
    ppermute x17, starting transfers between devices, swap(): return lax.ppermute(what, 'ctx', [(i, i ^ bits) for i in range(count)])  19 us
    pallas_call x15, Pallas kernels, call(): pl.pallas_call(kernel, out_shape=outs, in_specs=[VM] * len(args), out_spe...  6.45 us
    ppermute x2, starting transfers between devices, later(): lax.ppermute(what, 'ctx', [(i, (i + shift * 2 * CHIPS) % count) for i in...  6.03 us
    ppermute x17, waiting for transfers between devices, swap(): return lax.ppermute(what, 'ctx', [(i, i ^ bits) for i in range(count)])  5.89 us
    pallas_call x1, Pallas kernels, shards(): pl.pallas_call(functools.partial(first_kernel, groups), out_shape=[array(...  1.29 us
    unnamed x8, local copies, waits for them, and re-layouts  1 us
    pallas_call x1, Pallas kernels, shards(): pl.pallas_call(norm_kernel, out_shape=array((rows, width), BF16), in_spec...  0.95 us
  transfers between devices with their start and end apart: 19, of which 7 were waited for; matrix products, arithmetic and copies ran while one was open for 0% of the time, Pallas kernels for 16%

profile of v7, /device:TPU:0, one launch (start us, length us, event | category | flops | bytes accessed | tf_op | source)
XLA Modules:
  0.0 41.0 jit_solution(8080802636260268494)
XLA Ops:
  0.0 1.3 %shard_map.55 = (f32[32,128]{1,0:T(8,128)S(1)}, bf16[64,128]{1,0:T(8,128)(2,1)S(1)}, f32[64,64]{1,0:T(8,128)S(1)}, f32[64,128]{1,0:T(8,128)S(1)}, f32[1024,128]{1,0:T(8,128)S(1)}) custom-call(s32[1,4]{1,0:T(1,128)} %starts_hbm.1, bf16[64,4096]{1,0:T(8,128)(2,1)} %bitcast.5, bf16[64,4096]{1,0:T(8,128)(2,1)} %bitcast.11), custom_call_target="tpu_custom_call" | custom-call | tf_op jit(solution)/shard_map/pallas_call | solution.py:371
  1.3 0.5 %collective-permute-start.1 = (f32[1024,128]{1,0:T(8,128)S(1)}, f32[1024,128]{1,0:T(8,128)S(1)}, u32[]{:S(2)}, u32[]{:S(2)}) collective-permute-start(f32[1024,128]{1,0:T(8,128)S(1)} %get-tuple-element.36), channel_id=1, source_target_pairs={{0,1},{1,0},{2,3},{3,2},{4,5},{5,4},{6,7},{7,6},{8,9},{9,8},{10,11... | collective-permute-start | bytes 1572872 | tf_op jit(solution)/shard_map/ppermute | solution.py:357
  2.0 0.8 %copy-done = bf16[1,64,4096]{2,1,0:T(8,128)(2,1)S(1)} copy-done((bf16[1,64,4096]{2,1,0:T(8,128)(2,1)S(1)}, bf16[1,64,4096]{2,1,0:T(8,128)(2,1)}, u32[]{:S(2)}) %copy-start) | copy-done | bytes 524312
  3.5 1.7 %shard_map.57.refs_2_.refs_3_ = f32[64,1536]{1,0:T(8,128)S(1)} custom-call(f32[64,64]{1,0:T(8,128)S(1)} %get-tuple-element.32.allowed_ref, bf16[64,4096]{1,0:T(8,128)(2,1)S(1)} %bitcast.18, bf16[64,4096]{1,0:T(8,128)(2,1)S(1)} %bitcast.7, bf16[64,4096]{1,0:T(8,128)(2,1)S(1)} %bitcast.13, f32[1024,128]{1,0:T(8,128)S(1)} %get-tuple-element.34.refs_0_), custom_call_target="tpu_custom_call" | custom-call | tf_op jit(solution)/shard_map/pallas_call | solution.py:345
  5.3 4.0 %collective-permute-start.2 = (f32[256,128]{1,0:T(8,128)S(1)}, f32[256,128]{1,0:T(8,128)S(1)}, u32[]{:S(2)}, u32[]{:S(2)}) collective-permute-start(f32[256,128]{1,0:T(8,128)S(1)} %get-tuple-element.37), channel_id=1, source_target_pairs={{0,6},{1,7},{2,4},{3,5},{4,2},{5,3},{6,0},{7,1},{8,14},{9,15},{10,... | collective-permute-start | bytes 393224 | tf_op jit(solution)/shard_map/ppermute | solution.py:357
  9.3 0.5 %collective-permute-start.8 = (f32[256,128]{1,0:T(8,128)S(1)}, f32[256,128]{1,0:T(8,128)S(1)}, u32[]{:S(2)}, u32[]{:S(2)}) collective-permute-start(f32[256,128]{1,0:T(8,128)S(1)} %get-tuple-element.44), channel_id=1, source_target_pairs={{0,4},{1,5},{2,6},{3,7},{4,0},{5,1},{6,2},{7,3},{8,12},{9,13},{10,... | collective-permute-start | bytes 393224 | tf_op jit(solution)/shard_map/ppermute | solution.py:357
  10.3 2.5 %collective-permute-done.2.refs_2_.refs_1_ = f32[256,128]{1,0:T(8,128)S(1)} collective-permute-done((f32[256,128]{1,0:T(8,128)S(1)}, f32[256,128]{1,0:T(8,128)S(1)}, u32[]{:S(2)}, u32[]{:S(2)}) %collective-permute-start.2) | collective-permute-done | bytes 131104 | tf_op jit(solution)/shard_map/ppermute | solution.py:357
  12.8 2.7 %collective-permute-start.4 = (f32[256,128]{1,0:T(8,128)S(1)}, f32[256,128]{1,0:T(8,128)S(1)}, u32[]{:S(2)}, u32[]{:S(2)}) collective-permute-start(f32[256,128]{1,0:T(8,128)S(1)} %get-tuple-element.39), channel_id=1, source_target_pairs={{0,6},{1,7},{2,4},{3,5},{4,2},{5,3},{6,0},{7,1},{8,14},{9,15},{10,... | collective-permute-start | bytes 393224 | tf_op jit(solution)/shard_map/ppermute | solution.py:357
  15.5 0.5 %collective-permute-start.5 = (f32[256,128]{1,0:T(8,128)S(1)}, f32[256,128]{1,0:T(8,128)S(1)}, u32[]{:S(2)}, u32[]{:S(2)}) collective-permute-start(f32[256,128]{1,0:T(8,128)S(1)} %get-tuple-element.40), channel_id=1, source_target_pairs={{0,4},{1,5},{2,6},{3,7},{4,0},{5,1},{6,2},{7,3},{8,12},{9,13},{10,... | collective-permute-start | bytes 393224 | tf_op jit(solution)/shard_map/ppermute | solution.py:357
  16.0 0.4 collective-permute-start.6
  16.7 2.6 %collective-permute-start.10 = (f32[256,128]{1,0:T(8,128)S(1)}, f32[256,128]{1,0:T(8,128)S(1)}, u32[]{:S(2)}, u32[]{:S(2)}) collective-permute-start(f32[256,128]{1,0:T(8,128)S(1)} %shard_map.66), channel_id=1, source_target_pairs={{0,8},{1,9},{2,10},{3,11},{4,12},{5,13},{6,14},{7,15},{8,0},{9,1},... | collective-permute-start | bytes 393224 | tf_op jit(solution)/shard_map/ppermute | solution.py:360
  19.3 0.9 %collective-permute-done.4.refs_1_ = f32[256,128]{1,0:T(8,128)S(1)} collective-permute-done((f32[256,128]{1,0:T(8,128)S(1)}, f32[256,128]{1,0:T(8,128)S(1)}, u32[]{:S(2)}, u32[]{:S(2)}) %collective-permute-start.4) | collective-permute-done | bytes 131104 | tf_op jit(solution)/shard_map/ppermute | solution.py:357
  20.1 1.4 %collective-permute-done.5.refs_2_ = f32[256,128]{1,0:T(8,128)S(1)} collective-permute-done((f32[256,128]{1,0:T(8,128)S(1)}, f32[256,128]{1,0:T(8,128)S(1)}, u32[]{:S(2)}, u32[]{:S(2)}) %collective-permute-start.5) | collective-permute-done | bytes 131104 | tf_op jit(solution)/shard_map/ppermute | solution.py:357
  21.6 3.4 %collective-permute-start.7 = (f32[256,128]{1,0:T(8,128)S(1)}, f32[256,128]{1,0:T(8,128)S(1)}, u32[]{:S(2)}, u32[]{:S(2)}) collective-permute-start(f32[256,128]{1,0:T(8,128)S(1)} %shard_map.62), channel_id=1, source_target_pairs={{0,8},{1,9},{2,10},{3,11},{4,12},{5,13},{6,14},{7,15},{8,0},{9,1},... | collective-permute-start | bytes 393224 | tf_op jit(solution)/shard_map/ppermute | solution.py:360
  25.1 3.1 %collective-permute-start.11 = (f32[256,128]{1,0:T(8,128)S(1)}, f32[256,128]{1,0:T(8,128)S(1)}, u32[]{:S(2)}, u32[]{:S(2)}) collective-permute-start(f32[256,128]{1,0:T(8,128)S(1)} %get-tuple-element.47), channel_id=1, source_target_pairs={{0,6},{1,7},{2,4},{3,5},{4,2},{5,3},{6,0},{7,1},{8,14},{9,15},{10,... | collective-permute-start | bytes 393224 | tf_op jit(solution)/shard_map/ppermute | solution.py:357
  28.2 1.2 %collective-permute-start.12 = (f32[256,128]{1,0:T(8,128)S(1)}, f32[256,128]{1,0:T(8,128)S(1)}, u32[]{:S(2)}, u32[]{:S(2)}) collective-permute-start(f32[256,128]{1,0:T(8,128)S(1)} %get-tuple-element.48), channel_id=1, source_target_pairs={{0,4},{1,5},{2,6},{3,7},{4,0},{5,1},{6,2},{7,3},{8,12},{9,13},{10,... | collective-permute-start | bytes 393224 | tf_op jit(solution)/shard_map/ppermute | solution.py:357
  29.7 2.2 %collective-permute-start.14 = (f32[256,128]{1,0:T(8,128)S(1)}, f32[256,128]{1,0:T(8,128)S(1)}, u32[]{:S(2)}, u32[]{:S(2)}) collective-permute-start(f32[256,128]{1,0:T(8,128)S(1)} %get-tuple-element.50), channel_id=1, source_target_pairs={{0,6},{1,7},{2,4},{3,5},{4,2},{5,3},{6,0},{7,1},{8,14},{9,15},{10,... | collective-permute-start | bytes 393224 | tf_op jit(solution)/shard_map/ppermute | solution.py:357
  31.9 1.2 %collective-permute-start.15 = (f32[256,128]{1,0:T(8,128)S(1)}, f32[256,128]{1,0:T(8,128)S(1)}, u32[]{:S(2)}, u32[]{:S(2)}) collective-permute-start(f32[256,128]{1,0:T(8,128)S(1)} %get-tuple-element.51), channel_id=1, source_target_pairs={{0,4},{1,5},{2,6},{3,7},{4,0},{5,1},{6,2},{7,3},{8,12},{9,13},{10,... | collective-permute-start | bytes 393224 | tf_op jit(solution)/shard_map/ppermute | solution.py:357
  33.1 1.9 %collective-permute-start.16 = (f32[256,128]{1,0:T(8,128)S(1)}, f32[256,128]{1,0:T(8,128)S(1)}, u32[]{:S(2)}, u32[]{:S(2)}) collective-permute-start(f32[256,128]{1,0:T(8,128)S(1)} %get-tuple-element.52), channel_id=1, source_target_pairs={{0,2},{1,3},{2,0},{3,1},{4,6},{5,7},{6,4},{7,5},{8,10},{9,11},{10,... | collective-permute-start | bytes 393224 | tf_op jit(solution)/shard_map/ppermute | solution.py:357
  35.0 2.8 %shard_map.64.refs_6_.refs_4_ = f32[64,2560]{1,0:T(8,128)S(1)} custom-call(f32[64,64]{1,0:T(8,128)S(1)} %get-tuple-element.32.allowed_ref, bf16[64,4096]{1,0:T(8,128)(2,1)S(1)} %bitcast.19, bf16[64,4096]{1,0:T(8,128)(2,1)S(1)} %bitcast.9, bf16[64,4096]{1,0:T(8,128)(2,1)S(1)} %bitcast.15, f32[256,128]{1,0:T(8,128)S(1)} %get-tuple-element.42.refs_0_.refs_10_.refs_1_), custom_call_target="tpu_custom_call" | custom-call | tf_op jit(solution)/shard_map/pallas_call | solution.py:345
  38.4 0.4 %collective-permute-start.18 = (f32[64,1024]{1,0:T(8,128)S(1)}, f32[64,1024]{1,0:T(8,128)S(1)}, u32[]{:S(2)}, u32[]{:S(2)}) collective-permute-start(f32[64,1024]{1,0:T(8,128)S(1)} %shard_map.70), channel_id=1, source_target_pairs={{0,1},{1,0},{2,3},{3,2},{4,5},{5,4},{6,7},{7,6},{8,9},{9,8},{10,11... | collective-permute-start | bytes 786440 | tf_op jit(solution)/shard_map/ppermute | solution.py:357
  38.8 0.7 %collective-permute-done.17.refs_16_ = f32[64,1024]{1,0:T(8,128)S(1)} collective-permute-done((f32[64,1024]{1,0:T(8,128)S(1)}, f32[64,1024]{1,0:T(8,128)S(1)}, u32[]{:S(2)}, u32[]{:S(2)}) %collective-permute-start.17) | collective-permute-done | bytes 262176 | tf_op jit(solution)/shard_map/ppermute | solution.py:357
  39.6 0.4 shard_map.69
  40.0 0.9 %shard_map.71 = bf16[64,4096]{1,0:T(8,128)(2,1)} custom-call(f32[64,128]{1,0:T(8,128)S(1)} %get-tuple-element.30.refs_0_.use_ref, f32[1,4096]{1,0:T(1,128)S(1)} %bitcast.23, f32[64,4096]{1,0:T(8,128)S(1)} %get-tuple-element.53.mixed_ref, f32[64,128]{1,0:T(8,128)S(1)} %get-tuple-element.54.squares_ref, f32[64,1024]{1,0:T(8,128)S(1)} %collective-permute-done.18.sibling_ref), custom_call_target="tpu_custom_call" | custom-call | tf_op jit(solution)/shard_map/pallas_call | solution.py:448
  (39 shorter events, 2.8 us)
Async XLA Ops:
  0.0 1.8 %copy-start.2 = (bf16[1,64,4096]{2,1,0:T(8,128)(2,1)S(1)}, bf16[1,64,4096]{2,1,0:T(8,128)(2,1)}, u32[]{:S(2)}) copy-start(bf16[1,64,4096]{2,1,0:T(8,128)(2,1)} %param.5) | copy-start | bytes 1572868
  1.3 3.9 %collective-permute-start.1 = (f32[1024,128]{1,0:T(8,128)S(1)}, f32[1024,128]{1,0:T(8,128)S(1)}, u32[]{:S(2)}, u32[]{:S(2)}) collective-permute-start(f32[1024,128]{1,0:T(8,128)S(1)} %get-tuple-element.36), channel_id=1, source_target_pairs={{0,1},{1,0},{2,3},{3,2},{4,5},{5,4},{6,7},{7,6},{8,9},{9,8},{10,11... | collective-permute-start | bytes 1572872 | tf_op jit(solution)/shard_map/ppermute | solution.py:357
  1.8 1.0 %copy-start = (bf16[1,64,4096]{2,1,0:T(8,128)(2,1)S(1)}, bf16[1,64,4096]{2,1,0:T(8,128)(2,1)}, u32[]{:S(2)}) copy-start(bf16[1,64,4096]{2,1,0:T(8,128)(2,1)} %param.6) | copy-start | bytes 1572868
  1.8 1.2 %copy-start.1 = (bf16[1,64,4096]{2,1,0:T(8,128)(2,1)S(1)}, bf16[1,64,4096]{2,1,0:T(8,128)(2,1)}, u32[]{:S(2)}) copy-start(bf16[1,64,4096]{2,1,0:T(8,128)(2,1)} %param.7) | copy-start | bytes 1572868
  1.9 8.4 %collective-permute-start.3 = (f32[64,2048]{1,0:T(8,128)S(1)}, f32[64,2048]{1,0:T(8,128)S(1)}, u32[]{:S(2)}, u32[]{:S(2)}) collective-permute-start(f32[64,2048]{1,0:T(8,128)S(1)} %shard_map.60), channel_id=1, source_target_pairs={{0,1},{1,0},{2,3},{3,2},{4,5},{5,4},{6,7},{7,6},{8,9},{9,8},{10,11... | collective-permute-start | bytes 1572872 | tf_op jit(solution)/shard_map/ppermute | solution.py:357
  3.4 6.9 %collective-permute-start = (f32[1024,128]{1,0:T(8,128)S(1)}, f32[1024,128]{1,0:T(8,128)S(1)}, u32[]{:S(2)}, u32[]{:S(2)}) collective-permute-start(f32[1024,128]{1,0:T(8,128)S(1)} %get-tuple-element.35), channel_id=1, source_target_pairs={{0,1},{1,0},{2,3},{3,2},{4,5},{5,4},{6,7},{7,6},{8,9},{9,8},{10,11... | collective-permute-start | bytes 1572872 | tf_op jit(solution)/shard_map/ppermute | solution.py:357
  5.3 7.5 %collective-permute-start.2 = (f32[256,128]{1,0:T(8,128)S(1)}, f32[256,128]{1,0:T(8,128)S(1)}, u32[]{:S(2)}, u32[]{:S(2)}) collective-permute-start(f32[256,128]{1,0:T(8,128)S(1)} %get-tuple-element.37), channel_id=1, source_target_pairs={{0,6},{1,7},{2,4},{3,5},{4,2},{5,3},{6,0},{7,1},{8,14},{9,15},{10,... | collective-permute-start | bytes 393224 | tf_op jit(solution)/shard_map/ppermute | solution.py:357
  9.3 7.1 %collective-permute-start.8 = (f32[256,128]{1,0:T(8,128)S(1)}, f32[256,128]{1,0:T(8,128)S(1)}, u32[]{:S(2)}, u32[]{:S(2)}) collective-permute-start(f32[256,128]{1,0:T(8,128)S(1)} %get-tuple-element.44), channel_id=1, source_target_pairs={{0,4},{1,5},{2,6},{3,7},{4,0},{5,1},{6,2},{7,3},{8,12},{9,13},{10,... | collective-permute-start | bytes 393224 | tf_op jit(solution)/shard_map/ppermute | solution.py:357
  9.8 6.8 %collective-permute-start.9 = (f32[256,128]{1,0:T(8,128)S(1)}, f32[256,128]{1,0:T(8,128)S(1)}, u32[]{:S(2)}, u32[]{:S(2)}) collective-permute-start(f32[256,128]{1,0:T(8,128)S(1)} %get-tuple-element.45), channel_id=1, source_target_pairs={{0,2},{1,3},{2,0},{3,1},{4,6},{5,7},{6,4},{7,5},{8,10},{9,11},{10,... | collective-permute-start | bytes 393224 | tf_op jit(solution)/shard_map/ppermute | solution.py:357
  12.8 7.3 %collective-permute-start.4 = (f32[256,128]{1,0:T(8,128)S(1)}, f32[256,128]{1,0:T(8,128)S(1)}, u32[]{:S(2)}, u32[]{:S(2)}) collective-permute-start(f32[256,128]{1,0:T(8,128)S(1)} %get-tuple-element.39), channel_id=1, source_target_pairs={{0,6},{1,7},{2,4},{3,5},{4,2},{5,3},{6,0},{7,1},{8,14},{9,15},{10,... | collective-permute-start | bytes 393224 | tf_op jit(solution)/shard_map/ppermute | solution.py:357
  15.5 6.0 %collective-permute-start.5 = (f32[256,128]{1,0:T(8,128)S(1)}, f32[256,128]{1,0:T(8,128)S(1)}, u32[]{:S(2)}, u32[]{:S(2)}) collective-permute-start(f32[256,128]{1,0:T(8,128)S(1)} %get-tuple-element.40), channel_id=1, source_target_pairs={{0,4},{1,5},{2,6},{3,7},{4,0},{5,1},{6,2},{7,3},{8,12},{9,13},{10,... | collective-permute-start | bytes 393224 | tf_op jit(solution)/shard_map/ppermute | solution.py:357
  16.0 5.5 %collective-permute-start.6 = (f32[256,128]{1,0:T(8,128)S(1)}, f32[256,128]{1,0:T(8,128)S(1)}, u32[]{:S(2)}, u32[]{:S(2)}) collective-permute-start(f32[256,128]{1,0:T(8,128)S(1)} %get-tuple-element.41), channel_id=1, source_target_pairs={{0,2},{1,3},{2,0},{3,1},{4,6},{5,7},{6,4},{7,5},{8,10},{9,11},{10,... | collective-permute-start | bytes 393224 | tf_op jit(solution)/shard_map/ppermute | solution.py:357
  16.7 8.3 %collective-permute-start.10 = (f32[256,128]{1,0:T(8,128)S(1)}, f32[256,128]{1,0:T(8,128)S(1)}, u32[]{:S(2)}, u32[]{:S(2)}) collective-permute-start(f32[256,128]{1,0:T(8,128)S(1)} %shard_map.66), channel_id=1, source_target_pairs={{0,8},{1,9},{2,10},{3,11},{4,12},{5,13},{6,14},{7,15},{8,0},{9,1},... | collective-permute-start | bytes 393224 | tf_op jit(solution)/shard_map/ppermute | solution.py:360
  21.6 8.0 %collective-permute-start.7 = (f32[256,128]{1,0:T(8,128)S(1)}, f32[256,128]{1,0:T(8,128)S(1)}, u32[]{:S(2)}, u32[]{:S(2)}) collective-permute-start(f32[256,128]{1,0:T(8,128)S(1)} %shard_map.62), channel_id=1, source_target_pairs={{0,8},{1,9},{2,10},{3,11},{4,12},{5,13},{6,14},{7,15},{8,0},{9,1},... | collective-permute-start | bytes 393224 | tf_op jit(solution)/shard_map/ppermute | solution.py:360
  25.1 7.9 %collective-permute-start.11 = (f32[256,128]{1,0:T(8,128)S(1)}, f32[256,128]{1,0:T(8,128)S(1)}, u32[]{:S(2)}, u32[]{:S(2)}) collective-permute-start(f32[256,128]{1,0:T(8,128)S(1)} %get-tuple-element.47), channel_id=1, source_target_pairs={{0,6},{1,7},{2,4},{3,5},{4,2},{5,3},{6,0},{7,1},{8,14},{9,15},{10,... | collective-permute-start | bytes 393224 | tf_op jit(solution)/shard_map/ppermute | solution.py:357
  28.2 9.5 %collective-permute-start.12 = (f32[256,128]{1,0:T(8,128)S(1)}, f32[256,128]{1,0:T(8,128)S(1)}, u32[]{:S(2)}, u32[]{:S(2)}) collective-permute-start(f32[256,128]{1,0:T(8,128)S(1)} %get-tuple-element.48), channel_id=1, source_target_pairs={{0,4},{1,5},{2,6},{3,7},{4,0},{5,1},{6,2},{7,3},{8,12},{9,13},{10,... | collective-permute-start | bytes 393224 | tf_op jit(solution)/shard_map/ppermute | solution.py:357
  29.4 8.4 %collective-permute-start.13 = (f32[256,128]{1,0:T(8,128)S(1)}, f32[256,128]{1,0:T(8,128)S(1)}, u32[]{:S(2)}, u32[]{:S(2)}) collective-permute-start(f32[256,128]{1,0:T(8,128)S(1)} %get-tuple-element.49), channel_id=1, source_target_pairs={{0,2},{1,3},{2,0},{3,1},{4,6},{5,7},{6,4},{7,5},{8,10},{9,11},{10,... | collective-permute-start | bytes 393224 | tf_op jit(solution)/shard_map/ppermute | solution.py:357
  29.7 8.4 %collective-permute-start.14 = (f32[256,128]{1,0:T(8,128)S(1)}, f32[256,128]{1,0:T(8,128)S(1)}, u32[]{:S(2)}, u32[]{:S(2)}) collective-permute-start(f32[256,128]{1,0:T(8,128)S(1)} %get-tuple-element.50), channel_id=1, source_target_pairs={{0,6},{1,7},{2,4},{3,5},{4,2},{5,3},{6,0},{7,1},{8,14},{9,15},{10,... | collective-permute-start | bytes 393224 | tf_op jit(solution)/shard_map/ppermute | solution.py:357
  31.9 6.2 %collective-permute-start.15 = (f32[256,128]{1,0:T(8,128)S(1)}, f32[256,128]{1,0:T(8,128)S(1)}, u32[]{:S(2)}, u32[]{:S(2)}) collective-permute-start(f32[256,128]{1,0:T(8,128)S(1)} %get-tuple-element.51), channel_id=1, source_target_pairs={{0,4},{1,5},{2,6},{3,7},{4,0},{5,1},{6,2},{7,3},{8,12},{9,13},{10,... | collective-permute-start | bytes 393224 | tf_op jit(solution)/shard_map/ppermute | solution.py:357
  33.1 5.1 %collective-permute-start.16 = (f32[256,128]{1,0:T(8,128)S(1)}, f32[256,128]{1,0:T(8,128)S(1)}, u32[]{:S(2)}, u32[]{:S(2)}) collective-permute-start(f32[256,128]{1,0:T(8,128)S(1)} %get-tuple-element.52), channel_id=1, source_target_pairs={{0,2},{1,3},{2,0},{3,1},{4,6},{5,7},{6,4},{7,5},{8,10},{9,11},{10,... | collective-permute-start | bytes 393224 | tf_op jit(solution)/shard_map/ppermute | solution.py:357
  38.0 1.6 %copy-start.3 = (f32[4096]{0:T(1024)S(1)}, f32[4096]{0:T(1024)}, u32[]{:S(2)}) copy-start(f32[4096]{0:T(1024)} %param.9) | copy-start | bytes 49156
  38.0 1.6 %collective-permute-start.17 = (f32[64,1024]{1,0:T(8,128)S(1)}, f32[64,1024]{1,0:T(8,128)S(1)}, u32[]{:S(2)}, u32[]{:S(2)}) collective-permute-start(f32[64,1024]{1,0:T(8,128)S(1)} %shard_map.68), channel_id=1, source_target_pairs={{0,1},{1,0},{2,3},{3,2},{4,5},{5,4},{6,7},{7,6},{8,9},{9,8},{10,11... | collective-permute-start | bytes 786440 | tf_op jit(solution)/shard_map/ppermute | solution.py:357
  38.4 1.6 %collective-permute-start.18 = (f32[64,1024]{1,0:T(8,128)S(1)}, f32[64,1024]{1,0:T(8,128)S(1)}, u32[]{:S(2)}, u32[]{:S(2)}) collective-permute-start(f32[64,1024]{1,0:T(8,128)S(1)} %shard_map.70), channel_id=1, source_target_pairs={{0,1},{1,0},{2,3},{3,2},{4,5},{5,4},{6,7},{7,6},{8,9},{9,8},{10,11... | collective-permute-start | bytes 786440 | tf_op jit(solution)/shard_map/ppermute | solution.py:357

commit v8 on v7

--- a/solution.py
+++ b/solution.py
@@ -13,7 +13,7 @@
 FRONT = (((0, 1, 2, 3),), ((0, 1, 2, 3),))
 BACK = (((0, 1, 2, 3),), ((0, 1, 2, 3),))
 SPLIT = (1, 1)
-SLOTS = {'start': [(0, (0, 12))], 'enter1': [(0, (12, 32)), (1, (0, 32))]}
+SLOTS = {'start': [(0, (0, 12))], 'between': [(0, (12, 24))], 'enter1': [(0, (24, 32)), (1, (0, 32))]}
 F32 = jnp.float32
 BF16 = jnp.bfloat16
 HB = pl.BlockSpec(memory_space=pltpu.HBM)

time: 41.1 us -> 41.1 us (level)
    pallas_call x15 -> x16, Pallas kernels: 6.45 us -> 6.56 us  [call(): pl.pallas_call(kernel, out_shape=outs, in_specs=[VM] * len(args), out_spe...]
  transfers between devices with their start and end apart: 19 -> 19, of which waited for: 7 -> 8; matrix products, arithmetic and copies ran while one was open for 0% -> 0% of each run, Pallas kernels for 16% -> 16%
where the time goes in v8:
time: 41.1 us; the launch traced here: 40.9 us
  starting transfers between devices  24.7 us (60%)
  Pallas kernels  8.8 us (21%)
  waiting for transfers between devices  6.31 us (15%)
  local copies, waits for them, and re-layouts  1 us (2%)
    ppermute x17, starting transfers between devices, swap(): return lax.ppermute(what, 'ctx', [(i, i ^ bits) for i in range(count)])  18.7 us
    pallas_call x16, Pallas kernels, call(): pl.pallas_call(kernel, out_shape=outs, in_specs=[VM] * len(args), out_spe...  6.56 us
    ppermute x17, waiting for transfers between devices, swap(): return lax.ppermute(what, 'ctx', [(i, i ^ bits) for i in range(count)])  6.13 us
    ppermute x2, starting transfers between devices, later(): lax.ppermute(what, 'ctx', [(i, (i + shift * 2 * CHIPS) % count) for i in...  6.03 us
    pallas_call x1, Pallas kernels, shards(): pl.pallas_call(functools.partial(first_kernel, groups), out_shape=[array(...  1.29 us
    unnamed x8, local copies, waits for them, and re-layouts  1 us
    pallas_call x1, Pallas kernels, shards(): pl.pallas_call(norm_kernel, out_shape=array((rows, width), BF16), in_spec...  0.94 us
  transfers between devices with their start and end apart: 19, of which 8 were waited for; matrix products, arithmetic and copies ran while one was open for 0% of the time, Pallas kernels for 16%

profile of v8, /device:TPU:0, one launch (start us, length us, event | category | flops | bytes accessed | tf_op | source)
XLA Modules:
  0.0 40.9 jit_solution(16004921689532770815)
XLA Ops:
  0.0 1.3 %shard_map.55 = (f32[32,128]{1,0:T(8,128)S(1)}, bf16[64,128]{1,0:T(8,128)(2,1)S(1)}, f32[64,64]{1,0:T(8,128)S(1)}, f32[64,128]{1,0:T(8,128)S(1)}, f32[1024,128]{1,0:T(8,128)S(1)}) custom-call(s32[1,4]{1,0:T(1,128)} %starts_hbm.1, bf16[64,4096]{1,0:T(8,128)(2,1)} %bitcast.5, bf16[64,4096]{1,0:T(8,128)(2,1)} %bitcast.12), custom_call_target="tpu_custom_call" | custom-call | tf_op jit(solution)/shard_map/pallas_call | solution.py:371
  1.3 0.5 %collective-permute-start = (f32[1024,128]{1,0:T(8,128)S(1)}, f32[1024,128]{1,0:T(8,128)S(1)}, u32[]{:S(2)}, u32[]{:S(2)}) collective-permute-start(f32[1024,128]{1,0:T(8,128)S(1)} %get-tuple-element.35), channel_id=1, source_target_pairs={{0,1},{1,0},{2,3},{3,2},{4,5},{5,4},{6,7},{7,6},{8,9},{9,8},{10,11... | collective-permute-start | bytes 1572872 | tf_op jit(solution)/shard_map/ppermute | solution.py:357
  2.0 0.8 %copy-done = bf16[1,64,4096]{2,1,0:T(8,128)(2,1)S(1)} copy-done((bf16[1,64,4096]{2,1,0:T(8,128)(2,1)S(1)}, bf16[1,64,4096]{2,1,0:T(8,128)(2,1)}, u32[]{:S(2)}) %copy-start) | copy-done | bytes 524312
  3.5 1.7 %shard_map.57.refs_2_.refs_3_ = f32[64,1536]{1,0:T(8,128)S(1)} custom-call(f32[64,64]{1,0:T(8,128)S(1)} %get-tuple-element.32.allowed_ref, bf16[64,4096]{1,0:T(8,128)(2,1)S(1)} %bitcast.20, bf16[64,4096]{1,0:T(8,128)(2,1)S(1)} %bitcast.7, bf16[64,4096]{1,0:T(8,128)(2,1)S(1)} %bitcast.14, f32[1024,128]{1,0:T(8,128)S(1)} %get-tuple-element.34.refs_0_), custom_call_target="tpu_custom_call" | custom-call | tf_op jit(solution)/shard_map/pallas_call | solution.py:345
  5.3 4.0 %collective-permute-start.1 = (f32[256,128]{1,0:T(8,128)S(1)}, f32[256,128]{1,0:T(8,128)S(1)}, u32[]{:S(2)}, u32[]{:S(2)}) collective-permute-start(f32[256,128]{1,0:T(8,128)S(1)} %get-tuple-element.37), channel_id=1, source_target_pairs={{0,6},{1,7},{2,4},{3,5},{4,2},{5,3},{6,0},{7,1},{8,14},{9,15},{10,... | collective-permute-start | bytes 393224 | tf_op jit(solution)/shard_map/ppermute | solution.py:357
  9.3 0.5 %collective-permute-start.2 = (f32[256,128]{1,0:T(8,128)S(1)}, f32[256,128]{1,0:T(8,128)S(1)}, u32[]{:S(2)}, u32[]{:S(2)}) collective-permute-start(f32[256,128]{1,0:T(8,128)S(1)} %get-tuple-element.38), channel_id=1, source_target_pairs={{0,4},{1,5},{2,6},{3,7},{4,0},{5,1},{6,2},{7,3},{8,12},{9,13},{10,... | collective-permute-start | bytes 393224 | tf_op jit(solution)/shard_map/ppermute | solution.py:357
  10.3 2.5 %collective-permute-done.1.refs_1_.refs_2_ = f32[256,128]{1,0:T(8,128)S(1)} collective-permute-done((f32[256,128]{1,0:T(8,128)S(1)}, f32[256,128]{1,0:T(8,128)S(1)}, u32[]{:S(2)}, u32[]{:S(2)}) %collective-permute-start.1) | collective-permute-done | bytes 131104 | tf_op jit(solution)/shard_map/ppermute | solution.py:357
  12.8 2.7 %collective-permute-start.6 = (f32[256,128]{1,0:T(8,128)S(1)}, f32[256,128]{1,0:T(8,128)S(1)}, u32[]{:S(2)}, u32[]{:S(2)}) collective-permute-start(f32[256,128]{1,0:T(8,128)S(1)} %get-tuple-element.42), channel_id=1, source_target_pairs={{0,6},{1,7},{2,4},{3,5},{4,2},{5,3},{6,0},{7,1},{8,14},{9,15},{10,... | collective-permute-start | bytes 393224 | tf_op jit(solution)/shard_map/ppermute | solution.py:357
  15.5 0.5 %collective-permute-start.7 = (f32[256,128]{1,0:T(8,128)S(1)}, f32[256,128]{1,0:T(8,128)S(1)}, u32[]{:S(2)}, u32[]{:S(2)}) collective-permute-start(f32[256,128]{1,0:T(8,128)S(1)} %get-tuple-element.43), channel_id=1, source_target_pairs={{0,4},{1,5},{2,6},{3,7},{4,0},{5,1},{6,2},{7,3},{8,12},{9,13},{10,... | collective-permute-start | bytes 393224 | tf_op jit(solution)/shard_map/ppermute | solution.py:357
  16.7 2.6 %collective-permute-start.10 = (f32[256,128]{1,0:T(8,128)S(1)}, f32[256,128]{1,0:T(8,128)S(1)}, u32[]{:S(2)}, u32[]{:S(2)}) collective-permute-start(f32[256,128]{1,0:T(8,128)S(1)} %shard_map.59.refs_0_), channel_id=1, source_target_pairs={{0,8},{1,9},{2,10},{3,11},{4,12},{5,13},{6,14},{7,15},{8,0},{9,1},... | collective-permute-start | bytes 393224 | tf_op jit(solution)/shard_map/ppermute | solution.py:360
  19.3 1.7 %shard_map.60.refs_4_ = f32[64,1536]{1,0:T(8,128)S(1)} custom-call(f32[64,64]{1,0:T(8,128)S(1)} %get-tuple-element.32.allowed_ref, bf16[64,4096]{1,0:T(8,128)(2,1)S(1)} %bitcast.21, bf16[64,4096]{1,0:T(8,128)(2,1)S(1)} %bitcast.9, bf16[64,4096]{1,0:T(8,128)(2,1)S(1)} %bitcast.16, f32[256,128]{1,0:T(8,128)S(1)} %shard_map.59.refs_0_), custom_call_target="tpu_custom_call" | custom-call | tf_op jit(solution)/shard_map/pallas_call | solution.py:345
  21.0 0.5 %collective-permute-done.7.refs_2_ = f32[256,128]{1,0:T(8,128)S(1)} collective-permute-done((f32[256,128]{1,0:T(8,128)S(1)}, f32[256,128]{1,0:T(8,128)S(1)}, u32[]{:S(2)}, u32[]{:S(2)}) %collective-permute-start.7) | collective-permute-done | bytes 131104 | tf_op jit(solution)/shard_map/ppermute | solution.py:357
  21.6 3.4 %collective-permute-start.9 = (f32[256,128]{1,0:T(8,128)S(1)}, f32[256,128]{1,0:T(8,128)S(1)}, u32[]{:S(2)}, u32[]{:S(2)}) collective-permute-start(f32[256,128]{1,0:T(8,128)S(1)} %shard_map.64), channel_id=1, source_target_pairs={{0,8},{1,9},{2,10},{3,11},{4,12},{5,13},{6,14},{7,15},{8,0},{9,1},... | collective-permute-start | bytes 393224 | tf_op jit(solution)/shard_map/ppermute | solution.py:360
  25.1 3.1 %collective-permute-start.11 = (f32[256,128]{1,0:T(8,128)S(1)}, f32[256,128]{1,0:T(8,128)S(1)}, u32[]{:S(2)}, u32[]{:S(2)}) collective-permute-start(f32[256,128]{1,0:T(8,128)S(1)} %get-tuple-element.47), channel_id=1, source_target_pairs={{0,6},{1,7},{2,4},{3,5},{4,2},{5,3},{6,0},{7,1},{8,14},{9,15},{10,... | collective-permute-start | bytes 393224 | tf_op jit(solution)/shard_map/ppermute | solution.py:357
  28.2 1.2 %collective-permute-start.12 = (f32[256,128]{1,0:T(8,128)S(1)}, f32[256,128]{1,0:T(8,128)S(1)}, u32[]{:S(2)}, u32[]{:S(2)}) collective-permute-start(f32[256,128]{1,0:T(8,128)S(1)} %get-tuple-element.48), channel_id=1, source_target_pairs={{0,4},{1,5},{2,6},{3,7},{4,0},{5,1},{6,2},{7,3},{8,12},{9,13},{10,... | collective-permute-start | bytes 393224 | tf_op jit(solution)/shard_map/ppermute | solution.py:357
  29.7 2.2 %collective-permute-start.14 = (f32[256,128]{1,0:T(8,128)S(1)}, f32[256,128]{1,0:T(8,128)S(1)}, u32[]{:S(2)}, u32[]{:S(2)}) collective-permute-start(f32[256,128]{1,0:T(8,128)S(1)} %get-tuple-element.50), channel_id=1, source_target_pairs={{0,6},{1,7},{2,4},{3,5},{4,2},{5,3},{6,0},{7,1},{8,14},{9,15},{10,... | collective-permute-start | bytes 393224 | tf_op jit(solution)/shard_map/ppermute | solution.py:357
  31.9 1.2 %collective-permute-start.15 = (f32[256,128]{1,0:T(8,128)S(1)}, f32[256,128]{1,0:T(8,128)S(1)}, u32[]{:S(2)}, u32[]{:S(2)}) collective-permute-start(f32[256,128]{1,0:T(8,128)S(1)} %get-tuple-element.51), channel_id=1, source_target_pairs={{0,4},{1,5},{2,6},{3,7},{4,0},{5,1},{6,2},{7,3},{8,12},{9,13},{10,... | collective-permute-start | bytes 393224 | tf_op jit(solution)/shard_map/ppermute | solution.py:357
  33.1 1.9 %collective-permute-start.16 = (f32[256,128]{1,0:T(8,128)S(1)}, f32[256,128]{1,0:T(8,128)S(1)}, u32[]{:S(2)}, u32[]{:S(2)}) collective-permute-start(f32[256,128]{1,0:T(8,128)S(1)} %get-tuple-element.52), channel_id=1, source_target_pairs={{0,2},{1,3},{2,0},{3,1},{4,6},{5,7},{6,4},{7,5},{8,10},{9,11},{10,... | collective-permute-start | bytes 393224 | tf_op jit(solution)/shard_map/ppermute | solution.py:357
  35.0 1.2 %shard_map.66.refs_6_.refs_5_ = f32[64,1024]{1,0:T(8,128)S(1)} custom-call(f32[64,64]{1,0:T(8,128)S(1)} %get-tuple-element.32.allowed_ref, bf16[64,4096]{1,0:T(8,128)(2,1)S(1)} %bitcast.22, bf16[64,4096]{1,0:T(8,128)(2,1)S(1)} %bitcast.10, bf16[64,4096]{1,0:T(8,128)(2,1)S(1)} %bitcast.17, f32[256,128]{1,0:T(8,128)S(1)} %get-tuple-element.45.refs_0_.refs_11_.refs_1_), custom_call_target="tpu_custom_call" | custom-call | tf_op jit(solution)/shard_map/pallas_call | solution.py:345
  36.8 0.8 %collective-permute-done.15.refs_13_.refs_3_ = f32[256,128]{1,0:T(8,128)S(1)} collective-permute-done((f32[256,128]{1,0:T(8,128)S(1)}, f32[256,128]{1,0:T(8,128)S(1)}, u32[]{:S(2)}, u32[]{:S(2)}) %collective-permute-start.15) | collective-permute-done | bytes 131104 | tf_op jit(solution)/shard_map/ppermute | solution.py:357
  37.7 0.6 %collective-permute-done.16.refs_14_.refs_4_ = f32[256,128]{1,0:T(8,128)S(1)} collective-permute-done((f32[256,128]{1,0:T(8,128)S(1)}, f32[256,128]{1,0:T(8,128)S(1)}, u32[]{:S(2)}, u32[]{:S(2)}) %collective-permute-start.16) | collective-permute-done | bytes 131104 | tf_op jit(solution)/shard_map/ppermute | solution.py:357
  38.5 0.4 shard_map.70
  38.9 1.1 %collective-permute-done.18.sibling_ref = f32[64,1024]{1,0:T(8,128)S(1)} collective-permute-done((f32[64,1024]{1,0:T(8,128)S(1)}, f32[64,1024]{1,0:T(8,128)S(1)}, u32[]{:S(2)}, u32[]{:S(2)}) %collective-permute-start.18) | collective-permute-done | bytes 262176 | tf_op jit(solution)/shard_map/ppermute | solution.py:357
  40.0 0.9 %shard_map.72 = bf16[64,4096]{1,0:T(8,128)(2,1)} custom-call(f32[64,128]{1,0:T(8,128)S(1)} %get-tuple-element.30.refs_0_.use_ref, f32[1,4096]{1,0:T(1,128)S(1)} %bitcast.26, f32[64,4096]{1,0:T(8,128)S(1)} %get-tuple-element.53.mixed_ref, f32[64,128]{1,0:T(8,128)S(1)} %get-tuple-element.54.squares_ref, f32[64,1024]{1,0:T(8,128)S(1)} %collective-permute-done.18.sibling_ref), custom_call_target="tpu_custom_call" | custom-call | tf_op jit(solution)/shard_map/pallas_call | solution.py:448
  (40 shorter events, 3.4 us)
Async XLA Ops:
  0.0 1.8 %copy-start.2 = (bf16[1,64,4096]{2,1,0:T(8,128)(2,1)S(1)}, bf16[1,64,4096]{2,1,0:T(8,128)(2,1)}, u32[]{:S(2)}) copy-start(bf16[1,64,4096]{2,1,0:T(8,128)(2,1)} %param.5) | copy-start | bytes 1572868
  1.3 3.9 %collective-permute-start = (f32[1024,128]{1,0:T(8,128)S(1)}, f32[1024,128]{1,0:T(8,128)S(1)}, u32[]{:S(2)}, u32[]{:S(2)}) collective-permute-start(f32[1024,128]{1,0:T(8,128)S(1)} %get-tuple-element.35), channel_id=1, source_target_pairs={{0,1},{1,0},{2,3},{3,2},{4,5},{5,4},{6,7},{7,6},{8,9},{9,8},{10,11... | collective-permute-start | bytes 1572872 | tf_op jit(solution)/shard_map/ppermute | solution.py:357
  1.8 1.0 %copy-start = (bf16[1,64,4096]{2,1,0:T(8,128)(2,1)S(1)}, bf16[1,64,4096]{2,1,0:T(8,128)(2,1)}, u32[]{:S(2)}) copy-start(bf16[1,64,4096]{2,1,0:T(8,128)(2,1)} %param.6) | copy-start | bytes 1572868
  1.8 1.2 %copy-start.1 = (bf16[1,64,4096]{2,1,0:T(8,128)(2,1)S(1)}, bf16[1,64,4096]{2,1,0:T(8,128)(2,1)}, u32[]{:S(2)}) copy-start(bf16[1,64,4096]{2,1,0:T(8,128)(2,1)} %param.7) | copy-start | bytes 1572868
  1.9 8.4 %collective-permute-start.5 = (f32[64,2048]{1,0:T(8,128)S(1)}, f32[64,2048]{1,0:T(8,128)S(1)}, u32[]{:S(2)}, u32[]{:S(2)}) collective-permute-start(f32[64,2048]{1,0:T(8,128)S(1)} %shard_map.62), channel_id=1, source_target_pairs={{0,1},{1,0},{2,3},{3,2},{4,5},{5,4},{6,7},{7,6},{8,9},{9,8},{10,11... | collective-permute-start | bytes 1572872 | tf_op jit(solution)/shard_map/ppermute | solution.py:357
  3.4 6.9 %collective-permute-start.4 = (f32[1024,128]{1,0:T(8,128)S(1)}, f32[1024,128]{1,0:T(8,128)S(1)}, u32[]{:S(2)}, u32[]{:S(2)}) collective-permute-start(f32[1024,128]{1,0:T(8,128)S(1)} %get-tuple-element.40), channel_id=1, source_target_pairs={{0,1},{1,0},{2,3},{3,2},{4,5},{5,4},{6,7},{7,6},{8,9},{9,8},{10,11... | collective-permute-start | bytes 1572872 | tf_op jit(solution)/shard_map/ppermute | solution.py:357
  5.3 7.5 %collective-permute-start.1 = (f32[256,128]{1,0:T(8,128)S(1)}, f32[256,128]{1,0:T(8,128)S(1)}, u32[]{:S(2)}, u32[]{:S(2)}) collective-permute-start(f32[256,128]{1,0:T(8,128)S(1)} %get-tuple-element.37), channel_id=1, source_target_pairs={{0,6},{1,7},{2,4},{3,5},{4,2},{5,3},{6,0},{7,1},{8,14},{9,15},{10,... | collective-permute-start | bytes 393224 | tf_op jit(solution)/shard_map/ppermute | solution.py:357
  9.3 7.1 %collective-permute-start.2 = (f32[256,128]{1,0:T(8,128)S(1)}, f32[256,128]{1,0:T(8,128)S(1)}, u32[]{:S(2)}, u32[]{:S(2)}) collective-permute-start(f32[256,128]{1,0:T(8,128)S(1)} %get-tuple-element.38), channel_id=1, source_target_pairs={{0,4},{1,5},{2,6},{3,7},{4,0},{5,1},{6,2},{7,3},{8,12},{9,13},{10,... | collective-permute-start | bytes 393224 | tf_op jit(solution)/shard_map/ppermute | solution.py:357
  9.8 6.8 %collective-permute-start.3 = (f32[256,128]{1,0:T(8,128)S(1)}, f32[256,128]{1,0:T(8,128)S(1)}, u32[]{:S(2)}, u32[]{:S(2)}) collective-permute-start(f32[256,128]{1,0:T(8,128)S(1)} %get-tuple-element.39), channel_id=1, source_target_pairs={{0,2},{1,3},{2,0},{3,1},{4,6},{5,7},{6,4},{7,5},{8,10},{9,11},{10,... | collective-permute-start | bytes 393224 | tf_op jit(solution)/shard_map/ppermute | solution.py:357
  12.8 8.1 %collective-permute-start.6 = (f32[256,128]{1,0:T(8,128)S(1)}, f32[256,128]{1,0:T(8,128)S(1)}, u32[]{:S(2)}, u32[]{:S(2)}) collective-permute-start(f32[256,128]{1,0:T(8,128)S(1)} %get-tuple-element.42), channel_id=1, source_target_pairs={{0,6},{1,7},{2,4},{3,5},{4,2},{5,3},{6,0},{7,1},{8,14},{9,15},{10,... | collective-permute-start | bytes 393224 | tf_op jit(solution)/shard_map/ppermute | solution.py:357
  15.5 6.0 %collective-permute-start.7 = (f32[256,128]{1,0:T(8,128)S(1)}, f32[256,128]{1,0:T(8,128)S(1)}, u32[]{:S(2)}, u32[]{:S(2)}) collective-permute-start(f32[256,128]{1,0:T(8,128)S(1)} %get-tuple-element.43), channel_id=1, source_target_pairs={{0,4},{1,5},{2,6},{3,7},{4,0},{5,1},{6,2},{7,3},{8,12},{9,13},{10,... | collective-permute-start | bytes 393224 | tf_op jit(solution)/shard_map/ppermute | solution.py:357
  16.0 5.5 %collective-permute-start.8 = (f32[256,128]{1,0:T(8,128)S(1)}, f32[256,128]{1,0:T(8,128)S(1)}, u32[]{:S(2)}, u32[]{:S(2)}) collective-permute-start(f32[256,128]{1,0:T(8,128)S(1)} %get-tuple-element.44), channel_id=1, source_target_pairs={{0,2},{1,3},{2,0},{3,1},{4,6},{5,7},{6,4},{7,5},{8,10},{9,11},{10,... | collective-permute-start | bytes 393224 | tf_op jit(solution)/shard_map/ppermute | solution.py:357
  16.7 8.3 %collective-permute-start.10 = (f32[256,128]{1,0:T(8,128)S(1)}, f32[256,128]{1,0:T(8,128)S(1)}, u32[]{:S(2)}, u32[]{:S(2)}) collective-permute-start(f32[256,128]{1,0:T(8,128)S(1)} %shard_map.59.refs_0_), channel_id=1, source_target_pairs={{0,8},{1,9},{2,10},{3,11},{4,12},{5,13},{6,14},{7,15},{8,0},{9,1},... | collective-permute-start | bytes 393224 | tf_op jit(solution)/shard_map/ppermute | solution.py:360
  21.6 8.0 %collective-permute-start.9 = (f32[256,128]{1,0:T(8,128)S(1)}, f32[256,128]{1,0:T(8,128)S(1)}, u32[]{:S(2)}, u32[]{:S(2)}) collective-permute-start(f32[256,128]{1,0:T(8,128)S(1)} %shard_map.64), channel_id=1, source_target_pairs={{0,8},{1,9},{2,10},{3,11},{4,12},{5,13},{6,14},{7,15},{8,0},{9,1},... | collective-permute-start | bytes 393224 | tf_op jit(solution)/shard_map/ppermute | solution.py:360
  25.1 7.9 %collective-permute-start.11 = (f32[256,128]{1,0:T(8,128)S(1)}, f32[256,128]{1,0:T(8,128)S(1)}, u32[]{:S(2)}, u32[]{:S(2)}) collective-permute-start(f32[256,128]{1,0:T(8,128)S(1)} %get-tuple-element.47), channel_id=1, source_target_pairs={{0,6},{1,7},{2,4},{3,5},{4,2},{5,3},{6,0},{7,1},{8,14},{9,15},{10,... | collective-permute-start | bytes 393224 | tf_op jit(solution)/shard_map/ppermute | solution.py:357
  28.2 7.9 %collective-permute-start.12 = (f32[256,128]{1,0:T(8,128)S(1)}, f32[256,128]{1,0:T(8,128)S(1)}, u32[]{:S(2)}, u32[]{:S(2)}) collective-permute-start(f32[256,128]{1,0:T(8,128)S(1)} %get-tuple-element.48), channel_id=1, source_target_pairs={{0,4},{1,5},{2,6},{3,7},{4,0},{5,1},{6,2},{7,3},{8,12},{9,13},{10,... | collective-permute-start | bytes 393224 | tf_op jit(solution)/shard_map/ppermute | solution.py:357
  29.4 6.8 %collective-permute-start.13 = (f32[256,128]{1,0:T(8,128)S(1)}, f32[256,128]{1,0:T(8,128)S(1)}, u32[]{:S(2)}, u32[]{:S(2)}) collective-permute-start(f32[256,128]{1,0:T(8,128)S(1)} %get-tuple-element.49), channel_id=1, source_target_pairs={{0,2},{1,3},{2,0},{3,1},{4,6},{5,7},{6,4},{7,5},{8,10},{9,11},{10,... | collective-permute-start | bytes 393224 | tf_op jit(solution)/shard_map/ppermute | solution.py:357
  29.7 7.1 %collective-permute-start.14 = (f32[256,128]{1,0:T(8,128)S(1)}, f32[256,128]{1,0:T(8,128)S(1)}, u32[]{:S(2)}, u32[]{:S(2)}) collective-permute-start(f32[256,128]{1,0:T(8,128)S(1)} %get-tuple-element.50), channel_id=1, source_target_pairs={{0,6},{1,7},{2,4},{3,5},{4,2},{5,3},{6,0},{7,1},{8,14},{9,15},{10,... | collective-permute-start | bytes 393224 | tf_op jit(solution)/shard_map/ppermute | solution.py:357
  31.9 5.7 %collective-permute-start.15 = (f32[256,128]{1,0:T(8,128)S(1)}, f32[256,128]{1,0:T(8,128)S(1)}, u32[]{:S(2)}, u32[]{:S(2)}) collective-permute-start(f32[256,128]{1,0:T(8,128)S(1)} %get-tuple-element.51), channel_id=1, source_target_pairs={{0,4},{1,5},{2,6},{3,7},{4,0},{5,1},{6,2},{7,3},{8,12},{9,13},{10,... | collective-permute-start | bytes 393224 | tf_op jit(solution)/shard_map/ppermute | solution.py:357
  33.1 5.1 %collective-permute-start.16 = (f32[256,128]{1,0:T(8,128)S(1)}, f32[256,128]{1,0:T(8,128)S(1)}, u32[]{:S(2)}, u32[]{:S(2)}) collective-permute-start(f32[256,128]{1,0:T(8,128)S(1)} %get-tuple-element.52), channel_id=1, source_target_pairs={{0,2},{1,3},{2,0},{3,1},{4,6},{5,7},{6,4},{7,5},{8,10},{9,11},{10,... | collective-permute-start | bytes 393224 | tf_op jit(solution)/shard_map/ppermute | solution.py:357
  36.4 2.1 %copy-start.3 = (f32[4096]{0:T(1024)S(1)}, f32[4096]{0:T(1024)}, u32[]{:S(2)}) copy-start(f32[4096]{0:T(1024)} %param.9) | copy-start | bytes 49156
  36.4 2.1 %collective-permute-start.17 = (f32[64,1024]{1,0:T(8,128)S(1)}, f32[64,1024]{1,0:T(8,128)S(1)}, u32[]{:S(2)}, u32[]{:S(2)}) collective-permute-start(f32[64,1024]{1,0:T(8,128)S(1)} %shard_map.69), channel_id=1, source_target_pairs={{0,1},{1,0},{2,3},{3,2},{4,5},{5,4},{6,7},{7,6},{8,9},{9,8},{10,11... | collective-permute-start | bytes 786440 | tf_op jit(solution)/shard_map/ppermute | solution.py:357
  38.4 1.6 %collective-permute-start.18 = (f32[64,1024]{1,0:T(8,128)S(1)}, f32[64,1024]{1,0:T(8,128)S(1)}, u32[]{:S(2)}, u32[]{:S(2)}) collective-permute-start(f32[64,1024]{1,0:T(8,128)S(1)} %shard_map.71), channel_id=1, source_target_pairs={{0,1},{1,0},{2,3},{3,2},{4,5},{5,4},{6,7},{7,6},{8,9},{9,8},{10,11... | collective-permute-start | bytes 786440 | tf_op jit(solution)/shard_map/ppermute | solution.py:357
